TPU v7x, 32 devices: a whole 2x2x4 slice. The times are simulated.
32 devices in a mesh: dp: 8 (over y, x, core), mp: 4 (over z).
Axes of the slice: x: 2, y: 2, z: 4, core: 2. Of those that a mesh axis runs over, the one named last changes fastest.
Arguments:
- tokens: bfloat16 [2, 12288, 768], P(None, ('dp', 'mp')), may hold values from -6 to 6
- lengths: int32 [2, 24], P(None, 'dp'), may hold values from 1 to 512, 9216 in all within a row
- cotangent: bfloat16 [2, 12288, 768], P(None, ('dp', 'mp')), may hold values from -6 to 6
- attn_in: float32 [3, 768, 768], P(None, 'dp', 'mp'), may hold values from -0.078125 to 0.078125
- attn_out: float32 [768, 768], P('mp', 'dp'), may hold values from -4 to 4
- ffn_in: float32 [2, 768, 2048], P(None, 'dp', 'mp'), may hold values from -0.21875 to 0.21875
- ffn_out: float32 [2048, 768], P('mp', 'dp'), may hold values from -0.125 to 0.125
- gains: float32 [2, 768], P(None, 'dp'), may hold values from 0.4 to 2.4
- table: float32 [32, 12], P(None, 'mp'), may hold values from -3 to 3
- attn_in_mom: float32 [3, 768, 768], P(None, 'dp', 'mp'), may hold values from -1280 to 1280
- attn_out_mom: float32 [768, 768], P('mp', 'dp'), may hold values from -28 to 28
- ffn_in_mom: float32 [2, 768, 2048], P(None, 'dp', 'mp'), may hold values from -224 to 224
- ffn_out_mom: float32 [2048, 768], P('mp', 'dp'), may hold values from -512 to 512
- gain_first: float32 [2, 768], P(None, 'dp'), may hold values from -80 to 80
- gain_second: float32 [2, 768], P(None, 'dp'), may hold values from 614 to 2457
- table_first: float32 [32, 12], P(None, 'mp'), may hold values from -160 to 160
- table_second: float32 [32, 12], P(None, 'mp'), may hold values from 3072 to 12288
Outputs:
- output: bfloat16 [2, 12288, 768], P(None, ('dp', 'mp'))
- tokens_grad: float32 [2, 12288, 768], P(None, ('dp', 'mp'))
- attn_in_next: float32 [3, 768, 768], P(None, 'dp', 'mp')
- attn_out_next: float32 [768, 768], P('mp', 'dp')
- ffn_in_next: float32 [2, 768, 2048], P(None, 'dp', 'mp')
- ffn_out_next: float32 [2048, 768], P('mp', 'dp')
- attn_in_mom_next: float32 [3, 768, 768], P(None, 'dp', 'mp')
- attn_out_mom_next: float32 [768, 768], P('mp', 'dp')
- ffn_in_mom_next: float32 [2, 768, 2048], P(None, 'dp', 'mp')
- ffn_out_mom_next: float32 [2048, 768], P('mp', 'dp')
- gain_first_next: float32 [2, 768], P(None, 'dp')
- gain_second_next: float32 [2, 768], P(None, 'dp')
- gains_next: float32 [2, 768], P(None, 'dp')
- table_first_next: float32 [32, 12], P(None, 'mp')
- table_second_next: float32 [32, 12], P(None, 'mp')
- table_next: float32 [32, 12], P(None, 'mp')
Inputs may be any that keep to these rules, and one draw needn't show every extreme that they name: In each micro-batch the lengths sum to 3/4 of the 12288 positions and some document has all 512.
All inputs are finite; a program needn't handle non-finite values. No bound on the sum of `lengths` on one device may be relied on, other than what follows from the above.
Results may differ from a plain program's by a relative error of at most 0.02.
Values may be sent and summed in bfloat16 or wider, within the bound.
No kernel may reach another device: no remote copies, remote signals or barrier semaphores. Data moves between devices by JAX's collectives and lax.ppermute only.
A program may use at most 192 MiB of HBM per device.

v0:
```python
import jax
import jax.numpy as jnp
from jax import lax
from jax.sharding import PartitionSpec as P

D = 768
DH = 64
BUCKETS = 32
LEN = 512
NS = 2
STEP = 8


highest_precision = lax.Precision.HIGHEST
epsilon = 1e-06
negative_fill = -1e30
momentum_decay = 0.95
decay_rate = 0.01
linear_coefficient = 3.4445
coef_second = -4.775
coef_third = 2.0315
rate_attn_in = 0.25
rate_attn_out = 12.0
rate_ffn_in = 0.6
rate_ffn_out = 0.3
beta_one = 0.9
beta_two = 0.95
adam_epsilon = 1e-08
adam_rate = 0.3
bucket_marks = (12, 16, 23, 32, 46, 64, 91)


def bucket_table(length):
    position = jnp.arange(length, dtype=jnp.int32)
    relative = position[None, :] - position[:, None]
    distance = jnp.abs(relative)
    marks = jnp.array(bucket_marks, dtype=jnp.int32)
    far_bucket = 8 + jnp.sum(
        (distance[:, :, None] >= marks[None, None, :]).astype(jnp.int32), axis=2
    )
    near_far = jnp.where(distance < 8, distance, far_bucket)
    return near_far + 16 * (relative > 0).astype(jnp.int32)


def norm_rows(rows, gain):
    return rows * lax.rsqrt(jnp.mean(rows * rows, axis=-1, keepdims=True) + epsilon) * gain


def gated(gate_up):
    return jax.nn.gelu(gate_up[0], approximate=True) * gate_up[1]


def masked_scores(queries, keys_in, bias_dev, length_one):
    scores = (
        jnp.einsum("ihd,jhd->hij", queries, keys_in, preferred_element_type=jnp.float32) + bias_dev
    )
    valid = jnp.arange(keys_in.shape[0], dtype=jnp.int32) < length_one
    return jnp.where(valid[None, None, :], scores, negative_fill)


def grams_of(weight_blocks):
    return jnp.einsum("ouq,ouw->oqw", weight_blocks, weight_blocks, precision=highest_precision)


def polish(weight_blocks, gram_product):
    polynomial_term = coef_second * gram_product + coef_third * jnp.einsum(
        "bij,bjk->bik", gram_product, gram_product, precision=highest_precision
    )
    return linear_coefficient * weight_blocks + jnp.einsum(
        "rol,rlv->rov", weight_blocks, polynomial_term, precision=highest_precision
    )


def scaled(weight_blocks, gram_product):
    total = jnp.trace(gram_product, axis1=1, axis2=2)[:, None, None]
    return (weight_blocks * lax.rsqrt(total), gram_product / total)


def adam_update(param, grad, first, second):
    first_new = beta_one * first + (1.0 - beta_one) * grad
    second_new = beta_two * second + (1.0 - beta_two) * grad * grad
    corrected_first = first_new / (1.0 - beta_one**STEP)
    corrected_second = second_new / (1.0 - beta_two**STEP)
    return (
        first_new,
        second_new,
        param - adam_rate * corrected_first / (jnp.sqrt(corrected_second) + adam_epsilon),
    )


def shards(
    tokens,
    lengths,
    cotangent,
    attn_in,
    attn_out,
    ffn_in,
    ffn_out,
    gains,
    table,
    attn_in_mom,
    attn_out_mom,
    ffn_in_mom,
    ffn_out_mom,
    gain_first,
    gain_second,
    table_first,
    table_second,
):
    micro = tokens.shape[0]
    seq_dev = lengths.shape[1]
    heads_dev = table.shape[1]
    width_attn = attn_in.shape[2]
    width_ffn = ffn_in.shape[2]
    bucket = bucket_table(LEN)
    bias_dev = jnp.zeros((heads_dev, LEN, LEN), jnp.float32)
    for bucket_id in range(BUCKETS):
        bias_dev = jnp.where(bucket[None] == bucket_id, table[bucket_id][:, None, None], bias_dev)

    def forward_sequence(inputs):
        queries, keys_in, values_in, length_one = inputs
        scores = masked_scores(queries, keys_in, bias_dev, length_one)
        top_score = jnp.max(scores, axis=-1, keepdims=True)
        log_total = top_score + jnp.log(
            jnp.sum(jnp.exp(scores - top_score), axis=-1, keepdims=True)
        )
        soft = jnp.exp(scores - log_total).astype(jnp.bfloat16)
        attended = jnp.einsum("hij,jhd->ihd", soft, values_in, preferred_element_type=jnp.float32)
        return (attended.astype(jnp.bfloat16), log_total[..., 0])

    def backward_sequence(bias_grad, inputs):
        queries, keys_in, values_in, length_one, log_total, grad_att = inputs
        scores = masked_scores(queries, keys_in, bias_dev, length_one)
        soft = jnp.exp(scores - log_total[..., None])
        grad_soft = jnp.einsum(
            "ihd,jhd->hij", grad_att, values_in, preferred_element_type=jnp.float32
        )
        inner = jnp.sum(grad_soft * soft, axis=-1, keepdims=True)
        grad_scores = (soft * (grad_soft - inner)).astype(jnp.bfloat16)
        grad_query = jnp.einsum(
            "hij,jhd->ihd", grad_scores, keys_in, preferred_element_type=jnp.float32
        )
        grad_key = jnp.einsum(
            "hij,ihd->jhd", grad_scores, queries, preferred_element_type=jnp.float32
        )
        grad_value = jnp.einsum(
            "hij,ihd->jhd", soft.astype(jnp.bfloat16), grad_att, preferred_element_type=jnp.float32
        )
        stacked = jnp.stack([grad_query, grad_key, grad_value]).astype(jnp.bfloat16)
        return (bias_grad + grad_scores.astype(jnp.float32), stacked)

    params_low = (
        attn_in.astype(jnp.bfloat16),
        attn_out.astype(jnp.bfloat16),
        ffn_in.astype(jnp.bfloat16),
        ffn_out.astype(jnp.bfloat16),
        gains.astype(jnp.bfloat16),
    )

    def fetch_params():
        return (
            lax.all_gather(params_low[0], "dp", axis=1, tiled=True),
            lax.all_gather(params_low[1], "dp", axis=1, tiled=True),
            lax.all_gather(params_low[2], "dp", axis=1, tiled=True),
            lax.all_gather(params_low[3], "dp", axis=1, tiled=True),
            lax.all_gather(params_low[4], "dp", axis=1, tiled=True),
        )

    grad_attn_w = jnp.zeros((3, D, width_attn), jnp.float32)
    grad_out = jnp.zeros((width_attn, D), jnp.float32)
    grad_fin = jnp.zeros((2, D, width_ffn), jnp.float32)
    grad_fout = jnp.zeros((width_ffn, D), jnp.float32)
    grad_gain = jnp.zeros((2, D), jnp.float32)
    bias_grad = jnp.zeros((heads_dev, LEN, LEN), jnp.float32)
    outputs = []
    input_grads = []
    for micro_id in range(micro):
        attention_weight, w_out, w_fin, w_fout, gain_now = fetch_params()
        gain_vals = gain_now.astype(jnp.float32)
        rows = tokens[micro_id].astype(jnp.float32)
        normed_one = norm_rows(rows, gain_vals[0]).astype(jnp.bfloat16)
        normed_all = lax.all_gather(normed_one, "mp", axis=0, tiled=True)
        projected = jnp.einsum(
            "td,cdf->ctf", normed_all, attention_weight, preferred_element_type=jnp.float32
        ).astype(jnp.bfloat16)
        per_seq = projected.reshape(3, seq_dev, LEN, heads_dev, DH)
        lens_now = lengths[micro_id]
        attended, log_total = lax.map(
            forward_sequence, (per_seq[0], per_seq[1], per_seq[2], lens_now)
        )
        attended = attended.reshape(seq_dev * LEN, width_attn)
        branch_one = lax.psum_scatter(
            jnp.dot(attended, w_out, preferred_element_type=jnp.float32),
            "mp",
            scatter_dimension=0,
            tiled=True,
        )
        middle = rows + branch_one
        normed_two = norm_rows(middle, gain_vals[1]).astype(jnp.bfloat16)
        normed_all_two = lax.all_gather(normed_two, "mp", axis=0, tiled=True)
        gate_up = jnp.einsum(
            "td,cdf->ctf", normed_all_two, w_fin, preferred_element_type=jnp.float32
        )
        hidden = gated(gate_up).astype(jnp.bfloat16)
        branch_two = lax.psum_scatter(
            jnp.dot(hidden, w_fout, preferred_element_type=jnp.float32).astype(jnp.bfloat16),
            "mp",
            scatter_dimension=0,
            tiled=True,
        ).astype(jnp.float32)
        outputs.append((middle + branch_two).astype(jnp.bfloat16))
        attention_weight, w_out, w_fin, w_fout, gain_now = fetch_params()
        gain_vals = gain_now.astype(jnp.float32)
        grad_rows = cotangent[micro_id].astype(jnp.float32)
        grad_all = lax.all_gather(cotangent[micro_id], "mp", axis=0, tiled=True)
        grad_fout = grad_fout + jnp.einsum(
            "tf,td->fd", hidden, grad_all, preferred_element_type=jnp.float32
        )
        grad_hidden = jnp.einsum("td,fd->tf", grad_all, w_fout, preferred_element_type=jnp.float32)
        _, pull_gate = jax.vjp(gated, gate_up)
        grad_gate_up = pull_gate(grad_hidden)[0].astype(jnp.bfloat16)
        grad_fin = grad_fin + jnp.einsum(
            "td,ctf->cdf", normed_all_two, grad_gate_up, preferred_element_type=jnp.float32
        )
        grad_normed_two = lax.psum_scatter(
            jnp.einsum(
                "ctf,cdf->td", grad_gate_up, w_fin, preferred_element_type=jnp.float32
            ).astype(jnp.bfloat16),
            "mp",
            scatter_dimension=0,
            tiled=True,
        ).astype(jnp.float32)
        _, pull_norm_two = jax.vjp(norm_rows, middle, gain_vals[1])
        grad_middle_norm, grad_gain_two = pull_norm_two(grad_normed_two)
        grad_middle = grad_rows + grad_middle_norm
        grad_mid_all = lax.all_gather(grad_middle.astype(jnp.bfloat16), "mp", axis=0, tiled=True)
        grad_out = grad_out + jnp.einsum(
            "tf,td->fd", attended, grad_mid_all, preferred_element_type=jnp.float32
        )
        grad_att = jnp.einsum(
            "td,fd->tf", grad_mid_all, w_out, preferred_element_type=jnp.float32
        ).astype(jnp.bfloat16)
        grad_att_seq = grad_att.reshape(seq_dev, LEN, heads_dev, DH)
        bias_grad, grad_qkv = lax.scan(
            backward_sequence,
            bias_grad,
            (per_seq[0], per_seq[1], per_seq[2], lens_now, log_total, grad_att_seq),
        )
        projection_gradient = grad_qkv.reshape(seq_dev, 3, LEN, width_attn)
        sequence_normed = normed_all.reshape(seq_dev, LEN, D)
        grad_attn_w = grad_attn_w + jnp.einsum(
            "biy,baim->aym",
            sequence_normed,
            projection_gradient,
            preferred_element_type=jnp.float32,
        )
        grad_normed_part = jnp.einsum(
            "igrj,gbj->irb",
            projection_gradient,
            attention_weight,
            preferred_element_type=jnp.float32,
        )
        grad_normed_one = lax.psum_scatter(
            grad_normed_part.reshape(seq_dev * LEN, D).astype(jnp.bfloat16),
            "mp",
            scatter_dimension=0,
            tiled=True,
        ).astype(jnp.float32)
        _, pull_norm_one = jax.vjp(norm_rows, rows, gain_vals[0])
        grad_rows_norm, grad_gain_one = pull_norm_one(grad_normed_one)
        input_grads.append(grad_middle + grad_rows_norm)
        grad_gain = grad_gain + jnp.stack([grad_gain_one, grad_gain_two])
    output = jnp.stack(outputs)
    tokens_grad = jnp.stack(input_grads)
    shard_in, shard_out, shard_fin, shard_fout, shard_gain = (
        lax.psum_scatter(grad_attn_w, "dp", scatter_dimension=1, tiled=True),
        lax.psum_scatter(grad_out, "dp", scatter_dimension=1, tiled=True),
        lax.psum_scatter(grad_fin, "dp", scatter_dimension=1, tiled=True),
        lax.psum_scatter(grad_fout, "dp", scatter_dimension=1, tiled=True),
        lax.psum_scatter(grad_gain, "dp", scatter_dimension=1, tiled=True),
    )
    gain_grad = lax.psum(shard_gain, "mp")
    table_terms = []
    for bucket_id in range(BUCKETS):
        table_terms.append(
            jnp.sum(jnp.where(bucket[None] == bucket_id, bias_grad, 0.0), axis=(1, 2))
        )
    table_grad_dev = jnp.stack(table_terms)
    mom_in = momentum_decay * attn_in_mom + shard_in
    mom_out = momentum_decay * attn_out_mom + shard_out
    mom_fin = momentum_decay * ffn_in_mom + shard_fin
    mom_fout = momentum_decay * ffn_out_mom + shard_fout
    blocks_attn = jnp.concatenate([mom_in, mom_out.T[None]], axis=0)
    blocks_ffn = jnp.concatenate([mom_fin, mom_fout.T[None]], axis=0)
    gram_attn, gram_ffn, table_grad = lax.psum(
        (grams_of(blocks_attn), grams_of(blocks_ffn), table_grad_dev), "dp"
    )
    blocks_attn, gram_attn = scaled(blocks_attn, gram_attn)
    blocks_ffn, gram_ffn = scaled(blocks_ffn, gram_ffn)
    for ns_round in range(NS):
        if ns_round > 0:
            gram_attn, gram_ffn = lax.psum((grams_of(blocks_attn), grams_of(blocks_ffn)), "dp")
        blocks_attn = polish(blocks_attn, gram_attn)
        blocks_ffn = polish(blocks_ffn, gram_ffn)
    attn_in_next = attn_in * (1.0 - rate_attn_in * decay_rate) - rate_attn_in * blocks_attn[:3]
    attn_out_next = attn_out * (1.0 - rate_attn_out * decay_rate) - rate_attn_out * blocks_attn[3].T
    ffn_in_next = ffn_in * (1.0 - rate_ffn_in * decay_rate) - rate_ffn_in * blocks_ffn[:2]
    ffn_out_next = ffn_out * (1.0 - rate_ffn_out * decay_rate) - rate_ffn_out * blocks_ffn[2].T
    gain_first_next, gain_second_next, gains_next = adam_update(
        gains, gain_grad, gain_first, gain_second
    )
    table_first_next, table_second_next, table_next = adam_update(
        table, table_grad, table_first, table_second
    )
    return (
        output,
        tokens_grad,
        attn_in_next,
        attn_out_next,
        ffn_in_next,
        ffn_out_next,
        mom_in,
        mom_out,
        mom_fin,
        mom_fout,
        gain_first_next,
        gain_second_next,
        gains_next,
        table_first_next,
        table_second_next,
        table_next,
    )


def solution(mesh):
    placed = (
        P(None, ("dp", "mp"), None),
        P(None, "dp"),
        P(None, ("dp", "mp"), None),
        P(None, "dp", "mp"),
        P("mp", "dp"),
        P(None, "dp", "mp"),
        P("mp", "dp"),
        P(None, "dp"),
        P(None, "mp"),
        P(None, "dp", "mp"),
        P("mp", "dp"),
        P(None, "dp", "mp"),
        P("mp", "dp"),
        P(None, "dp"),
        P(None, "dp"),
        P(None, "mp"),
        P(None, "mp"),
    )
    return jax.shard_map(
        shards,
        mesh=mesh,
        in_specs=placed,
        out_specs=(
            P(None, ("dp", "mp"), None),
            P(None, ("dp", "mp"), None),
            P(None, "dp", "mp"),
            P("mp", "dp"),
            P(None, "dp", "mp"),
            P("mp", "dp"),
            P(None, "dp", "mp"),
            P("mp", "dp"),
            P(None, "dp", "mp"),
            P("mp", "dp"),
            P(None, "dp"),
            P(None, "dp"),
            P(None, "dp"),
            P(None, "mp"),
            P(None, "mp"),
            P(None, "mp"),
        ),
        check_vma=False,
    )
```

profile of v0, /device:TPU:0, one launch (start us, length us, event | category | flops | bytes accessed | tf_op | source)
XLA Modules:
  0.0 1298.1 jit_solution(7116152785236932466)
XLA Ops:
  26.3 13.4 %all_gather.56 = bf16[3,768,192]{2,0,1:T(4,128)(2,1)S(1)} all-gather(bf16[3,96,192]{2,0,1:T(4,128)(2,1)S(1)} %copy.693), channel_id=1, replica_groups=mesh['dp'=8,'mp'=4] {'dp'}, dimensions={1}, use_global_device_ids=true | all-gather | bytes 995328 | tf_op jit(solution)/shard_map/all_gather | solution.py:162
  131.2 48.7 %while.53 = (s32[]{:T(128)}, bf16[3,512,3,64]{1,3,2,0:T(8,128)(2,1)}, f32[3,3,512]{2,1,0:T(4,128)S(1)}, bf16[3,512,3,64]{1,3,2,0:T(8,128)(2,1)S(1)}, s32[3]{0:T(...) while((s32[]{:T(128)}, ...), condition=%wide.region_13.14_spmd.clone, body=%wide.region_10.13_spmd.clone.sunk | while | flops 232094720 | bytes 18691696 | solution.py:188
  132.4 13.2 %fusion.327 = (f32[3,512]{1,0:T(4,128)S(1)}, f32[3,512,512]{1,2,0:T(8,128)S(1)}) fusion(f32[3]{0:T(128)S(1)} %get-tuple-element.5530, pred[512,512]{0,1:T(8,128)(4,1)} %get-tuple-element.5531, f32[3]{0:T(128)S(1)} %get-tuple-element.5532, pred[512,512]{0,1:T(8,128)(4,1)} %get-tuple-element.5533, f32[3]{0:T(128)S(1)} %get-tuple-element.5534, ...), kind=kOutput, calls=%fused_computation.436.clone.1 | convolution fusion | flops 128186880 | bytes 11951616 | tf_op jit(solution)/shard_map/while/body/eval_jaxpr/ihd,jhd->hij/dot_general | solution.py:55
  148.7 13.2 %fusion.327 = (f32[3,512]{1,0:T(4,128)S(1)}, f32[3,512,512]{1,2,0:T(8,128)S(1)}) fusion(f32[3]{0:T(128)S(1)} %get-tuple-element.5530, pred[512,512]{0,1:T(8,128)(4,1)} %get-tuple-element.5531, f32[3]{0:T(128)S(1)} %get-tuple-element.5532, pred[512,512]{0,1:T(8,128)(4,1)} %get-tuple-element.5533, f32[3]{0:T(128)S(1)} %get-tuple-element.5534, ...), kind=kOutput, calls=%fused_computation.436.clone.1 | convolution fusion | flops 128186880 | bytes 11951616 | tf_op jit(solution)/shard_map/while/body/eval_jaxpr/ihd,jhd->hij/dot_general | solution.py:55
  164.9 13.2 %fusion.327 = (f32[3,512]{1,0:T(4,128)S(1)}, f32[3,512,512]{1,2,0:T(8,128)S(1)}) fusion(f32[3]{0:T(128)S(1)} %get-tuple-element.5530, pred[512,512]{0,1:T(8,128)(4,1)} %get-tuple-element.5531, f32[3]{0:T(128)S(1)} %get-tuple-element.5532, pred[512,512]{0,1:T(8,128)(4,1)} %get-tuple-element.5533, f32[3]{0:T(128)S(1)} %get-tuple-element.5534, ...), kind=kOutput, calls=%fused_computation.436.clone.1 | convolution fusion | flops 128186880 | bytes 11951616 | tf_op jit(solution)/shard_map/while/body/eval_jaxpr/ihd,jhd->hij/dot_general | solution.py:55
  190.3 49.0 %while.52 = (s32[]{:T(128)}, bf16[3,512,3,64]{1,3,2,0:T(8,128)(2,1)S(1)}, f32[3,3,512]{2,1,0:T(4,128)S(1)}, bf16[3,512,3,64]{1,3,2,0:T(8,128)(2,1)S(1)}, s32[3]{...) while((s32[]{:T(128)}, ...), condition=%wide.region_5.6_spmd.clone, body=%wide.region_2.5_spmd.clone.sunk | while | flops 232094720 | bytes 18677696 | solution.py:188
  192.2 13.3 %fusion.324 = (f32[3,512]{1,0:T(4,128)S(1)}, f32[3,512,512]{1,2,0:T(8,128)S(1)}) fusion(f32[3]{0:T(128)} %get-tuple-element.5314, pred[512,512]{0,1:T(8,128)(4,1)} %get-tuple-element.5315, f32[3]{0:T(128)} %get-tuple-element.5316, pred[512,512]{0,1:T(8,128)(4,1)} %get-tuple-element.5317, f32[3]{0:T(128)} %get-tuple-element.5318, ...), kind=kOutput, calls=%fused_computation.435.clone.1 | convolution fusion | flops 128186880 | bytes 11937616 | tf_op jit(solution)/shard_map/while/body/eval_jaxpr/ihd,jhd->hij/dot_general | solution.py:55
  208.5 13.3 %fusion.324 = (f32[3,512]{1,0:T(4,128)S(1)}, f32[3,512,512]{1,2,0:T(8,128)S(1)}) fusion(f32[3]{0:T(128)} %get-tuple-element.5314, pred[512,512]{0,1:T(8,128)(4,1)} %get-tuple-element.5315, f32[3]{0:T(128)} %get-tuple-element.5316, pred[512,512]{0,1:T(8,128)(4,1)} %get-tuple-element.5317, f32[3]{0:T(128)} %get-tuple-element.5318, ...), kind=kOutput, calls=%fused_computation.435.clone.1 | convolution fusion | flops 128186880 | bytes 11937616 | tf_op jit(solution)/shard_map/while/body/eval_jaxpr/ihd,jhd->hij/dot_general | solution.py:55
  224.8 13.3 %fusion.324 = (f32[3,512]{1,0:T(4,128)S(1)}, f32[3,512,512]{1,2,0:T(8,128)S(1)}) fusion(f32[3]{0:T(128)} %get-tuple-element.5314, pred[512,512]{0,1:T(8,128)(4,1)} %get-tuple-element.5315, f32[3]{0:T(128)} %get-tuple-element.5316, pred[512,512]{0,1:T(8,128)(4,1)} %get-tuple-element.5317, f32[3]{0:T(128)} %get-tuple-element.5318, ...), kind=kOutput, calls=%fused_computation.435.clone.1 | convolution fusion | flops 128186880 | bytes 11937616 | tf_op jit(solution)/shard_map/while/body/eval_jaxpr/ihd,jhd->hij/dot_general | solution.py:55
  245.7 24.7 %reduce-scatter.25.cloned.1.call-done = f32[384,768]{1,0:T(8,128)} async-done(((f32[1536,768]{1,0:T(8,128)}), f32[384,768]{1,0:T(8,128)}) %reduce-scatter.25.cloned.1.call-update) | async-done | bytes 1179664 | tf_op jit(solution)/shard_map/reduce_scatter | solution.py:192
  270.4 88.0 %reduce-scatter.21.cloned.1.call-done = f32[384,768]{1,0:T(8,128)} async-done(((f32[1536,768]{1,0:T(8,128)}), f32[384,768]{1,0:T(8,128)}) %reduce-scatter.21.cloned.1.call-update) | async-done | bytes 1179664 | tf_op jit(solution)/shard_map/reduce_scatter | solution.py:192
  377.7 35.1 %all-gather.21.cloned.1.call-done = bf16[1536,768]{1,0:T(8,128)(2,1)} async-done(((bf16[384,768]{1,0:T(8,128)(2,1)}), bf16[1536,768]{1,0:T(8,128)(2,1)}) %all-gather.21.cloned.1.call-update) | async-done | bytes 2359312 | tf_op jit(solution)/shard_map/all_gather | solution.py:200
  420.3 42.7 %all-gather.29.cloned.1.call-done = bf16[1,1536,768]{2,1,0:T(8,128)(2,1)} async-done(((bf16[1,384,768]{2,1,0:T(8,128)(2,1)}), bf16[1,1536,768]{2,1,0:T(8,128)(2,1)}) %all-gather.29.cloned.1.call-update) | async-done | bytes 2359312 | tf_op jit(solution)/shard_map/all_gather | solution.py:215
  478.5 34.7 %all-gather.15.cloned.1.call-done = bf16[1536,768]{1,0:T(8,128)(2,1)} async-done(((bf16[384,768]{1,0:T(8,128)(2,1)}), bf16[1536,768]{1,0:T(8,128)(2,1)}) %all-gather.15.cloned.1.call-update) | async-done | bytes 2359312 | tf_op jit(solution)/shard_map/all_gather | solution.py:200
  520.7 42.9 %all-gather.27.cloned.1.call-done = bf16[1,1536,768]{2,1,0:T(8,128)(2,1)} async-done(((bf16[1,384,768]{2,1,0:T(8,128)(2,1)}), bf16[1,1536,768]{2,1,0:T(8,128)(2,1)}) %all-gather.27.cloned.1.call-update) | async-done | bytes 2359312 | tf_op jit(solution)/shard_map/all_gather | solution.py:215
  583.3 29.6 %reduce-scatter.33.cloned.1.call-done = bf16[384,768]{1,0:T(8,128)(2,1)} async-done(((bf16[1536,768]{1,0:T(8,128)(2,1)}), bf16[384,768]{1,0:T(8,128)(2,1)}) %reduce-scatter.33.cloned.1.call-update) | async-done | bytes 589840 | tf_op jit(solution)/shard_map/reduce_scatter | solution.py:225
  612.9 49.3 %reduce-scatter.29.cloned.1.call-done = bf16[384,768]{1,0:T(8,128)(2,1)} async-done(((bf16[1536,768]{1,0:T(8,128)(2,1)}), bf16[384,768]{1,0:T(8,128)(2,1)}) %reduce-scatter.29.cloned.1.call-update) | async-done | bytes 589840 | tf_op jit(solution)/shard_map/reduce_scatter | solution.py:225
  666.8 44.8 %reduce-scatter.23.cloned.1.call-done = bf16[384,768]{1,0:T(8,128)(2,1)} async-done(((bf16[1536,768]{1,0:T(8,128)(2,1)}), bf16[384,768]{1,0:T(8,128)(2,1)}) %reduce-scatter.23.cloned.1.call-update) | async-done | bytes 589840 | tf_op jit(solution)/shard_map/reduce_scatter | solution.py:205
  735.3 29.7 %all-gather.25.cloned.1.call-done = bf16[1536,768]{1,0:T(8,128)(2,1)} async-done(((bf16[384,768]{1,0:T(8,128)(2,1)}), bf16[1536,768]{1,0:T(8,128)(2,1)}) %all-gather.25.cloned.1.call-update) | async-done | bytes 2359312 | tf_op jit(solution)/shard_map/all_gather | solution.py:236
  772.7 43.1 %all-gather.23.cloned.1.call-done = bf16[1536,768]{1,0:T(8,128)(2,1)} async-done(((bf16[384,768]{1,0:T(8,128)(2,1)}), bf16[1536,768]{1,0:T(8,128)(2,1)}) %all-gather.23.cloned.1.call-update) | async-done | bytes 2359312 | tf_op jit(solution)/shard_map/all_gather | solution.py:236
  824.8 72.4 %while.55 = (s32[]{:T(128)}, f32[3,512,512]{1,2,0:T(8,128)S(1)}, bf16[3,3,512,3,64]{2,4,3,1,0:T(8,128)(2,1)}, s32[3]{0:T(128)}, bf16[3,512,3,64]{1,3,2,0:T(8,128...) while((s32[]{:T(128)}, f32[3,512,512]{1,2,0:T(8,128)S(1)}, ...), condition=%wide.region_21.22_spmd.clone, body=%wide.region_19.21_spmd.clone.sunk | while | flops 539982848 | bytes 43826924 | solution.py:244
  827.5 13.8 %fusion.349 = f32[3,512,512]{1,2,0:T(8,128)S(1)} fusion(f32[3]{0:T(128)} %get-tuple-element.5754, f32[3]{0:T(128)} %get-tuple-element.5756, f32[3]{0:T(128)} %get-tuple-element.5758, f32[3]{0:T(128)} %get-tuple-element.5760, f32[3]{0:T(128)} %get-tuple-element.5762, f32[3]{0:T(128)} %get-tuple-element.5764, f32[3]{0:T(128)} %get-tuple-element.5766, ...), kind=kOutput, calls=%fused_computation.86.clone.1 | convolution fusion | flops 128188416 | bytes 11949616 | tf_op jit(solution)/shard_map/while/body/eval_jaxpr/ihd,jhd->hij/dot_general | solution.py:55
  851.6 13.8 %fusion.349 = f32[3,512,512]{1,2,0:T(8,128)S(1)} fusion(f32[3]{0:T(128)} %get-tuple-element.5754, f32[3]{0:T(128)} %get-tuple-element.5756, f32[3]{0:T(128)} %get-tuple-element.5758, f32[3]{0:T(128)} %get-tuple-element.5760, f32[3]{0:T(128)} %get-tuple-element.5762, f32[3]{0:T(128)} %get-tuple-element.5764, f32[3]{0:T(128)} %get-tuple-element.5766, ...), kind=kOutput, calls=%fused_computation.86.clone.1 | convolution fusion | flops 128188416 | bytes 11949616 | tf_op jit(solution)/shard_map/while/body/eval_jaxpr/ihd,jhd->hij/dot_general | solution.py:55
  875.7 13.8 %fusion.349 = f32[3,512,512]{1,2,0:T(8,128)S(1)} fusion(f32[3]{0:T(128)} %get-tuple-element.5754, f32[3]{0:T(128)} %get-tuple-element.5756, f32[3]{0:T(128)} %get-tuple-element.5758, f32[3]{0:T(128)} %get-tuple-element.5760, f32[3]{0:T(128)} %get-tuple-element.5762, f32[3]{0:T(128)} %get-tuple-element.5764, f32[3]{0:T(128)} %get-tuple-element.5766, ...), kind=kOutput, calls=%fused_computation.86.clone.1 | convolution fusion | flops 128188416 | bytes 11949616 | tf_op jit(solution)/shard_map/while/body/eval_jaxpr/ihd,jhd->hij/dot_general | solution.py:55
  898.8 71.2 %while.54 = (s32[]{:T(128)}, f32[3,512,512]{1,2,0:T(8,128)S(1)}, bf16[3,3,512,3,64]{2,4,3,1,0:T(8,128)(2,1)}, s32[3]{0:T(128)S(1)}, bf16[3,512,3,64]{1,3,2,0:T(8...) while((s32[]{:T(128)}, f32[3,512,512]{1,2,0:T(8,128)S(1)}, ...), condition=%wide.region_28.29_spmd.clone, body=%wide.region_26.28_spmd.clone.sunk | while | flops 539196416 | bytes 43826908 | solution.py:244
  900.9 13.8 %fusion.337 = f32[3,512,512]{1,2,0:T(8,128)S(1)} fusion(f32[3]{0:T(128)} %get-tuple-element.5977, f32[3]{0:T(128)} %get-tuple-element.5979, f32[3]{0:T(128)} %get-tuple-element.5981, f32[3]{0:T(128)} %get-tuple-element.5983, f32[3]{0:T(128)} %get-tuple-element.5985, f32[3]{0:T(128)} %get-tuple-element.5987, f32[3]{0:T(128)} %get-tuple-element.5989, ...), kind=kOutput, calls=%fused_computation.47.clone.1 | convolution fusion | flops 128188416 | bytes 11949616 | tf_op jit(solution)/shard_map/while/body/eval_jaxpr/ihd,jhd->hij/dot_general | solution.py:55
  924.6 13.8 %fusion.337 = f32[3,512,512]{1,2,0:T(8,128)S(1)} fusion(f32[3]{0:T(128)} %get-tuple-element.5977, f32[3]{0:T(128)} %get-tuple-element.5979, f32[3]{0:T(128)} %get-tuple-element.5981, f32[3]{0:T(128)} %get-tuple-element.5983, f32[3]{0:T(128)} %get-tuple-element.5985, f32[3]{0:T(128)} %get-tuple-element.5987, f32[3]{0:T(128)} %get-tuple-element.5989, ...), kind=kOutput, calls=%fused_computation.47.clone.1 | convolution fusion | flops 128188416 | bytes 11949616 | tf_op jit(solution)/shard_map/while/body/eval_jaxpr/ihd,jhd->hij/dot_general | solution.py:55
  948.2 13.8 %fusion.337 = f32[3,512,512]{1,2,0:T(8,128)S(1)} fusion(f32[3]{0:T(128)} %get-tuple-element.5977, f32[3]{0:T(128)} %get-tuple-element.5979, f32[3]{0:T(128)} %get-tuple-element.5981, f32[3]{0:T(128)} %get-tuple-element.5983, f32[3]{0:T(128)} %get-tuple-element.5985, f32[3]{0:T(128)} %get-tuple-element.5987, f32[3]{0:T(128)} %get-tuple-element.5989, ...), kind=kOutput, calls=%fused_computation.47.clone.1 | convolution fusion | flops 128188416 | bytes 11949616 | tf_op jit(solution)/shard_map/while/body/eval_jaxpr/ihd,jhd->hij/dot_general | solution.py:55
  1011.1 43.6 %reduce-scatter.37.cloned.1.call-done = f32[96,576]{1,0:T(8,128)} async-done(((f32[768,576]{1,0:T(8,128)}), f32[96,576]{1,0:T(8,128)}) %reduce-scatter.37.cloned.1.call-update) | async-done | bytes 221200
  1110.6 27.1 %all-reduce.15.cloned.1.call-done = (f32[4,192,192]{2,1,0:T(8,128)}, f32[3,512,512]{2,1,0:T(8,128)}) async-done(((f32[4,192,192]{2,1,0:T(8,128)}, f32[3,512,512]{2,1,0:T(8,128)}), (f32[4,192,192]{2,1,0:T(8,128)}, f32[3,512,512]{2,1,0:T(8,128)})) %all-reduce.15.cloned.1.call-update) | async-done | bytes 3735568 | tf_op jit(solution)/shard_map/psum | solution.py:295
  1157.0 16.2 %reduce-scatter.31.cloned.1.call-done = bf16[384,768]{1,0:T(8,128)(2,1)} async-done(((bf16[1536,768]{1,0:T(8,128)(2,1)}), bf16[384,768]{1,0:T(8,128)(2,1)}) %reduce-scatter.31.cloned.1.call-update) | async-done | bytes 589840 | tf_op jit(solution)/shard_map/reduce_scatter | solution.py:263
  1231.0 14.2 %psum.47 = f32[32,3]{0,1:T(4,128)} all-reduce(f32[32,3]{0,1:T(4,128)} %stack.191), channel_id=1, replica_groups=mesh['dp'=8,'mp'=4] {'dp'}, use_global_device_ids=true, to_apply=%region_79.80 | all-reduce | flops 96 | bytes 768 | tf_op jit(solution)/shard_map/psum | solution.py:295
  (654 shorter events, 537.2 us)
Async XLA Ops:
  8.0 103.9 %all-gather.19.cloned.1.call-start = ((), (), s32[]{:S(2)}) async-start(), calls=%async_computation.17 | async-start | bytes 2949120 | tf_op jit(solution)/shard_map/all_gather | solution.py:182
  24.5 102.4 %all-gather.13.cloned.1.call-start = ((), (), s32[]{:S(2)}) async-start(), calls=%async_computation.12 | async-start | bytes 2949120 | tf_op jit(solution)/shard_map/all_gather | solution.py:182
  25.2 245.2 %reduce-scatter.25.cloned.1.call-start = ((), (), s32[]{:S(2)}) async-start(), calls=%async_computation.18 | async-start | bytes 5898240 | tf_op jit(solution)/shard_map/reduce_scatter | solution.py:192
  110.5 129.5 %copy-start.13 = (bf16[192,768]{0,1:T(8,128)(2,1)}, bf16[192,768]{0,1:T(8,128)(2,1)S(1)}, u32[]{:S(2)}) copy-start(bf16[192,768]{0,1:T(8,128)(2,1)S(1)} %all_gather.57) | copy-start | bytes 884740
  186.2 172.2 %reduce-scatter.21.cloned.1.call-start = ((), (), s32[]{:S(2)}) async-start(), calls=%async_computation.13 | async-start | bytes 5898240 | tf_op jit(solution)/shard_map/reduce_scatter | solution.py:192
  243.9 114.4 %copy-start = (bf16[2,384,768]{2,1,0:T(8,128)(2,1)S(1)}, bf16[2,384,768]{2,1,0:T(8,128)(2,1)}, u32[]{:S(2)}) copy-start(bf16[2,384,768]{2,1,0:T(8,128)(2,1)} %param.26) | copy-start | bytes 3538948
  244.0 133.8 %all-gather.17.cloned.1.call-start = ((), (), s32[]{:S(2)}) async-start(), calls=%async_computation.15 | async-start | bytes 1769472 | tf_op jit(solution)/shard_map/all_gather | solution.py:164
  245.6 115.3 %copy-start.68 = (f32[768]{0:T(1024)S(1)}, f32[768]{0:T(1024)}, u32[]{:S(2)}) copy-start(f32[768]{0:T(1024)} %get-tuple-element.2696) | copy-start | bytes 9220
  245.6 167.2 %all-gather.21.cloned.1.call-start = ((), (), s32[]{:S(2)}) async-start(), calls=%async_computation.19 | async-start | bytes 2949120 | tf_op jit(solution)/shard_map/all_gather | solution.py:200
  360.4 351.2 %copy-start.2 = (f32[384,768]{1,0:T(8,128)}, f32[384,768]{1,0:T(8,128)S(1)}, u32[]{:S(2)}) copy-start(f32[384,768]{1,0:T(8,128)S(1)} %get-tuple-element.3325) | copy-start | bytes 3538948
  360.4 351.2 %copy-start.4 = (f32[384,768]{1,0:T(8,128)}, f32[384,768]{1,0:T(8,128)S(1)}, u32[]{:S(2)}) copy-start(f32[384,768]{1,0:T(8,128)S(1)} %get-tuple-element.3358) | copy-start | bytes 3538948
  360.9 350.6 %copy-start.74 = (f32[384]{0:T(512)}, f32[384]{0:T(512)S(1)}, u32[]{:S(2)}) copy-start(f32[384]{0:T(512)S(1)} %fusion.203) | copy-start | bytes 4612
  360.9 350.6 %copy-start.76 = (f32[384]{0:T(512)}, f32[384]{0:T(512)S(1)}, u32[]{:S(2)}) copy-start(f32[384]{0:T(512)S(1)} %fusion.205) | copy-start | bytes 4612
  362.2 100.8 %all-gather.29.cloned.1.call-start = ((), (), s32[]{:S(2)}) async-start(), calls=%async_computation.28 | async-start | bytes 2949120 | tf_op jit(solution)/shard_map/all_gather | solution.py:215
  363.7 149.6 %all-gather.15.cloned.1.call-start = ((), (), s32[]{:S(2)}) async-start(), calls=%async_computation.14 | async-start | bytes 2949120 | tf_op jit(solution)/shard_map/all_gather | solution.py:200
  364.4 199.1 %all-gather.27.cloned.1.call-start = ((), (), s32[]{:S(2)}) async-start(), calls=%async_computation.27 | async-start | bytes 2949120 | tf_op jit(solution)/shard_map/all_gather | solution.py:215
  365.2 247.7 %reduce-scatter.33.cloned.1.call-start = ((), (), s32[]{:S(2)}) async-start(), calls=%async_computation.24 | async-start | bytes 2949120 | tf_op jit(solution)/shard_map/reduce_scatter | solution.py:225
  478.3 183.9 %reduce-scatter.29.cloned.1.call-start = ((), (), s32[]{:S(2)}) async-start(), calls=%async_computation.21 | async-start | bytes 2949120 | tf_op jit(solution)/shard_map/reduce_scatter | solution.py:225
  578.7 132.9 %reduce-scatter.23.cloned.1.call-start = ((), (), s32[]{:S(2)}) async-start(), calls=%async_computation.16 | async-start | bytes 2949120 | tf_op jit(solution)/shard_map/reduce_scatter | solution.py:205
  583.2 181.8 %all-gather.25.cloned.1.call-start = ((), (), s32[]{:S(2)}) async-start(), calls=%async_computation.25 | async-start | bytes 2949120 | tf_op jit(solution)/shard_map/all_gather | solution.py:236
  715.0 100.8 %all-gather.23.cloned.1.call-start = ((), (), s32[]{:S(2)}) async-start(), calls=%async_computation.22 | async-start | bytes 2949120 | tf_op jit(solution)/shard_map/all_gather | solution.py:236
  715.5 278.8 %all-reduce.11.cloned.1.call-start = ((), (), s32[]{:S(2)}) async-start(), calls=%async_computation.33 | async-start | bytes 6291456
  728.3 268.3 %reduce-scatter.41.cloned.1.call-start = ((), (), s32[]{:S(2)}) async-start(), calls=%async_computation.31 | async-start | bytes 1769472
  734.8 275.4 %reduce-scatter.39.cloned.1.call-start = ((), (), s32[]{:S(2)}) async-start(), calls=%async_computation.30 | async-start | bytes 884736
  976.3 78.5 %reduce-scatter.37.cloned.1.call-start = ((), (), s32[]{:S(2)}) async-start(), calls=%async_computation.29 | async-start | bytes 2211840
  992.3 145.3 %all-reduce.15.cloned.1.call-start = ((), (), s32[]{:S(2)}) async-start(), calls=%async_computation.35 | async-start | bytes 7864320 | tf_op jit(solution)/shard_map/psum | solution.py:295
  1011.1 131.5 %copy-start.29 = (f32[192,96]{0,1:T(8,128)}, f32[192,96]{0,1:T(8,128)S(1)}, u32[]{:S(2)}) copy-start(f32[192,96]{0,1:T(8,128)S(1)} %bitcast_add_fusion.2) | copy-start | bytes 221188
  1059.6 97.4 %reduce-scatter.35.cloned.1.call-start = ((), (), s32[]{:S(2)}) async-start(), calls=%async_computation.26 | async-start | bytes 2949120 | tf_op jit(solution)/shard_map/reduce_scatter | solution.py:263
  1075.1 98.1 %reduce-scatter.31.cloned.1.call-start = ((), (), s32[]{:S(2)}) async-start(), calls=%async_computation.23 | async-start | bytes 2949120 | tf_op jit(solution)/shard_map/reduce_scatter | solution.py:263
  1091.1 158.3 %reduce-scatter.27.cloned.1.call-start = ((), (), s32[]{:S(2)}) async-start(), calls=%async_computation.20 | async-start | bytes 2949120 | tf_op jit(solution)/shard_map/reduce_scatter | solution.py:205
  1095.6 166.9 %reduce-scatter.43.cloned.1.call-start = ((), (), s32[]{:S(2)}) async-start(), calls=%async_computation.32 | async-start | bytes 442368
  1177.3 98.7 %all-reduce.13.cloned.1.call-start = ((), (), s32[]{:S(2)}) async-start(), calls=%async_computation.34 | async-start | bytes 7864320 | tf_op jit(solution)/shard_map/psum | solution.py:302
  (142 other events, 2255.8 us)
Sparse Core Ops, SparseCore 0:
  24.6 50.7 all-gather.18
  77.5 49.2 all-gather.12
  186.3 84.0 reduce-scatter.24
  272.5 85.7 reduce-scatter.20
  715.1 49.8 all-gather.24
  766.4 49.2 all-gather.22
  1075.2 48.1 reduce-scatter.34
  1125.7 47.4 reduce-scatter.30
  1175.6 47.5 reduce-scatter.26
  1226.0 36.5 reduce-scatter.42
Sparse Core Ops, SparseCore 1:
  246.9 25.1 all-gather.16
  362.3 50.5 all-gather.20
  414.3 48.6 all-gather.28
  464.6 48.6 all-gather.14
  514.9 48.6 all-gather.26
  566.4 46.4 reduce-scatter.32
  615.0 47.1 reduce-scatter.28
  664.4 47.1 reduce-scatter.22
  728.4 68.3 all-reduce.10
  800.4 38.3 reduce-scatter.40
  976.4 33.7 reduce-scatter.38
  1014.6 40.2 reduce-scatter.36
  1059.7 77.8 all-reduce.14
  1181.4 78.4 all-reduce.12
where the time goes:
time: 1310 us; the launch traced here: 1300 us
  waiting for transfers between devices  578 us (44%)
  matrix products  336 us (26%)
  local copies, waits for them, and re-layouts  194 us (15%)
  other arithmetic  98.5 us (8%)
  blocking collectives  70 us (5%)
  between operations  18.8 us (1%)
    dot_general x12, matrix products, masked_scores(): jnp.einsum('ihd,jhd->hij', queries, keys_in, preferred_element_type=jnp.f...  162 us
    reduce_scatter x2, waiting for transfers between devices, shards(): lax.psum_scatter(jnp.dot(attended, w_out, preferred_element_type=jnp.floa...  113 us
    unnamed x342, local copies, waits for them, and re-layouts  89.1 us
    all_gather x2, waiting for transfers between devices, shards(): grad_all = lax.all_gather(cotangent[micro_id], 'mp', axis=0, tiled=True)  85.6 us
    reduce_scatter x2, waiting for transfers between devices, shards(): lax.psum_scatter(jnp.einsum('ctf,cdf->td', grad_gate_up, w_fin, preferred...  78.9 us
    all_gather x2, waiting for transfers between devices, shards(): lax.all_gather(grad_middle.astype(jnp.bfloat16), 'mp', axis=0, tiled=True)  72.8 us
    all_gather x2, waiting for transfers between devices, shards(): normed_all_two = lax.all_gather(normed_two, 'mp', axis=0, tiled=True)  69.9 us
    unnamed x29, waiting for transfers between devices  61.2 us
  transfers between devices with their start and end apart: 24, of which 17 were waited for; matrix products, arithmetic and copies ran while one was open for 41% of the time, Pallas kernels for 0%

commit v1 on v0

v1 whole, which is shorter than its diff:
```python
import functools

import jax
import jax.numpy as jnp
import numpy as np
from jax import lax
from jax.experimental import pallas as pl
from jax.experimental.pallas import tpu as pltpu
from jax.sharding import PartitionSpec as P

D = 768
H = 12
DH = 64
BUCKETS = 32
LEN = 512
STEP = 8
QB = 128
SKEW = 1024
PAIRS = H // 2

epsilon = 1e-06
negative_fill = -1e30
momentum_decay = 0.95
decay_rate = 0.01
linear_coefficient = 3.4445
coef_second = -4.775
coef_third = 2.0315
rate_attn_in = 0.25
rate_attn_out = 12.0
rate_ffn_in = 0.6
rate_ffn_out = 0.3
beta_one = 0.9
beta_two = 0.95
adam_epsilon = 1e-08
adam_rate = 0.3
bucket_marks = (12, 16, 23, 32, 46, 64, 91)

HIGHEST = lax.Precision.HIGHEST
HIGH = lax.Precision.HIGH
bf16 = jnp.bfloat16
f32 = jnp.float32
NN = (((1,), (0,)), ((), ()))
NT = (((1,), (1,)), ((), ()))
TN = (((0,), (0,)), ((), ()))


def dot(a, b, dims=NN):
    return lax.dot_general(a, b, dims, preferred_element_type=f32)


def skew_onehot():
    place = np.arange(SKEW)
    relative = np.where(place < SKEW - QB + 1, place, place - SKEW) - (LEN - QB)
    distance = np.abs(relative)
    far = 8 + sum((distance >= mark).astype(np.int32) for mark in bucket_marks)
    bucket = np.where(distance < 8, distance, far) + 16 * (relative > 0)
    return (bucket[:, None] == np.arange(BUCKETS)[None, :]).astype(np.float32)


def half_lanes(shape, half):
    lane = lax.broadcasted_iota(jnp.int32, shape, 1)
    return (lane < DH) if half == 0 else (lane >= DH)


def make_bias(line_ref, bias_ref):
    for half in range(2):
        line = jnp.broadcast_to(line_ref[0, half : half + 1, :], (QB, SKEW))
        bias_ref[half] = pltpu.roll(line, 0, 1, stride=1, stride_axis=0).T


def both_heads(block):
    zero = jnp.zeros_like(block)
    return jnp.concatenate(
        [
            jnp.where(half_lanes(block.shape, 0), block, zero),
            jnp.where(half_lanes(block.shape, 1), block, zero),
        ],
        axis=0,
    )


def exp_scores(meta, block, mb, keys, queries_two, bias_ref):
    start = pl.multiple_of((LEN - QB) - QB * meta[3 + block], QB)
    length = meta[6 + 2 * mb + meta[block]]
    bias = jnp.concatenate([bias_ref[0, pl.ds(start, LEN), :], bias_ref[1, pl.ds(start, LEN), :]], axis=1)
    scores = dot(keys, queries_two, NT) + bias
    row = lax.broadcasted_iota(jnp.int32, scores.shape, 0)
    scores = jnp.where(row < length, scores, negative_fill)
    top = jnp.max(scores, axis=0, keepdims=True)
    weights = jnp.exp(scores - top)
    return weights, jnp.sum(weights, axis=0, keepdims=True)


def attend_kernel(meta, q_ref, k_ref, v_ref, line_ref, o_ref, bias_ref):
    mb = pl.program_id(1)

    @pl.when(mb == 0)
    def _():
        make_bias(line_ref, bias_ref)

    for block in range(3):
        rows = pl.ds(pl.multiple_of(meta[block] * LEN, LEN), LEN)
        keys, values = k_ref[0, rows, :], v_ref[0, rows, :]
        queries_two = both_heads(q_ref[0, block * QB : (block + 1) * QB, :])
        weights, total = exp_scores(meta, block, mb, keys, queries_two, bias_ref)
        out_two = dot(values.T, weights.astype(bf16)) / total
        top = lax.broadcasted_iota(jnp.int32, (QB, QB), 0) < DH
        out = jnp.where(top, out_two[:, :QB], out_two[:, QB:])
        o_ref[0, block * QB : (block + 1) * QB, :] = out.T.astype(bf16)


def attend_back_kernel(
    meta, q_ref, k_ref, v_ref, do_ref, line_ref, dq_ref, dk_ref, dv_ref, diag_ref,
    bias_ref, acc_ref, dk_acc, dv_acc,
):
    mb = pl.program_id(1)

    @pl.when(mb == 0)
    def _():
        make_bias(line_ref, bias_ref)
        acc_ref[...] = jnp.zeros_like(acc_ref)

    dk_acc[...] = jnp.zeros_like(dk_acc)
    dv_acc[...] = jnp.zeros_like(dv_acc)
    for block in range(3):
        rows = pl.ds(pl.multiple_of(meta[block] * LEN, LEN), LEN)
        own = slice(block * QB, (block + 1) * QB)
        keys, values = k_ref[0, rows, :], v_ref[0, rows, :]
        queries_two = both_heads(q_ref[0, own, :])
        grad_two = both_heads(do_ref[0, own, :])
        weights, total = exp_scores(meta, block, mb, keys, queries_two, bias_ref)
        soft = weights * (1.0 / total)
        grad_soft = dot(values, grad_two, NT)
        inner = jnp.sum(grad_soft * soft, axis=0, keepdims=True)
        grad_scores = soft * (grad_soft - inner)
        start = pl.multiple_of((LEN - QB) - QB * meta[3 + block], QB)
        acc_ref[0, pl.ds(start, LEN), :] += grad_scores[:, :QB]
        acc_ref[1, pl.ds(start, LEN), :] += grad_scores[:, QB:]
        grad_low = grad_scores.astype(bf16)
        dk_acc[rows, :] += dot(grad_low, queries_two)
        dv_acc[rows, :] += dot(soft.astype(bf16), grad_two)
        dq_two = dot(keys.T, grad_low)
        top = lax.broadcasted_iota(jnp.int32, (QB, QB), 0) < DH
        dq_ref[0, own, :] = jnp.where(top, dq_two[:, :QB], dq_two[:, QB:]).T.astype(bf16)
    dk_ref[0] = dk_acc[...].astype(bf16)
    dv_ref[0] = dv_acc[...].astype(bf16)

    @pl.when(mb == pl.num_programs(1) - 1)
    def _():
        row = lax.broadcasted_iota(jnp.int32, (QB, QB), 0)
        lane = lax.broadcasted_iota(jnp.int32, (QB, QB), 1)
        flip = (row + lane == QB - 1).astype(f32)
        for half in range(2):
            turned = lax.dot_general(flip, acc_ref[half], NT, precision=HIGHEST, preferred_element_type=f32)
            shifted = pltpu.roll(turned, SKEW - QB + 1, 1, stride=1, stride_axis=0)
            diag_ref[0, half : half + 1, :] = jnp.sum(shifted, axis=0, keepdims=True)


def attend(meta, q, k, v, line):
    micro, rows, _ = q.shape
    window = k.shape[1]
    own = pl.BlockSpec((1, rows, QB), lambda p, m, _: (m, 0, p))
    wide = pl.BlockSpec((1, window, QB), lambda p, m, _: (m, 0, p))
    lines = pl.BlockSpec((1, 2, SKEW), lambda p, m, _: (p, 0, 0))
    return pl.pallas_call(
        attend_kernel,
        grid_spec=pltpu.PrefetchScalarGridSpec(
            num_scalar_prefetch=1,
            grid=(PAIRS, micro),
            in_specs=[own, wide, wide, lines],
            out_specs=own,
            scratch_shapes=[pltpu.VMEM((2, SKEW, QB), f32)],
        ),
        out_shape=jax.ShapeDtypeStruct(q.shape, bf16),
        compiler_params=pltpu.CompilerParams(vmem_limit_bytes=40 << 20),
        name="attend",
    )(meta, q, k, v, line)


def attend_back(meta, q, k, v, grad, line):
    micro, rows, _ = q.shape
    window = k.shape[1]
    own = pl.BlockSpec((1, rows, QB), lambda p, m, _: (m, 0, p))
    wide = pl.BlockSpec((1, window, QB), lambda p, m, _: (m, 0, p))
    lines = pl.BlockSpec((1, 2, SKEW), lambda p, m, _: (p, 0, 0))
    return pl.pallas_call(
        attend_back_kernel,
        grid_spec=pltpu.PrefetchScalarGridSpec(
            num_scalar_prefetch=1,
            grid=(PAIRS, micro),
            in_specs=[own, wide, wide, own, lines],
            out_specs=[own, wide, wide, lines],
            scratch_shapes=[
                pltpu.VMEM((2, SKEW, QB), f32),
                pltpu.VMEM((2, SKEW, QB), f32),
                pltpu.VMEM((window, QB), f32),
                pltpu.VMEM((window, QB), f32),
            ],
        ),
        out_shape=[
            jax.ShapeDtypeStruct(q.shape, bf16),
            jax.ShapeDtypeStruct(k.shape, bf16),
            jax.ShapeDtypeStruct(k.shape, bf16),
            jax.ShapeDtypeStruct(line.shape, f32),
        ],
        compiler_params=pltpu.CompilerParams(vmem_limit_bytes=40 << 20),
        name="attend_back",
    )(meta, q, k, v, grad, line)


ROWS = 256


def gelu_and_slope(gate):
    root = 0.7978845608028654
    cube = 0.044715
    square = gate * gate
    bend = jnp.tanh(root * gate * (1.0 + cube * square))
    half = 0.5 * (1.0 + bend)
    slope = half + 0.5 * gate * (1.0 - bend * bend) * (root * (1.0 + 3.0 * cube * square))
    return gate * half, slope


def ffn_kernel(
    y_ref, dy_ref, gain_ref, w_ref, out_ref, dy1_ref, dh1_ref, dgain_ref, grad_ref,
    n_ref, nt_ref, dyt_ref, acc_ref, dn_ref, hid_ref, dgate_ref, dup_ref,
):
    step = pl.program_id(0)
    tokens = y_ref.shape[0]
    width = w_ref.shape[2] // 3
    gate_cols, up_cols, down_cols = (slice(c * width, (c + 1) * width) for c in range(3))

    @pl.when(step == 0)
    def _():
        y = y_ref[...]
        rho = lax.rsqrt(jnp.mean(y * y, axis=-1, keepdims=True) + epsilon)
        normed = (y * rho * gain_ref[...]).astype(bf16)
        n_ref[...] = normed
        nt_ref[...] = normed.T
        dyt_ref[...] = dy_ref[...].T
        acc_ref[...] = y
        dn_ref[...] = jnp.zeros_like(dn_ref)

    def tile(t, _):
        rows = pl.ds(pl.multiple_of(t * ROWS, ROWS), ROWS)
        normed = n_ref[rows, :]
        gate = dot(normed, w_ref[0, :, gate_cols])
        up = dot(normed, w_ref[0, :, up_cols])
        grad_hid = dot(dy_ref[rows, :], w_ref[0, :, down_cols])
        act, slope = gelu_and_slope(gate)
        hid = (act * up).astype(bf16)
        dgate = (grad_hid * up * slope).astype(bf16)
        dup = (grad_hid * act).astype(bf16)
        hid_ref[rows, :] = hid
        dgate_ref[rows, :] = dgate
        dup_ref[rows, :] = dup
        acc_ref[rows, :] += dot(hid, w_ref[0, :, down_cols], NT)
        dn_ref[rows, :] += dot(dgate, w_ref[0, :, gate_cols], NT) + dot(dup, w_ref[0, :, up_cols], NT)
        return 0

    lax.fori_loop(0, tokens // ROWS, tile, 0)

    def grads(t, _):
        rows = pl.ds(pl.multiple_of(t * ROWS, ROWS), ROWS)
        grad_ref[0, rows, gate_cols] = dot(nt_ref[rows, :], dgate_ref[...]).astype(bf16)
        grad_ref[0, rows, up_cols] = dot(nt_ref[rows, :], dup_ref[...]).astype(bf16)
        grad_ref[0, rows, down_cols] = dot(dyt_ref[rows, :], hid_ref[...]).astype(bf16)
        return 0

    lax.fori_loop(0, D // ROWS, grads, 0)

    @pl.when(step == pl.num_programs(0) - 1)
    def _():
        out_ref[...] = acc_ref[...].astype(bf16)
        y = y_ref[...]
        rho = lax.rsqrt(jnp.mean(y * y, axis=-1, keepdims=True) + epsilon)
        scaled_y = y * rho
        dn = dn_ref[...]
        dgain_ref[...] = jnp.sum(dn * scaled_y, axis=0, keepdims=True)
        u = dn * gain_ref[...]
        inner = jnp.mean(u * scaled_y, axis=-1, keepdims=True)
        dy1 = dy_ref[...].astype(f32) + rho * (u - scaled_y * inner)
        dy1_ref[...] = dy1
        dh1_ref[...] = dy1.astype(bf16)


def ffn(y, dy, gain, weights):
    tokens = y.shape[0]
    groups, _, columns = weights.shape
    width = columns // 3
    whole = pl.BlockSpec((tokens, D), lambda m: (0, 0))
    one = pl.BlockSpec((1, D), lambda m: (0, 0))
    group = pl.BlockSpec((1, D, columns), lambda m: (m, 0, 0))
    return pl.pallas_call(
        ffn_kernel,
        grid=(groups,),
        in_specs=[whole, whole, one, group],
        out_specs=[whole, whole, whole, one, group],
        out_shape=[
            jax.ShapeDtypeStruct((tokens, D), bf16),
            jax.ShapeDtypeStruct((tokens, D), f32),
            jax.ShapeDtypeStruct((tokens, D), bf16),
            jax.ShapeDtypeStruct((1, D), f32),
            jax.ShapeDtypeStruct(weights.shape, bf16),
        ],
        scratch_shapes=[
            pltpu.VMEM((tokens, D), bf16),
            pltpu.VMEM((D, tokens), bf16),
            pltpu.VMEM((D, tokens), bf16),
            pltpu.VMEM((tokens, D), f32),
            pltpu.VMEM((tokens, D), f32),
            pltpu.VMEM((tokens, width), bf16),
            pltpu.VMEM((tokens, width), bf16),
            pltpu.VMEM((tokens, width), bf16),
        ],
        compiler_params=pltpu.CompilerParams(vmem_limit_bytes=52 << 20),
        name="ffn",
    )(y, dy, gain, weights)


def grams_of(blocks):
    return jnp.einsum("our,ouw->orw", blocks, blocks, precision=HIGHEST)


def orthogonal(blocks, gram):
    total = jnp.trace(gram, axis1=1, axis2=2)[:, None, None]
    mul = functools.partial(jnp.einsum, "oij,ojk->oik", precision=HIGH)
    first = gram / total
    start = blocks * lax.rsqrt(total)
    eye = jnp.eye(gram.shape[1], dtype=f32)[None]
    step = linear_coefficient * eye + coef_second * first + coef_third * mul(first, first)
    second = mul(mul(first, step), step)
    once = mul(start, step)
    turn = mul(once, second)
    return linear_coefficient * once + coef_second * turn + coef_third * mul(turn, second)


def adam_update(param, grad, first, second):
    first_new = beta_one * first + (1.0 - beta_one) * grad
    second_new = beta_two * second + (1.0 - beta_two) * grad * grad
    corrected_first = first_new / (1.0 - beta_one**STEP)
    corrected_second = second_new / (1.0 - beta_two**STEP)
    return (
        first_new,
        second_new,
        param - adam_rate * corrected_first / (jnp.sqrt(corrected_second) + adam_epsilon),
    )


def gather_blocks(shard):
    n_dp, n_mp = lax.axis_size("dp"), lax.axis_size("mp")
    rows, columns = shard.shape
    whole = lax.all_gather(shard, ("dp", "mp"), axis=0, tiled=False)
    return whole.reshape(n_dp, n_mp, rows, columns).transpose(1, 0, 2, 3).reshape(n_mp, n_dp * rows, columns)


def scatter_blocks(grads):
    n_dp, n_mp = lax.axis_size("dp"), lax.axis_size("mp")
    _, all_rows, columns = grads.shape
    rows = all_rows // n_dp
    parts = grads.reshape(n_mp, n_dp, rows, columns).transpose(1, 0, 2, 3).reshape(n_dp * n_mp * rows, columns)
    return lax.psum_scatter(parts, ("dp", "mp"), scatter_dimension=0, tiled=True).astype(f32)


def shards(
    tokens, lengths, cotangent, attn_in, attn_out, ffn_in, ffn_out, gains, table,
    attn_in_mom, attn_out_mom, ffn_in_mom, ffn_out_mom,
    gain_first, gain_second, table_first, table_second,
):
    micro, own_rows, _ = tokens.shape
    here = lax.axis_index("mp")
    n_mp = lax.axis_size("mp")
    width = attn_in.shape[2]
    heads_dev = table.shape[1]

    attn_low = jnp.concatenate([attn_in[0], attn_in[1], attn_in[2], attn_out.T], axis=1).astype(bf16)
    ffn_low = jnp.concatenate([ffn_in[0], ffn_in[1], ffn_out.T], axis=1).astype(bf16)
    gain_low = lax.all_gather(gains.astype(bf16), "dp", axis=1, tiled=True).astype(f32)
    table_all = lax.all_gather(table, "mp", axis=1, tiled=True)
    attn_all = gather_blocks(attn_low)
    ffn_all = gather_blocks(ffn_low)
    w_q, w_k, w_v, w_o = (
        attn_all.reshape(n_mp, D, 4, width).transpose(2, 1, 0, 3).reshape(4, D, n_mp * width)
    )

    onehot = skew_onehot()
    line = lax.dot_general(
        table_all, onehot, (((0,), (1,)), ((), ())), precision=HIGHEST, preferred_element_type=f32
    ).reshape(PAIRS, 2, SKEW)

    first_row = own_rows * here
    first_doc = first_row // LEN
    inset = first_row - first_doc * LEN
    before = lax.ppermute(tokens, "mp", [(j, j + 1) for j in range(n_mp - 1)])
    after = lax.ppermute(tokens, "mp", [(j + 1, j) for j in range(n_mp - 1)])
    side = jnp.concatenate([before, tokens, after, jnp.zeros((micro, 2 * LEN - own_rows - own_rows + QB, D), bf16)], axis=1)
    window = lax.dynamic_slice_in_dim(side, own_rows - inset, 2 * LEN, axis=1)
    block_place = first_row // QB + jnp.arange(own_rows // QB, dtype=jnp.int32)
    slot = block_place // (LEN // QB) - first_doc
    lens_window = lax.dynamic_slice_in_dim(
        jnp.concatenate([lengths, jnp.ones((micro, 1), lengths.dtype)], axis=1), first_doc, 2, axis=1
    )
    meta = jnp.concatenate([slot, block_place % (LEN // QB), lens_window.reshape(-1)]).astype(jnp.int32)

    def unit(rows):
        return rows * lax.rsqrt(jnp.mean(rows * rows, axis=-1, keepdims=True) + epsilon)

    rows = tokens.reshape(micro * own_rows, D).astype(f32)
    normed_own = (unit(rows) * gain_low[0]).astype(bf16)
    window_rows = window.reshape(micro * 2 * LEN, D).astype(f32)
    normed_window = (unit(window_rows) * gain_low[0]).astype(bf16)
    q = dot(normed_own, w_q).astype(bf16).reshape(micro, own_rows, D)
    k = dot(normed_window, w_k).astype(bf16).reshape(micro, 2 * LEN, D)
    v = dot(normed_window, w_v).astype(bf16).reshape(micro, 2 * LEN, D)
    attended = attend(meta, q, k, v, line).reshape(micro * own_rows, D)
    middle = rows + dot(attended, w_o, NT)

    dy = cotangent.reshape(micro * own_rows, D)
    output, grad_middle, grad_mid_low, grad_gain_two, grad_ffn = ffn(middle, dy, gain_low[1:2], ffn_all)
    shard_ffn = scatter_blocks(grad_ffn)

    grad_w_o = dot(grad_mid_low, attended, TN)
    grad_att = dot(grad_mid_low, w_o).astype(bf16).reshape(micro, own_rows, D)
    grad_q, grad_k, grad_v, diag = attend_back(meta, q, k, v, grad_att, line)
    grad_q = grad_q.reshape(micro * own_rows, D)
    grad_k = grad_k.reshape(micro * 2 * LEN, D)
    grad_v = grad_v.reshape(micro * 2 * LEN, D)
    grad_w_q = dot(normed_own, grad_q, TN)
    grad_w_k = dot(normed_window, grad_k, TN)
    grad_w_v = dot(normed_window, grad_v, TN)
    grad_attn = (
        jnp.stack([grad_w_q, grad_w_k, grad_w_v, grad_w_o])
        .astype(bf16)
        .reshape(4, D, n_mp, width)
        .transpose(2, 1, 0, 3)
        .reshape(n_mp, D, 4 * width)
    )
    shard_attn = scatter_blocks(grad_attn)

    grad_normed_own = dot(grad_q, w_q, NT)
    grad_normed_window = (dot(grad_k, w_k, NT) + dot(grad_v, w_v, NT)).reshape(micro, 2 * LEN, D)
    grad_side = lax.dynamic_update_slice_in_dim(
        jnp.zeros(side.shape, f32), grad_normed_window, own_rows - inset, axis=1
    )
    own_part = grad_side[:, own_rows : 2 * own_rows].reshape(micro * own_rows, D) + grad_normed_own
    back = lax.ppermute(grad_side[:, :own_rows].astype(bf16), "mp", [(j + 1, j) for j in range(n_mp - 1)])
    forth = lax.ppermute(
        grad_side[:, 2 * own_rows : 3 * own_rows].astype(bf16), "mp", [(j, j + 1) for j in range(n_mp - 1)]
    )
    grad_normed = own_part + (back.astype(f32) + forth.astype(f32)).reshape(micro * own_rows, D)
    rho = lax.rsqrt(jnp.mean(rows * rows, axis=-1, keepdims=True) + epsilon)
    grad_gain_one = jnp.sum(grad_normed * rows * rho, axis=0, keepdims=True)
    u = grad_normed * gain_low[0]
    tokens_grad = grad_middle + rho * (u - rows * rho * rho * jnp.mean(u * rows, axis=-1, keepdims=True))

    table_sum = lax.dot_general(
        onehot, diag.reshape(H, SKEW), (((0,), (1,)), ((), ())), precision=HIGHEST, preferred_element_type=f32
    )
    gain_sum = jnp.concatenate([grad_gain_one, grad_gain_two])
    gain_sum, table_sum = lax.psum((gain_sum, table_sum), ("dp", "mp"))
    gain_grad = lax.dynamic_slice_in_dim(gain_sum, lax.axis_index("dp") * gains.shape[1], gains.shape[1], axis=1)
    table_grad = lax.dynamic_slice_in_dim(table_sum, here * heads_dev, heads_dev, axis=1)

    rows_dev = attn_in.shape[1]
    width_ffn = ffn_in.shape[2]
    parts_attn = shard_attn.reshape(rows_dev, 4, width).transpose(1, 0, 2)
    parts_ffn = shard_ffn.reshape(rows_dev, 3, width_ffn).transpose(1, 0, 2)
    mom_in = momentum_decay * attn_in_mom + parts_attn[:3]
    mom_out_t = momentum_decay * attn_out_mom.T + parts_attn[3]
    mom_fin = momentum_decay * ffn_in_mom + parts_ffn[:2]
    mom_fout_t = momentum_decay * ffn_out_mom.T + parts_ffn[2]
    blocks_attn = jnp.concatenate([mom_in, mom_out_t[None]])
    blocks_ffn = jnp.concatenate([mom_fin, mom_fout_t[None]])
    gram_ffn = lax.psum(grams_of(blocks_ffn), "dp")
    gram_attn = lax.psum(grams_of(blocks_attn), "dp")
    orth_ffn = orthogonal(blocks_ffn, gram_ffn)
    orth_attn = orthogonal(blocks_attn, gram_attn)
    attn_in_next = attn_in * (1.0 - rate_attn_in * decay_rate) - rate_attn_in * orth_attn[:3]
    attn_out_next = attn_out * (1.0 - rate_attn_out * decay_rate) - rate_attn_out * orth_attn[3].T
    ffn_in_next = ffn_in * (1.0 - rate_ffn_in * decay_rate) - rate_ffn_in * orth_ffn[:2]
    ffn_out_next = ffn_out * (1.0 - rate_ffn_out * decay_rate) - rate_ffn_out * orth_ffn[2].T
    gain_first_next, gain_second_next, gains_next = adam_update(gains, gain_grad, gain_first, gain_second)
    table_first_next, table_second_next, table_next = adam_update(table, table_grad, table_first, table_second)
    return (
        output.reshape(tokens.shape),
        tokens_grad.reshape(tokens.shape),
        attn_in_next,
        attn_out_next,
        ffn_in_next,
        ffn_out_next,
        mom_in,
        mom_out_t.T,
        mom_fin,
        mom_fout_t.T,
        gain_first_next,
        gain_second_next,
        gains_next,
        table_first_next,
        table_second_next,
        table_next,
    )


def solution(mesh):
    token = P(None, ("dp", "mp"), None)
    columns = P(None, "dp", "mp")
    flipped = P("mp", "dp")
    gain = P(None, "dp")
    head = P(None, "mp")
    return jax.shard_map(
        shards,
        mesh=mesh,
        in_specs=(
            token, P(None, "dp"), token, columns, flipped, columns, flipped, gain, head,
            columns, flipped, columns, flipped, gain, gain, head, head,
        ),
        out_specs=(
            token, token, columns, flipped, columns, flipped, columns, flipped, columns, flipped,
            gain, gain, gain, head, head, head,
        ),
        check_vma=False,
    )
```

time: 1310 us -> 670 us (0.51)
  waiting for transfers between devices: 578 us -> 256 us
  matrix products: 336 us -> 57 us
  local copies, waits for them, and re-layouts: 194 us -> 83.1 us
  Pallas kernels: 0 us -> 99.9 us
  other arithmetic: 98.5 us -> 38.2 us
  blocking collectives: 70 us -> 95.4 us
    dot_general x76 -> x28, matrix products: 329 us -> 57 us  [the longest x12 30.6 us: dot(): return lax.dot_general(a, b, dims, preferred_element_type=f32)]
    all_gather x9 -> x2, waiting for transfers between devices: 237 us -> 21.5 us  [gather_blocks(): whole = lax.all_gather(shard, ('dp', 'mp'), axis=0, tiled=False)]
    pallas_call x0 -> x3, Pallas kernels: none -> 99.9 us  [the longest x1 41.4 us: attend_back(): pl.pallas_call(attend_back_kernel, grid_spec=pltpu.PrefetchScalarGridSpec...]
    unnamed x342 -> x95, local copies, waits for them, and re-layouts: 89.1 us -> 11.2 us
    unnamed x29 -> x5, waiting for transfers between devices: 61.2 us -> 0.08 us
    reduce_scatter x8 -> x2, waiting for transfers between devices: 253 us -> 211 us  [scatter_blocks(): lax.psum_scatter(parts, ('dp', 'mp'), scatter_dimension=0, tiled=True)]
    reduce_sum x15 -> x4, other arithmetic: 36.6 us -> 6.26 us  [the longest x2 4.35 us: unit(): jnp.mean(rows * rows, axis=-1, keepdims=True) + epsilon]
    another operation x39 -> x3, local copies, waits for them, and re-layouts: 46.7 us -> 26.2 us  [the longest x1 11.5 us: scatter_blocks(): grads.reshape(n_mp, n_dp, rows, columns).transpose(1, 0, 2, 3)]
  transfers between devices with their start and end apart: 24 -> 9, of which waited for: 17 -> 4; matrix products, arithmetic and copies ran while one was open for 41% -> 16% of each run, Pallas kernels for 0% -> 4%
where the time goes in v1:
time: 670 us; the launch traced here: 659 us
  waiting for transfers between devices  256 us (38%)
  Pallas kernels  99.9 us (15%)
  blocking collectives  95.4 us (14%)
  local copies, waits for them, and re-layouts  83.1 us (12%)
  matrix products  57 us (9%)
  other arithmetic  38.2 us (6%)
  between operations  15.2 us (2%)
  starting transfers between devices  13.8 us (2%)
    reduce_scatter x2, waiting for transfers between devices, scatter_blocks(): lax.psum_scatter(parts, ('dp', 'mp'), scatter_dimension=0, tiled=True)  211 us
    all_gather x1, blocking collectives, shards(): table_all = lax.all_gather(table, 'mp', axis=1, tiled=True)  45.4 us
    pallas_call x1, Pallas kernels, attend_back(): pl.pallas_call(attend_back_kernel, grid_spec=pltpu.PrefetchScalarGridSpec...  41.4 us
    psum x1, blocking collectives, shards(): gain_sum, table_sum = lax.psum((gain_sum, table_sum), ('dp', 'mp'))  41.2 us
    pallas_call x1, Pallas kernels, ffn(): pl.pallas_call(ffn_kernel, grid=(groups,), in_specs=[whole, whole, one, g...  35.4 us
    dot_general x12, matrix products, dot(): return lax.dot_general(a, b, dims, preferred_element_type=f32)  30.6 us
    psum x1, waiting for transfers between devices, shards(): gram_attn = lax.psum(grams_of(blocks_attn), 'dp')  23.3 us
    pallas_call x1, Pallas kernels, attend(): pl.pallas_call(attend_kernel, grid_spec=pltpu.PrefetchScalarGridSpec(num_...  23.1 us
  transfers between devices with their start and end apart: 9, of which 4 were waited for; matrix products, arithmetic and copies ran while one was open for 16% of the time, Pallas kernels for 4%

profile of v1, /device:TPU:0, one launch (start us, length us, event | category | flops | bytes accessed | tf_op | source)
XLA Modules:
  0.0 658.8 jit_solution(2159305959582086460)
XLA Ops:
  13.1 5.0 collective-permute-start
  19.4 45.4 %all-gather.1 = f32[4,3,32]{2,1,0:T(4,128)S(1)} all-gather(f32[1,3,32]{2,1,0:T(4,128)S(1)} %bitcast.248), channel_id=1, replica_groups=mesh['dp'=8,'mp'=4] {'mp'}, dimensions={0}, use_global_device_ids=true | all-gather | bytes 1920 | tf_op jit(solution)/shard_map/all_gather | solution.py:379
  64.9 8.8 %all-gather = bf16[8,96,2]{1,2,0:T(2,128)(2,1)S(1)} all-gather(bf16[1,96,2]{1,2,0:T(2,128)(2,1)S(1)} %convert_bitcast_fusion.2), channel_id=1, replica_groups=mesh['dp'=8,'mp'=4] {'dp'}, dimensions={0}, use_global_device_ids=true | all-gather | bytes 3456 | tf_op jit(solution)/shard_map/all_gather | solution.py:378
  76.4 4.0 fusion
  83.0 8.6 %copy.84 = bf16[8,4,96,768]{2,0,3,1:T(8,128)(2,1)} copy(bf16[8,4,96,768]{3,2,1,0:T(8,128)(2,1)} %bitcast.226) | data formatting | bytes 9437184 | tf_op jit(solution)/shard_map/reshape | solution.py:354
  91.6 10.9 %reshape_reshape.6 = bf16[4,768,4,192]{1,3,2,0:T(8,128)(2,1)} reshape(bf16[4,8,96,768]{2,1,3,0:T(8,128)(2,1)} %bitcast.217) | data formatting | bytes 9437184 | tf_op jit(solution)/shard_map/reshape;reshape | solution.py:383
  102.5 3.8 fusion.75
  109.4 2.9 convolution_convert_fusion
  112.3 2.9 convolution_convert_fusion.1
  115.2 23.1 %attend.1 = bf16[2,384,768]{2,1,0:T(8,128)(2,1)S(1)} custom-call(s32[10]{0:T(128)S(1)} %pad_add_fusion.meta, bf16[2,384,768]{2,1,0:T(8,128)(2,1)S(1)} %bitcast.207, bf16[2,1024,768]{2,1,0:T(8,128)(2,1)S(1)} %bitcast.205, bf16[2,1024,768]{2,1,0:T(8,128)(2,1)S(1)} %bitcast.203, f32[6,2,1024]{2,1,0:T(2,128)S(1)} %reshape.364.line_ref), custom_call_target="tpu_custom_call" | custom-call | tf_op jit(solution)/shard_map/attend/pallas_call | solution.py:165
  139.9 4.1 bitcast_add_fusion.2.y_ref
  144.0 21.5 %all-gather.7.cloned.1.call-done = bf16[32,96,1536]{2,1,0:T(8,128)(2,1)} async-done(((bf16[1,96,1536]{2,1,0:T(8,128)(2,1)}), bf16[32,96,1536]{2,1,0:T(8,128)(2,1)}) %all-gather.7.cloned.1.call-update) | async-done | bytes 9437200 | tf_op jit(solution)/shard_map/all_gather | solution.py:353
  165.5 8.3 %copy.85 = bf16[8,4,96,1536]{3,2,0,1:T(8,128)(2,1)} copy(bf16[8,4,96,1536]{3,2,1,0:T(8,128)(2,1)} %bitcast.221) | data formatting | bytes 18874368 | tf_op jit(solution)/shard_map/reshape | solution.py:354
  173.8 35.4 %ffn.1 = (bf16[768,768]{1,0:T(8,128)(2,1)}, f32[768,768]{1,0:T(8,128)}, bf16[768,768]{1,0:T(8,128)(2,1)S(1)}, f32[1,768]{1,0:T(1,128)S(1)}, bf16[4,768,1536]{2,1,0:T(8,128)(2,1)}) custom-call(f32[768,768]{1,0:T(8,128)} %bitcast_add_fusion.2.y_ref, bf16[768,768]{1,0:T(8,128)(2,1)} %bitcast.246, f32[1,768]{1,0:T(1,128)S(1)} %get-tuple-element.127.gain_ref, ...), custom_call_target="tpu_custom_call" | custom-call | tf_op jit(solution)/shard_map/ffn/pallas_call | solution.py:294
  212.7 41.4 %attend_back.1 = (bf16[2,384,768]{2,1,0:T(8,128)(2,1)S(1)}, bf16[2,1024,768]{2,1,0:T(8,128)(2,1)S(1)}, bf16[2,1024,768]{2,1,0:T(8,128)(2,1)S(1)}, f32[6,2,1024]{2,1,0:T(2,128)S(1)}) custom-call(s32[10]{0:T(128)S(1)} %pad_add_fusion.meta, bf16[2,384,768]{2,1,0:T(8,128)(2,1)S(1)} %bitcast.208, bf16[2,1024,768]{2,1,0:T(8,128)(2,1)S(1)} %bitcast.206, ...), custom_call_target="tpu_custom_call" | custom-call | tf_op jit(solution)/shard_map/attend_back/pallas_call | solution.py:186
  266.8 11.5 %reshape_reshape.7 = bf16[4,8,96,768]{2,1,3,0:T(8,128)(2,1)} reshape(bf16[4,768,4,192]{1,3,2,0:T(8,128)(2,1)} %copy.90) | data formatting | bytes 9437184 | tf_op jit(solution)/shard_map/reshape;reshape | solution.py:361
  278.3 8.5 %copy.91 = bf16[8,4,96,768]{3,2,1,0:T(8,128)(2,1)} copy(bf16[8,4,96,768]{2,0,3,1:T(8,128)(2,1)} %bitcast.218) | data formatting | bytes 9437184 | tf_op jit(solution)/shard_map/transpose | solution.py:361
  286.9 8.3 %copy.96 = bf16[4,8,96,1536]{3,2,0,1:T(8,128)(2,1)} copy(bf16[4,8,96,1536]{3,2,1,0:T(8,128)(2,1)} %bitcast.222) | data formatting | bytes 18874368 | tf_op jit(solution)/shard_map/reshape | solution.py:361
  299.4 5.1 fusion.79
  304.5 2.9 convolution_add_fusion
  313.0 3.3 fusion.74
  317.6 5.8 collective-permute-start.3
  324.4 74.8 %reduce-scatter.3.cloned.1.call-done = bf16[96,768]{1,0:T(8,128)(2,1)} async-done(((bf16[3072,768]{1,0:T(8,128)(2,1)}), bf16[96,768]{1,0:T(8,128)(2,1)}) %reduce-scatter.3.cloned.1.call-update) | async-done | bytes 147472 | tf_op jit(solution)/shard_map/reduce_scatter | solution.py:362
  404.0 136.7 %reduce-scatter.5.cloned.1.call-done = bf16[96,1536]{1,0:T(8,128)(2,1)} async-done(((bf16[3072,1536]{1,0:T(8,128)(2,1)}), bf16[96,1536]{1,0:T(8,128)(2,1)}) %reduce-scatter.5.cloned.1.call-update) | async-done | bytes 294928 | tf_op jit(solution)/shard_map/reduce_scatter | solution.py:362
  545.3 4.3 fusion.38
  552.4 3.0 fusion.22
  555.4 41.2 %all-reduce.1 = (f32[2,768]{1,0:T(2,128)S(1)}, f32[32,12]{0,1:T(8,128)S(1)}) all-reduce(f32[2,768]{1,0:T(2,128)S(1)} %pad_maximum_fusion.8, f32[32,12]{0,1:T(8,128)} %fusion.83), channel_id=1, replica_groups=mesh['dp'=8,'mp'=4] {'dp','mp'}, use_global_device_ids=true, to_apply=%region_10.11 | all-reduce | flops 1920 | bytes 15360 | tf_op jit(solution)/shard_map/psum | solution.py:460
  599.3 4.5 fusion.19
  604.6 23.3 %all-reduce.5.cloned.1.call-done = (f32[4,192,192]{2,1,0:T(8,128)}, f32[3,512,512]{2,1,0:T(8,128)}) async-done(((f32[4,192,192]{2,1,0:T(8,128)}, f32[3,512,512]{2,1,0:T(8,128)}), (f32[4,192,192]{2,1,0:T(8,128)}, f32[3,512,512]{2,1,0:T(8,128)})) %all-reduce.5.cloned.1.call-update) | async-done | bytes 3735568 | tf_op jit(solution)/shard_map/psum | solution.py:475
  635.5 2.9 fusion.70
  638.5 3.3 fusion.7
  643.4 3.6 fusion.6
  (189 shorter events, 74.5 us)
Async XLA Ops:
  7.2 66.5 %copy-start.16 = (f32[1024,32]{1,0:T(8,128)S(1)}, f32[1024,32]{1,0:T(8,128)}, u32[]{:S(2)}) copy-start(f32[1024,32]{1,0:T(8,128)} %constant.166.clone) | copy-start | bytes 393220
  7.2 5.9 copy-start.8
  7.2 12.2 %copy-start.42 = (f32[32,3]{0,1:T(4,128)S(1)}, f32[32,3]{0,1:T(4,128)}, u32[]{:S(2)}) copy-start(f32[32,3]{0,1:T(4,128)} %param.26) | copy-start | bytes 1156
  7.2 57.7 %copy-start.43 = (f32[2,96]{1,0:T(2,128)S(1)}, f32[2,96]{1,0:T(2,128)}, u32[]{:S(2)}) copy-start(f32[2,96]{1,0:T(2,128)} %param.25) | copy-start | bytes 2308
  7.2 67.0 %copy-start.44 = (s32[2,3]{1,0:T(2,128)S(1)}, s32[2,3]{1,0:T(2,128)}, u32[]{:S(2)}) copy-start(s32[2,3]{1,0:T(2,128)} %param.19) | copy-start | bytes 76
  7.2 75.7 %all-gather.5.cloned.1.call-start = ((), (), s32[]{:S(2)}) async-start(), calls=%async_computation.2 | async-start | bytes 4866048 | tf_op jit(solution)/shard_map/all_gather | solution.py:353
  8.4 66.1 %copy-start.32 = (f32[192,96]{0,1:T(8,128)}, f32[192,96]{0,1:T(8,128)S(1)}, u32[]{:S(2)}) copy-start(f32[192,96]{0,1:T(8,128)S(1)} %copy.83) | copy-start | bytes 221188
  10.2 155.3 %all-gather.7.cloned.1.call-start = ((), (), s32[]{:S(2)}) async-start(), calls=%async_computation.3 | async-start | bytes 9732096 | tf_op jit(solution)/shard_map/all_gather | solution.py:353
  13.0 386.1 %reduce-scatter.3.cloned.1.call-start = ((), (), s32[]{:S(2)}) async-start(), calls=%async_computation.4 | async-start | bytes 4866048 | tf_op jit(solution)/shard_map/reduce_scatter | solution.py:362
  13.1 63.3 %collective-permute-start = (bf16[2,384,768]{2,1,0:T(8,128)(2,1)S(1)}, bf16[2,384,768]{2,1,0:T(8,128)(2,1)S(1)}, u32[]{:S(2)}, u32[]{:S(2)}) collective-permute-start(bf16[2,384,768]{2,1,0:T(8,128)(2,1)S(1)} %copy-done.8), channel_id=1, source_target_pairs={{0,1},{1,2},{2,3},{4,5},{5,6},{6,7},{8,9},{9,10},{10,11},{12,13},{... | collective-permute-start | bytes 3538952 | tf_op jit(solution)/shard_map/ppermute | solution.py:394
  18.1 58.3 %collective-permute-start.1 = (bf16[2,384,768]{2,1,0:T(8,128)(2,1)S(1)}, bf16[2,384,768]{2,1,0:T(8,128)(2,1)}, u32[]{:S(2)}, u32[]{:S(2)}) collective-permute-start(bf16[2,384,768]{2,1,0:T(8,128)(2,1)S(1)} %copy-done.8), channel_id=1, source_target_pairs={{1,0},{2,1},{3,2},{5,4},{6,5},{7,6},{9,8},{10,9},{11,10},{13,12},{... | collective-permute-start | bytes 3538952 | tf_op jit(solution)/shard_map/ppermute | solution.py:395
  102.5 3.8 copy-start.24
  106.3 6.0 copy-start.20
  106.3 6.1 copy-start.22
  107.4 7.8 %copy-start.3 = (bf16[768,768]{1,0:T(8,128)(2,1)}, bf16[768,768]{1,0:T(8,128)(2,1)S(1)}, u32[]{:S(2)}) copy-start(bf16[768,768]{1,0:T(8,128)(2,1)S(1)} %convolution_convert_fusion.4) | copy-start | bytes 3538948
  115.2 23.2 %copy-start.1 = (bf16[2048,768]{1,0:T(8,128)(2,1)}, bf16[2048,768]{1,0:T(8,128)(2,1)S(1)}, u32[]{:S(2)}) copy-start(bf16[2048,768]{1,0:T(8,128)(2,1)S(1)} %convolution_convert_fusion.1) | copy-start | bytes 9437188
  173.8 35.4 %copy-start.23 = (bf16[1,768,4,192]{1,3,0,2:T(8,128)(2,1)S(1)}, bf16[1,768,4,192]{1,3,0,2:T(8,128)(2,1)}, u32[]{:S(2)}) copy-start(bf16[1,768,4,192]{1,3,0,2:T(8,128)(2,1)} %get-tuple-element.114) | copy-start | bytes 3538948
  212.7 41.4 %copy-start.25 = (bf16[2,384,768]{2,1,0:T(8,128)(2,1)S(1)}, bf16[2,384,768]{2,1,0:T(8,128)(2,1)}, u32[]{:S(2)}) copy-start(bf16[2,384,768]{2,1,0:T(8,128)(2,1)} %fusion.14) | copy-start | bytes 3538948
  254.1 6.8 %copy-start.5 = (bf16[2,1024,768]{2,1,0:T(8,128)(2,1)}, bf16[2,1024,768]{2,1,0:T(8,128)(2,1)S(1)}, u32[]{:S(2)}) copy-start(bf16[2,1024,768]{2,1,0:T(8,128)(2,1)S(1)} %get-tuple-element.29) | copy-start | bytes 9437188
  254.1 4.2 copy-start.13
  286.9 253.8 %reduce-scatter.5.cloned.1.call-start = ((), (), s32[]{:S(2)}) async-start(), calls=%async_computation.5 | async-start | bytes 9732096 | tf_op jit(solution)/shard_map/reduce_scatter | solution.py:362
  295.3 332.6 %all-reduce.5.cloned.1.call-start = ((), (), s32[]{:S(2)}) async-start(), calls=%async_computation.6 | async-start | bytes 7864320 | tf_op jit(solution)/shard_map/psum | solution.py:475
  299.4 5.1 copy-start.6
  299.4 5.1 copy-start.21
  316.3 233.4 %collective-permute-start.2 = (bf16[2,384,768]{2,1,0:T(8,128)(2,1)}, bf16[2,384,768]{2,1,0:T(8,128)(2,1)}, u32[]{:S(2)}, u32[]{:S(2)}) collective-permute-start(bf16[2,384,768]{2,1,0:T(8,128)(2,1)} %get-tuple-element.112), channel_id=1, source_target_pairs={{1,0},{2,1},{3,2},{5,4},{6,5},{7,6},{9,8},{10,9},{11,10},{13,12},{... | collective-permute-start | bytes 3538952 | tf_op jit(solution)/shard_map/ppermute | solution.py:446
  317.6 232.1 %collective-permute-start.3 = (bf16[2,384,768]{2,1,0:T(8,128)(2,1)}, bf16[2,384,768]{2,1,0:T(8,128)(2,1)}, u32[]{:S(2)}, u32[]{:S(2)}) collective-permute-start(bf16[2,384,768]{2,1,0:T(8,128)(2,1)} %get-tuple-element.113), channel_id=1, source_target_pairs={{0,1},{1,2},{2,3},{4,5},{5,6},{6,7},{8,9},{9,10},{10,11},{12,13},{... | collective-permute-start | bytes 3538952 | tf_op jit(solution)/shard_map/ppermute | solution.py:447
  401.1 140.6 %copy-start.30 = (f32[1,96,192]{2,1,0:T(8,128)}, f32[1,96,192]{2,1,0:T(8,128)S(1)}, u32[]{:S(2)}) copy-start(f32[1,96,192]{2,1,0:T(8,128)S(1)} %get-tuple-element.121) | copy-start | bytes 221188
  402.2 147.4 %copy-start.14 = (f32[3,96,192]{2,1,0:T(8,128)}, f32[3,96,192]{2,1,0:T(8,128)S(1)}, u32[]{:S(2)}) copy-start(f32[3,96,192]{2,1,0:T(8,128)S(1)} %slice_add_fusion.1) | copy-start | bytes 663556
  543.4 6.2 copy-start.34
  599.3 4.5 copy-start.38
  599.3 28.5 %copy-start.39 = (pred[192,192]{1,0:T(8,128)(4,1)S(1)}, pred[192,192]{1,0:T(8,128)(4,1)}, u32[]{:S(2)}) copy-start(pred[192,192]{1,0:T(8,128)(4,1)} %iota_compare_fusion.1) | copy-start | bytes 110596
  599.3 29.9 %copy-start.40 = (f32[192,192]{1,0:T(8,128)S(1)}, f32[192,192]{1,0:T(8,128)}, u32[]{:S(2)}) copy-start(f32[192,192]{1,0:T(8,128)} %broadcast_select_fusion.1) | copy-start | bytes 442372
  (22 other events, 43.8 us)
Sparse Core Ops, SparseCore 0:
  11.4 69.7 all-gather.4
  84.7 80.8 all-gather.6
  287.0 112.1 reduce-scatter.2
  405.9 134.7 reduce-scatter.4
  549.8 78.0 all-reduce.4

commit v2 on v1

v2 whole, which is shorter than its diff:
```python
import functools

import jax
import jax.numpy as jnp
import numpy as np
from jax import lax
from jax.experimental import pallas as pl
from jax.experimental.pallas import tpu as pltpu
from jax.sharding import PartitionSpec as P

D = 768
H = 12
DH = 64
BUCKETS = 32
LEN = 512
STEP = 8
QB = 128
SKEW = 1024
PAIRS = H // 2
TILE = 128
HEAD_ORDER = (0, 1, 3, 4, 6, 7, 9, 10, 2, 5, 8, 11)

epsilon = 1e-06
negative_fill = -1e30
momentum_decay = 0.95
decay_rate = 0.01
linear_coefficient = 3.4445
coef_second = -4.775
coef_third = 2.0315
rate_attn_in = 0.25
rate_attn_out = 12.0
rate_ffn_in = 0.6
rate_ffn_out = 0.3
beta_one = 0.9
beta_two = 0.95
adam_epsilon = 1e-08
adam_rate = 0.3
bucket_marks = (12, 16, 23, 32, 46, 64, 91)

HIGHEST = lax.Precision.HIGHEST
HIGH = lax.Precision.HIGH
bf16 = jnp.bfloat16
f32 = jnp.float32
NN = (((1,), (0,)), ((), ()))
NT = (((1,), (1,)), ((), ()))
TN = (((0,), (0,)), ((), ()))


VMEM_GRANT = 60 << 20
ANY = pl.BlockSpec(memory_space=pltpu.HBM)
SMEM = pl.BlockSpec(memory_space=pltpu.SMEM)
VMEM = pl.BlockSpec(memory_space=pltpu.VMEM)


def dot(a, b, dims=NN):
    return lax.dot_general(a, b, dims, preferred_element_type=f32)


def skew_onehot():
    place = np.arange(SKEW)
    relative = np.where(place < SKEW - QB + 1, place, place - SKEW) - (LEN - QB)
    distance = np.abs(relative)
    far = 8 + sum((distance >= mark).astype(np.int32) for mark in bucket_marks)
    bucket = np.where(distance < 8, distance, far) + 16 * (relative > 0)
    return (bucket[:, None] == np.arange(BUCKETS)[None, :]).astype(np.float32)


def cost(micros):
    return pl.CostEstimate(flops=int(micros * 3e8), bytes_accessed=0, transcendentals=0)


def half_lanes(shape, half):
    lane = lax.broadcasted_iota(jnp.int32, shape, 1)
    return (lane < DH) if half == 0 else (lane >= DH)


def bias_kernel(line_ref, bias_ref):
    for half in range(2):
        line = jnp.broadcast_to(line_ref[0, half : half + 1, :], (QB, SKEW))
        bias_ref[0, half] = pltpu.roll(line, 0, 1, stride=1, stride_axis=0).T


def make_bias(line):
    return pl.pallas_call(
        bias_kernel,
        grid=(PAIRS,),
        compiler_params=pltpu.CompilerParams(vmem_limit_bytes=VMEM_GRANT),
        in_specs=[pl.BlockSpec((1, 2, SKEW), lambda p: (p, 0, 0))],
        out_specs=pl.BlockSpec((1, 2, SKEW, QB), lambda p: (p, 0, 0, 0)),
        out_shape=jax.ShapeDtypeStruct((PAIRS, 2, SKEW, QB), f32),
        cost_estimate=cost(8),
        name="make_bias",
    )(line)


def diag_kernel(acc_ref, diag_ref):
    row = lax.broadcasted_iota(jnp.int32, (QB, QB), 0)
    lane = lax.broadcasted_iota(jnp.int32, (QB, QB), 1)
    flip = (row + lane == QB - 1).astype(f32)
    for half in range(2):
        turned = lax.dot_general(flip, acc_ref[0, half], NT, precision=HIGHEST, preferred_element_type=f32)
        shifted = pltpu.roll(turned, SKEW - QB + 1, 1, stride=1, stride_axis=0)
        diag_ref[0, half : half + 1, :] = jnp.sum(shifted, axis=0, keepdims=True)


def diagonals(acc):
    return pl.pallas_call(
        diag_kernel,
        grid=(PAIRS,),
        compiler_params=pltpu.CompilerParams(vmem_limit_bytes=VMEM_GRANT),
        in_specs=[pl.BlockSpec((1, 2, SKEW, QB), lambda p: (p, 0, 0, 0))],
        out_specs=pl.BlockSpec((1, 2, SKEW), lambda p: (p, 0, 0)),
        out_shape=jax.ShapeDtypeStruct((PAIRS, 2, SKEW), f32),
        cost_estimate=cost(1),
        name="diagonals",
    )(acc)


def both_heads(block):
    zero = jnp.zeros_like(block)
    return jnp.concatenate(
        [
            jnp.where(half_lanes(block.shape, 0), block, zero),
            jnp.where(half_lanes(block.shape, 1), block, zero),
        ],
        axis=0,
    )


def exp_scores(meta, block, mb, keys, queries_two, bias_ref):
    start = pl.multiple_of((LEN - QB) - QB * meta[3 + block], QB)
    length = meta[6 + 2 * mb + meta[block]]
    bias = jnp.concatenate([bias_ref[0, 0, pl.ds(start, LEN), :], bias_ref[0, 1, pl.ds(start, LEN), :]], axis=1)
    scores = dot(keys, queries_two, NT) + bias
    row = lax.broadcasted_iota(jnp.int32, scores.shape, 0)
    scores = jnp.where(row < length, scores, negative_fill)
    top = jnp.max(scores, axis=0, keepdims=True)
    weights = jnp.exp(scores - top)
    return weights, jnp.sum(weights, axis=0, keepdims=True)


def attend_kernel(mb, meta, q_ref, k_ref, v_ref, bias_ref, *refs):
    o_ref = refs[-1]
    for block in range(3):
        rows = pl.ds(pl.multiple_of(meta[block] * LEN, LEN), LEN)
        keys, values = k_ref[0, rows, :], v_ref[0, rows, :]
        queries_two = both_heads(q_ref[0, block * QB : (block + 1) * QB, :])
        weights, total = exp_scores(meta, block, mb, keys, queries_two, bias_ref)
        out_two = dot(values.T, weights.astype(bf16)) / total
        top = lax.broadcasted_iota(jnp.int32, (QB, QB), 0) < DH
        out = jnp.where(top, out_two[:, :QB], out_two[:, QB:])
        o_ref[0, block * QB : (block + 1) * QB, :] = out.T.astype(bf16)


def attend_back_kernel(kept, meta, q_ref, k_ref, v_ref, do_ref, bias_ref, *refs):
    dq_ref, dk_ref, dv_ref, acc_ref, dk_acc, dv_acc = refs[kept:]
    mb = pl.program_id(1)

    @pl.when(mb == 0)
    def _():
        acc_ref[...] = jnp.zeros_like(acc_ref)

    dk_acc[...] = jnp.zeros_like(dk_acc)
    dv_acc[...] = jnp.zeros_like(dv_acc)
    for block in range(3):
        rows = pl.ds(pl.multiple_of(meta[block] * LEN, LEN), LEN)
        own = slice(block * QB, (block + 1) * QB)
        keys, values = k_ref[0, rows, :], v_ref[0, rows, :]
        queries_two = both_heads(q_ref[0, own, :])
        grad_two = both_heads(do_ref[0, own, :])
        weights, total = exp_scores(meta, block, mb, keys, queries_two, bias_ref)
        soft = weights * (1.0 / total)
        grad_soft = dot(values, grad_two, NT)
        inner = jnp.sum(grad_soft * soft, axis=0, keepdims=True)
        grad_scores = soft * (grad_soft - inner)
        start = pl.multiple_of((LEN - QB) - QB * meta[3 + block], QB)
        acc_ref[0, 0, pl.ds(start, LEN), :] += grad_scores[:, :QB]
        acc_ref[0, 1, pl.ds(start, LEN), :] += grad_scores[:, QB:]
        grad_low = grad_scores.astype(bf16)
        dk_acc[rows, :] += dot(grad_low, queries_two)
        dv_acc[rows, :] += dot(soft.astype(bf16), grad_two)
        dq_two = dot(keys.T, grad_low)
        top = lax.broadcasted_iota(jnp.int32, (QB, QB), 0) < DH
        dq_ref[0, own, :] = jnp.where(top, dq_two[:, :QB], dq_two[:, QB:]).T.astype(bf16)
    dk_ref[0] = dk_acc[...].astype(bf16)
    dv_ref[0] = dv_acc[...].astype(bf16)


def attend(meta, q, k, v, bias, mb, earlier=()):
    rows, window = q.shape[1], k.shape[1]
    own = pl.BlockSpec((1, rows, QB), lambda p, _: (mb, 0, p))
    wide = pl.BlockSpec((1, window, QB), lambda p, _: (mb, 0, p))
    lines = pl.BlockSpec((1, 2, SKEW, QB), lambda p, _: (p, 0, 0, 0))
    return pl.pallas_call(
        functools.partial(attend_kernel, mb),
        grid_spec=pltpu.PrefetchScalarGridSpec(
            num_scalar_prefetch=1,
            grid=(PAIRS,),
            in_specs=[own, wide, wide, lines] + [ANY] * len(earlier),
            out_specs=own,
        ),
        out_shape=jax.ShapeDtypeStruct(q.shape, bf16),
        input_output_aliases={5 + j: j for j in range(len(earlier))},
        compiler_params=pltpu.CompilerParams(vmem_limit_bytes=VMEM_GRANT),
        cost_estimate=cost(11),
        name="attend",
    )(meta, q, k, v, bias, *earlier)


def attend_back(meta, q, k, v, grad, bias, pairs, earlier=(), after=()):
    micro, rows, _ = q.shape
    window = k.shape[1]
    first, count = pairs
    own = pl.BlockSpec((1, rows, QB), lambda p, m, _: (m, 0, p + first))
    wide = pl.BlockSpec((1, window, QB), lambda p, m, _: (m, 0, p + first))
    lines = pl.BlockSpec((1, 2, SKEW, QB), lambda p, m, _: (p + first, 0, 0, 0))
    kept = len(earlier) + len(after)
    return pl.pallas_call(
        functools.partial(attend_back_kernel, kept),
        grid_spec=pltpu.PrefetchScalarGridSpec(
            num_scalar_prefetch=1,
            grid=(count, micro),
            in_specs=[own, wide, wide, own, lines] + [ANY] * kept,
            out_specs=[own, wide, wide, lines],
            scratch_shapes=[pltpu.VMEM((window, QB), f32), pltpu.VMEM((window, QB), f32)],
        ),
        out_shape=[
            jax.ShapeDtypeStruct(q.shape, bf16),
            jax.ShapeDtypeStruct(k.shape, bf16),
            jax.ShapeDtypeStruct(k.shape, bf16),
            jax.ShapeDtypeStruct(bias.shape, f32),
        ],
        input_output_aliases={6 + j: j for j in range(len(earlier))},
        compiler_params=pltpu.CompilerParams(vmem_limit_bytes=VMEM_GRANT),
        cost_estimate=cost(7 * count),
        name="attend_back",
    )(meta, q, k, v, grad, bias, *earlier, *after)


PARTS = 8
PART = D // PARTS


def part_rows(place, k):
    return pl.ds(pl.multiple_of((place[0] ^ k) * PART, PART), PART)


def entry_of(place, group):
    return lax.rem(group - place[1] + 4, 4)


def wait_for(ref, sem):
    pltpu.make_async_copy(ref, ref, sem).wait()


def lower_lanes(shape):
    return lax.broadcasted_iota(jnp.int32, shape, 1) < DH


def join_kernel(place, *refs):
    pieces, (w_ref, rest_ref, sems) = refs[:PARTS], refs[-3:]
    for group in range(4):
        entry = entry_of(place, group)
        for k, piece in enumerate(pieces):
            rows = part_rows(place, k)
            lanes = pl.ds(group * TILE, TILE)
            pltpu.make_async_copy(piece.at[entry, pl.ds(0, 4)], w_ref.at[:, rows, lanes], sems.at[0]).start()
            pltpu.make_async_copy(piece.at[entry, pl.ds(4, 2)], rest_ref.at[group, :, rows], sems.at[1]).start()
    wait_for(rest_ref, sems.at[1])
    lower = lower_lanes((D, TILE))
    for two in range(2):
        lanes = slice((4 + two) * TILE, (5 + two) * TILE)
        for both in range(2):
            even, odd = rest_ref[2 * two, both], rest_ref[2 * two + 1, both]
            w_ref[2 * both, :, lanes] = jnp.where(lower, even, odd)
            w_ref[2 * both + 1, :, lanes] = pltpu.roll(jnp.where(lower, odd, even).astype(f32), DH, 1).astype(bf16)
    wait_for(w_ref.at[:, :, pl.ds(0, 4 * TILE)], sems.at[0])


def join(place, pieces, later=()):
    return pl.pallas_call(
        join_kernel,
        in_specs=[SMEM] + [ANY] * (PARTS + len(later)),
        out_specs=VMEM,
        out_shape=jax.ShapeDtypeStruct((4, D, D), bf16),
        scratch_shapes=[pltpu.VMEM((4, 2, D, TILE), bf16), pltpu.SemaphoreType.DMA((2,))],
        compiler_params=pltpu.CompilerParams(vmem_limit_bytes=VMEM_GRANT),
        cost_estimate=cost(5),
        name="join",
    )(place, *pieces, *later)


def project_kernel(x_ref, own_ref, gain_ref, w_ref, *refs):
    q_ref, k_ref, v_ref, n_ref, n_own_ref = refs[-5:]

    def norm(rows):
        rows = rows.astype(f32)
        rho = lax.rsqrt(jnp.mean(rows * rows, axis=-1, keepdims=True) + epsilon)
        return (rows * rho * gain_ref[...]).astype(bf16)

    normed = norm(x_ref[...])
    n_ref[0] = normed
    k_ref[0] = dot(normed, w_ref[1]).astype(bf16)
    v_ref[0] = dot(normed, w_ref[2]).astype(bf16)
    normed = norm(own_ref[0])
    n_own_ref[0] = normed
    q_ref[0] = dot(normed, w_ref[0]).astype(bf16)


PROJECT_STEPS = 4


def project(window, own, gain, weights, mb, earlier=(), later=()):
    micro, own_rows, _ = own.shape
    rows, few = window.shape[0] // PROJECT_STEPS, own_rows // PROJECT_STEPS
    wide = pl.BlockSpec((1, rows, D), lambda t: (mb, t, 0))
    small = pl.BlockSpec((1, few, D), lambda t: (mb, t, 0))
    many_shape = jax.ShapeDtypeStruct((micro, window.shape[0], D), bf16)
    few_shape = jax.ShapeDtypeStruct(own.shape, bf16)
    return pl.pallas_call(
        project_kernel,
        grid=(PROJECT_STEPS,),
        in_specs=[
            pl.BlockSpec((rows, D), lambda t: (t, 0)),
            small,
            pl.BlockSpec((1, D), lambda t: (0, 0)),
            pl.BlockSpec((3, D, D), lambda t: (0, 0, 0)),
        ]
        + [ANY] * (len(earlier) + len(later)),
        out_specs=[small, wide, wide, wide, small],
        out_shape=[few_shape, many_shape, many_shape, many_shape, few_shape],
        input_output_aliases={4 + j: j for j in range(len(earlier))},
        compiler_params=pltpu.CompilerParams(vmem_limit_bytes=VMEM_GRANT),
        cost_estimate=cost(7),
        name="project",
    )(window, own, gain, weights, *earlier, *later)


GRAD_STEPS = 8


def attn_grads_kernel(place, n_ref, dk_ref, dv_ref, own_ref, dq_ref, dh_ref, o_ref, even_ref, odd_ref, *scratch):
    acc_ref, main_ref, rest_ref, sems = scratch
    step = pl.program_id(0)

    @pl.when(step == 0)
    def _():
        acc_ref[...] = jnp.zeros_like(acc_ref)

    turned = n_ref[...].T
    acc_ref[1] += dot(turned, dk_ref[...])
    acc_ref[2] += dot(turned, dv_ref[...])

    @pl.when(step % 2 == 1)
    def _():
        acc_ref[0] += dot(own_ref[...].T, dq_ref[...])
        acc_ref[3] += dot(dh_ref[...].T, o_ref[...])

    @pl.when(step == GRAD_STEPS - 1)
    def _():
        lower = lower_lanes((D, TILE))
        for c in range(4):
            main_ref[c] = acc_ref[c, :, : 4 * TILE].astype(bf16)
        for group in range(4):
            entry = entry_of(place, group)
            for k in range(PARTS):
                part = (odd_ref if k % 2 else even_ref).at[k // 2, entry, pl.ds(0, 4)]
                source = main_ref.at[:, part_rows(place, k), pl.ds(group * TILE, TILE)]
                pltpu.make_async_copy(source, part, sems.at[0]).start()
        for two in range(2):
            lanes = slice((4 + two) * TILE, (5 + two) * TILE)
            for both in range(2):
                one = acc_ref[2 * both, :, lanes]
                other = pltpu.roll(acc_ref[2 * both + 1, :, lanes], DH, 1)
                rest_ref[2 * two, both] = jnp.where(lower, one, other).astype(bf16)
                rest_ref[2 * two + 1, both] = jnp.where(lower, other, one).astype(bf16)
        for group in range(4):
            entry = entry_of(place, group)
            for k in range(PARTS):
                part = (odd_ref if k % 2 else even_ref).at[k // 2, entry, pl.ds(4, 2)]
                source = rest_ref.at[group, :, part_rows(place, k)]
                pltpu.make_async_copy(source, part, sems.at[0]).start()
        wait_for(even_ref, sems.at[0])
        wait_for(odd_ref, sems.at[0])


def attn_grads(place, normed_window, dk, dv, normed_own, dq, dh, o):
    rows, few = dk.shape[0] // GRAD_STEPS, dq.shape[0] // (GRAD_STEPS // 2)
    wide = pl.BlockSpec((rows, D), lambda t: (t, 0))
    small = pl.BlockSpec((few, D), lambda t: (t // 2, 0))
    parts = jax.ShapeDtypeStruct((PARTS // 2, 4, 6, PART, TILE), bf16)
    return pl.pallas_call(
        attn_grads_kernel,
        grid=(GRAD_STEPS,),
        in_specs=[SMEM, wide, wide, wide, small, small, small, small],
        out_specs=[ANY] * 2,
        out_shape=[parts] * 2,
        scratch_shapes=[
            pltpu.VMEM((4, D, D), f32),
            pltpu.VMEM((4, D, 4 * TILE), bf16),
            pltpu.VMEM((4, 2, D, TILE), bf16),
            pltpu.SemaphoreType.DMA((1,)),
        ],
        compiler_params=pltpu.CompilerParams(vmem_limit_bytes=VMEM_GRANT),
        cost_estimate=cost(10),
        name="attn_grads",
    )(place, normed_window, dk, dv, normed_own, dq, dh, o)


ROWS = 256


def gelu_and_slope(gate):
    root = 0.7978845608028654
    cube = 0.044715
    square = gate * gate
    bend = jnp.tanh(root * gate * (1.0 + cube * square))
    half = 0.5 * (1.0 + bend)
    slope = half + 0.5 * gate * (1.0 - bend * bend) * (root * (1.0 + 3.0 * cube * square))
    return gate * half, slope


def ffn_kernel(first, last, entries, place, *refs):
    refs = list(refs)
    take = lambda count: [refs.pop(0) for _ in range(count)]
    y_ref, dy_ref, gain_ref = take(3)
    acc_in, dn_in = (None, None) if first else take(2)
    (all_w,) = take(1)
    outs = take(3 if last else 2)
    even_ref, odd_ref = take(2)
    w_ref, g_ref, n_ref, nt_ref, dyt_ref, acc_ref, dn_ref, hid_ref, dgate_ref, dup_ref, w_sems, g_sems = refs
    tokens = y_ref.shape[0]
    width = w_ref.shape[2] // 3
    gate_cols, up_cols, down_cols = (slice(c * width, (c + 1) * width) for c in range(3))

    for at, entry in enumerate(entries):
        group = lax.rem(entry + place[1], 4)
        for k in range(PARTS):
            pltpu.make_async_copy(all_w.at[k, group], w_ref.at[at, pl.ds(k * PART, PART)], w_sems.at[at]).start()
    y = y_ref[...]
    rho = lax.rsqrt(jnp.mean(y * y, axis=-1, keepdims=True) + epsilon)
    normed = (y * rho * gain_ref[...]).astype(bf16)
    n_ref[...] = normed
    nt_ref[...] = normed.T
    dyt_ref[...] = dy_ref[...].T
    acc_ref[...] = y if first else acc_in[...]
    dn_ref[...] = jnp.zeros_like(dn_ref) if first else dn_in[...]

    def one_group(at, _):
        wait_for(w_ref.at[at], w_sems.at[at])
        w = w_ref.at[at]

        def tile(t, _):
            rows = pl.ds(pl.multiple_of(t * ROWS, ROWS), ROWS)
            normed = n_ref[rows, :]
            gate = dot(normed, w[:, gate_cols])
            up = dot(normed, w[:, up_cols])
            grad_hid = dot(dy_ref[rows, :], w[:, down_cols])
            act, slope = gelu_and_slope(gate)
            hid = (act * up).astype(bf16)
            dgate = (grad_hid * up * slope).astype(bf16)
            dup = (grad_hid * act).astype(bf16)
            hid_ref[rows, :] = hid
            dgate_ref[rows, :] = dgate
            dup_ref[rows, :] = dup
            acc_ref[rows, :] += dot(hid, w[:, down_cols], NT)
            dn_ref[rows, :] += dot(dgate, w[:, gate_cols], NT) + dot(dup, w[:, up_cols], NT)
            return 0

        lax.fori_loop(0, tokens // ROWS, tile, 0)

        def grads(t, _):
            rows = pl.ds(pl.multiple_of(t * ROWS, ROWS), ROWS)
            g_ref[at, rows, gate_cols] = dot(nt_ref[rows, :], dgate_ref[...]).astype(bf16)
            g_ref[at, rows, up_cols] = dot(nt_ref[rows, :], dup_ref[...]).astype(bf16)
            g_ref[at, rows, down_cols] = dot(dyt_ref[rows, :], hid_ref[...]).astype(bf16)
            return 0

        lax.fori_loop(0, D // ROWS, grads, 0)
        for k in range(PARTS):
            part = (odd_ref if k % 2 else even_ref).at[k // 2, at]
            pltpu.make_async_copy(g_ref.at[at, part_rows(place, k)], part, g_sems.at[0]).start()
        return 0

    lax.fori_loop(0, len(entries), one_group, 0)

    if last:
        out_ref, dy1_ref, dh1_ref = outs
        out_ref[...] = acc_ref[...].astype(bf16)
        y = y_ref[...]
        rho = lax.rsqrt(jnp.mean(y * y, axis=-1, keepdims=True) + epsilon)
        scaled_y = y * rho
        u = dn_ref[...] * gain_ref[...]
        inner = jnp.mean(u * scaled_y, axis=-1, keepdims=True)
        dy1 = dy_ref[...].astype(f32) + rho * (u - scaled_y * inner)
        dy1_ref[...] = dy1
        dh1_ref[...] = dy1.astype(bf16)
    else:
        outs[0][...] = acc_ref[...]
        outs[1][...] = dn_ref[...]
    wait_for(even_ref, g_sems.at[0])
    wait_for(odd_ref, g_sems.at[0])


def ffn(place, y, dy, gain, weights, entries, sums=None, last=False):
    tokens = y.shape[0]
    columns = weights.shape[3]
    wide = lambda dtype: jax.ShapeDtypeStruct((tokens, D), dtype)
    outs = [wide(bf16), wide(f32), wide(bf16)] if last else [wide(f32), wide(f32)]
    operands = [y, dy, gain] + list(sums or [])
    parts = jax.ShapeDtypeStruct((PARTS // 2, len(entries), PART, columns), bf16)
    results = pl.pallas_call(
        functools.partial(ffn_kernel, sums is None, last, entries),
        in_specs=[SMEM] + [VMEM] * len(operands) + [ANY],
        out_specs=[VMEM] * len(outs) + [ANY] * 2,
        out_shape=outs + [parts] * 2,
        scratch_shapes=[
            pltpu.VMEM((len(entries), D, columns), bf16),
            pltpu.VMEM((len(entries), D, columns), bf16),
            pltpu.VMEM((tokens, D), bf16),
            pltpu.VMEM((D, tokens), bf16),
            pltpu.VMEM((D, tokens), bf16),
            pltpu.VMEM((tokens, D), f32),
            pltpu.VMEM((tokens, D), f32),
            pltpu.VMEM((tokens, columns // 3), bf16),
            pltpu.VMEM((tokens, columns // 3), bf16),
            pltpu.VMEM((tokens, columns // 3), bf16),
            pltpu.SemaphoreType.DMA((len(entries),)),
            pltpu.SemaphoreType.DMA((1,)),
        ],
        compiler_params=pltpu.CompilerParams(vmem_limit_bytes=VMEM_GRANT),
        cost_estimate=cost(20),
        name="ffn",
    )(place, *operands, weights)
    return results[: len(outs)], results[len(outs) :]


def grams_of(blocks):
    return jnp.einsum("our,ouw->orw", blocks, blocks, precision=HIGHEST)


def orthogonal(blocks, gram):
    total = jnp.trace(gram, axis1=1, axis2=2)[:, None, None]
    mul = functools.partial(jnp.einsum, "oij,ojk->oik", precision=HIGH)
    first = gram / total
    start = blocks * lax.rsqrt(total)
    eye = jnp.eye(gram.shape[1], dtype=f32)[None]
    step = linear_coefficient * eye + coef_second * first + coef_third * mul(first, first)
    second = mul(mul(first, step), step)
    once = mul(start, step)
    turn = mul(once, second)
    return linear_coefficient * once + coef_second * turn + coef_third * mul(turn, second)


def adam_update(param, grad, first, second):
    first_new = beta_one * first + (1.0 - beta_one) * grad
    second_new = beta_two * second + (1.0 - beta_two) * grad * grad
    corrected_first = first_new / (1.0 - beta_one**STEP)
    corrected_second = second_new / (1.0 - beta_two**STEP)
    return (
        first_new,
        second_new,
        param - adam_rate * corrected_first / (jnp.sqrt(corrected_second) + adam_epsilon),
    )


def direct():
    return lax.axis_size("dp") == PARTS and lax.axis_size("mp") == 4


def swap(x, bit):
    return lax.ppermute(x, "dp", [(j, j ^ bit) for j in range(lax.axis_size("dp"))])


def from_above(x, k):
    return lax.ppermute(x, "mp", [((j + k) % 4, j) for j in range(4)])


def to_above(x, k):
    return lax.ppermute(x, "mp", [(j, (j + k) % 4) for j in range(4)])


def behind(x, *others):
    return lax.optimization_barrier((x, others))[0]


def total(*terms):
    return sum(term.astype(f32) for term in terms)


def gather_all(shard):
    rows, columns = shard.shape
    whole = lax.all_gather(shard, ("dp", "mp"), axis=0, tiled=False)
    if rows == PART:
        return whole.reshape(PARTS, 4, PART, columns)
    whole = whole.reshape(-1, 4, rows, columns).transpose(1, 0, 2, 3).reshape(4, PARTS, PART, columns)
    return whole.transpose(1, 0, 2, 3)


def gather_pieces(shard):
    tiles, rows, _ = shard.shape
    if not direct():
        whole = lax.all_gather(shard, ("dp", "mp"), axis=0, tiled=False)
        whole = whole.reshape(PARTS, -1, 4, tiles, rows, TILE).transpose(0, 2, 3, 1, 4, 5)
        return list(whole.reshape(PARTS, 4, tiles, PART, TILE))
    own = jnp.stack([shard] + [from_above(shard, k) for k in (1, 2, 3)])
    return own


def spread_pieces(own, meanwhile):
    if not direct():
        return own
    along, across = behind((swap(own, 2), swap(own, 4)), meanwhile)
    far = jnp.concatenate([swap(along[:2], 4), swap(across[2:], 2)])
    even = [own, along, across, far]
    return [piece for here in even for piece in (here, swap(here, 1))]


def scatter_core(even, odd):
    return total(even, swap(odd, 1)).astype(bf16)


def scatter_plane(mine, meanwhile=()):
    others = behind((swap(mine[1], 2), swap(mine[2], 4), swap(mine[3], 6)), meanwhile)
    return total(mine[0], *others).astype(bf16)


def scatter_plain(even, odd, rows):
    whole = jnp.stack([even, odd], axis=1)
    whole = whole.reshape(PARTS, 4, -1, PART // rows, rows, whole.shape[-1])
    parts = whole.transpose(0, 3, 1, 2, 4, 5)
    parts = parts.reshape((-1,) + parts.shape[3:])
    return lax.psum_scatter(parts, ("dp", "mp"), scatter_dimension=0, tiled=False).astype(f32)


def gather_small(x, axis_name, axis):
    if not direct():
        return lax.all_gather(x, axis_name, axis=axis, tiled=True)
    here = lax.axis_index(axis_name)
    size = lax.axis_size(axis_name)
    bit = 1
    while bit < size:
        other = lax.ppermute(x, axis_name, [(j, j ^ bit) for j in range(size)])
        upper = (here & bit) != 0
        x = jnp.concatenate([jnp.where(upper, other, x), jnp.where(upper, x, other)], axis=axis)
        bit *= 2
    return x


def sum_line(x):
    if not direct():
        return lax.psum(x, "mp")
    return x + from_above(x, 1) + from_above(x, 2) + from_above(x, 3)


def sum_planes(x, meanwhile=()):
    if not direct():
        return lax.psum(x, "dp")
    odd = (lax.axis_index("dp") & 1) != 0
    low = lambda v: v.astype(bf16)
    mine = total(jnp.where(odd, x[2:], x[:2]), swap(low(jnp.where(odd, x[:2], x[2:])), 1))
    one, two = mine[0], mine[1]
    one, two = behind((total(one, swap(low(one), 2)), total(two, swap(low(two), 4))), meanwhile)
    one, two = total(one, swap(low(one), 4)), total(two, swap(low(two), 2))
    mine = low(jnp.stack([one, two]))
    other = swap(mine, 1)
    return jnp.concatenate([jnp.where(odd, other, mine), jnp.where(odd, mine, other)]).astype(f32)


def shards(
    tokens, lengths, cotangent, attn_in, attn_out, ffn_in, ffn_out, gains, table,
    attn_in_mom, attn_out_mom, ffn_in_mom, ffn_out_mom,
    gain_first, gain_second, table_first, table_second,
):
    micro, own_rows, _ = tokens.shape
    here = lax.axis_index("mp")
    n_mp = lax.axis_size("mp")
    width = attn_in.shape[2]
    heads_dev = table.shape[1]

    rows_dev = attn_in.shape[1]
    width_ffn = ffn_in.shape[2]
    index = jnp.stack([lax.axis_index("dp"), here]).astype(jnp.int32)
    place = index if direct() else jnp.zeros_like(index)
    odd_group = (here & 1) != 0

    ffn_low = jnp.concatenate([ffn_in[0], ffn_in[1], ffn_out.T], axis=1).astype(bf16)
    attn_low = [part.astype(bf16) for part in (attn_in[0], attn_in[1], attn_in[2], attn_out.T)]
    tails = [part[:, TILE:] for part in attn_low]
    beside = lambda one, two: jnp.where(
        odd_group, jnp.concatenate([two, one], axis=1), jnp.concatenate([one, two], axis=1)
    )
    attn_tiles = jnp.stack([part[:, :TILE] for part in attn_low] + [beside(*tails[:2]), beside(*tails[2:])])
    gain_low = gather_small(gains.astype(bf16), "dp", 1).astype(f32)
    table_all = gather_small(table, "mp", 1)[:, np.array(HEAD_ORDER)]
    onehot = skew_onehot()
    line = lax.dot_general(
        table_all, onehot, (((0,), (1,)), ((), ())), precision=HIGHEST, preferred_element_type=f32
    ).reshape(PAIRS, 2, SKEW)
    attn_own = behind(gather_pieces(attn_tiles), gain_low, line)
    halo, ffn_low = behind((tokens, ffn_low), attn_own)
    up, down = [(j, j + 1) for j in range(n_mp - 1)], [(j + 1, j) for j in range(n_mp - 1)]
    sides = []
    for mb in range(micro):
        part = behind(halo[mb], sides)
        sides.append((lax.ppermute(part, "mp", up), lax.ppermute(part, "mp", down)))
    ffn_all = gather_all(ffn_low)
    bias = make_bias(behind(line, attn_own))
    attn_pieces = spread_pieces(attn_own, (bias, sides[0]))
    weights = join(place, behind(attn_pieces, sides))
    w_q, w_k, w_v, w_o = weights

    first_row = own_rows * here
    first_doc = first_row // LEN
    inset = first_row - first_doc * LEN
    gap = jnp.zeros((2 * LEN - 2 * own_rows + QB, D), bf16)
    block_place = first_row // QB + jnp.arange(own_rows // QB, dtype=jnp.int32)
    slot = block_place // (LEN // QB) - first_doc
    lens_window = lax.dynamic_slice_in_dim(
        jnp.concatenate([lengths, jnp.ones((micro, 1), lengths.dtype)], axis=1), first_doc, 2, axis=1
    )
    meta = jnp.concatenate([slot, block_place % (LEN // QB), lens_window.reshape(-1)]).astype(jnp.int32)

    projected, attended = (), ()
    for mb in range(micro):
        above, below = behind(sides[mb], weights, attended)
        window = jnp.concatenate([above, tokens[mb], below, gap])
        window = lax.dynamic_slice_in_dim(window, own_rows - inset, 2 * LEN, axis=0)
        projected = project(window, tokens, gain_low[0:1], weights, mb, projected, attended)
        q, k, v, normed_window, normed_own = projected
        attended = (attend(meta, q, k, v, bias, mb, attended),)
    attended = attended[0].reshape(micro * own_rows, D)
    normed_window = normed_window.reshape(micro * 2 * LEN, D)
    normed_own = normed_own.reshape(micro * own_rows, D)
    rows = tokens.reshape(micro * own_rows, D).astype(f32)
    middle = rows + dot(attended, w_o, NT)

    dy = cotangent.reshape(micro * own_rows, D)
    ffn_args = (place, middle, dy, gain_low[1:2], ffn_all)
    sums, (even_one, odd_one) = ffn(*ffn_args, (0, 1))
    (output, grad_middle, grad_mid_low), (even_two, odd_two) = ffn(*ffn_args, (2, 3), sums, last=True)
    if direct():
        mine_one, mine_two = scatter_core(even_one, odd_one), scatter_core(even_two, odd_two)
    else:
        shard_ffn = scatter_plain(
            jnp.concatenate([even_one, even_two], axis=1), jnp.concatenate([odd_one, odd_two], axis=1), rows_dev
        )[0]
        mine_one = mine_two = ()

    grad_att = dot(grad_mid_low, w_o).astype(bf16).reshape(micro, own_rows, D)
    back_args = (meta, q, k, v, grad_att, bias)
    grads = attend_back(*back_args, (0, 2), (), [mine_one] if direct() else ())
    grads = attend_back(*back_args, (2, 2), grads, [mine_two] if direct() else ())
    line_one, line_two = (), ()
    if direct():
        line_one = scatter_plane(mine_one, grads)
        line_two = scatter_plane(behind(mine_two, line_one))
        sent_one = to_above(line_one[1], 1)
    grad_q, grad_k, grad_v, grad_bias = attend_back(*back_args, (4, 2), grads, [line_one] if direct() else ())
    grad_q = grad_q.reshape(micro * own_rows, D)
    grad_k = grad_k.reshape(micro * 2 * LEN, D)
    grad_v = grad_v.reshape(micro * 2 * LEN, D)
    even, odd = attn_grads(
        place, normed_window, grad_k, grad_v, normed_own, grad_q, grad_mid_low, attended
    )
    grad_q, grad_k, grad_v = behind((grad_q, grad_k, grad_v), even)
    grad_normed_own = dot(grad_q, w_q, NT)
    grad_normed_window = (dot(grad_k, w_k, NT) + dot(grad_v, w_v, NT)).reshape(micro, 2 * LEN, D)
    edge = ((0, 0), (own_rows, own_rows), (0, 0))
    sent = jnp.pad(grad_normed_window.astype(bf16), edge)
    back = lax.dynamic_slice_in_dim(sent, inset, own_rows, axis=1)
    forth = lax.dynamic_slice_in_dim(sent, inset + 2 * own_rows, own_rows, axis=1)
    own_part = lax.dynamic_slice_in_dim(grad_normed_window, inset, own_rows, axis=1)
    own_part = own_part.reshape(micro * own_rows, D) + grad_normed_own
    if direct():
        shard_ffn = total(line_one[0], sent_one, to_above(line_two[0], 2), to_above(line_two[1], 3))
        mine_attn = behind(scatter_core(even, odd), back, forth, shard_ffn)
        back, forth = behind((back, forth), mine_attn)
    else:
        mine_attn = even
    back, forth = lax.ppermute(back, "mp", down), lax.ppermute(forth, "mp", up)
    if direct():
        line_attn = scatter_plane(mine_attn, (back, forth))
        shard_attn = total(line_attn[0], *[to_above(line_attn[k], k) for k in (1, 2, 3)])
    else:
        line_attn = even
        shard_attn = scatter_plain(even, odd, rows_dev)
    grad_bias = behind(grad_bias, mine_attn)
    back, forth = behind((back, forth), shard_attn)
    grad_normed = own_part + (back.astype(f32) + forth.astype(f32)).reshape(micro * own_rows, D)
    rho = lax.rsqrt(jnp.mean(rows * rows, axis=-1, keepdims=True) + epsilon)
    u = grad_normed * gain_low[0]
    tokens_grad = grad_middle + rho * (u - rows * rho * rho * jnp.mean(u * rows, axis=-1, keepdims=True))

    pick = lambda tile, second: jnp.where(odd_group ^ second, tile[:, DH:], tile[:, :DH])
    parts_attn = jnp.stack(
        [
            jnp.concatenate([shard_attn[c], pick(shard_attn[4 + c // 2], c % 2 == 1)], axis=1)
            for c in range(4)
        ]
    )
    parts_ffn = shard_ffn.reshape(rows_dev, 3, width_ffn).transpose(1, 0, 2)
    low = lambda v: v.astype(bf16).astype(f32)
    gain_terms = jnp.stack(
        [jnp.sum(low(attn_in) * parts_attn[:3], axis=(0, 2)), jnp.sum(low(ffn_in) * parts_ffn[:2], axis=(0, 2))]
    )
    mom_in = momentum_decay * attn_in_mom + parts_attn[:3]
    mom_out_t = momentum_decay * attn_out_mom.T + parts_attn[3]
    mom_fin = momentum_decay * ffn_in_mom + parts_ffn[:2]
    mom_fout_t = momentum_decay * ffn_out_mom.T + parts_ffn[2]
    blocks_attn = jnp.concatenate([mom_in, mom_out_t[None]])
    blocks_ffn = jnp.concatenate([mom_fin, mom_fout_t[None]])
    gram_ffn = behind(grams_of(blocks_ffn), line_attn)
    gram_ffn = sum_planes(gram_ffn.reshape(4, -1, width_ffn)).reshape(gram_ffn.shape)
    table_sum = lax.dot_general(
        onehot,
        diagonals(grad_bias).reshape(H, SKEW),
        (((0,), (1,)), ((), ())),
        precision=HIGHEST,
        preferred_element_type=f32,
    )
    gram_attn = grams_of(blocks_attn)
    gram_ffn = behind(gram_ffn, gram_attn)
    orth_ffn = orthogonal(blocks_ffn, gram_ffn)
    extra = jnp.pad(table_sum.reshape(4, 1, -1), ((0, 0), (0, 15), (0, width - BUCKETS * H // 4)))
    summed = sum_planes(jnp.concatenate([gram_attn, extra], axis=1), orth_ffn)
    table_sum = summed[:, width, : BUCKETS * H // 4]
    orth_attn = orthogonal(blocks_attn, summed[:, :width])
    small = jnp.concatenate([gain_terms.reshape(-1), table_sum.reshape(-1)])
    small = sum_line(jnp.pad(small, (0, -small.size % 1024)).reshape(-1, 128)).reshape(-1)
    gain_grad = small[: gain_terms.size].reshape(gain_terms.shape) / low(gains)
    table_sum = small[gain_terms.size : gain_terms.size + BUCKETS * H].reshape(BUCKETS, H)
    table_sum = table_sum[:, np.argsort(np.array(HEAD_ORDER))]
    table_grad = lax.dynamic_slice_in_dim(table_sum, here * heads_dev, heads_dev, axis=1)
    attn_in_next = attn_in * (1.0 - rate_attn_in * decay_rate) - rate_attn_in * orth_attn[:3]
    attn_out_next = attn_out * (1.0 - rate_attn_out * decay_rate) - rate_attn_out * orth_attn[3].T
    ffn_in_next = ffn_in * (1.0 - rate_ffn_in * decay_rate) - rate_ffn_in * orth_ffn[:2]
    ffn_out_next = ffn_out * (1.0 - rate_ffn_out * decay_rate) - rate_ffn_out * orth_ffn[2].T
    gain_first_next, gain_second_next, gains_next = adam_update(gains, gain_grad, gain_first, gain_second)
    table_first_next, table_second_next, table_next = adam_update(table, table_grad, table_first, table_second)
    return (
        output.reshape(tokens.shape),
        tokens_grad.reshape(tokens.shape),
        attn_in_next,
        attn_out_next,
        ffn_in_next,
        ffn_out_next,
        mom_in,
        mom_out_t.T,
        mom_fin,
        mom_fout_t.T,
        gain_first_next,
        gain_second_next,
        gains_next,
        table_first_next,
        table_second_next,
        table_next,
    )


def solution(mesh):
    token = P(None, ("dp", "mp"), None)
    columns = P(None, "dp", "mp")
    flipped = P("mp", "dp")
    gain = P(None, "dp")
    head = P(None, "mp")
    return jax.shard_map(
        shards,
        mesh=mesh,
        in_specs=(
            token, P(None, "dp"), token, columns, flipped, columns, flipped, gain, head,
            columns, flipped, columns, flipped, gain, gain, head, head,
        ),
        out_specs=(
            token, token, columns, flipped, columns, flipped, columns, flipped, columns, flipped,
            gain, gain, gain, head, head, head,
        ),
        check_vma=False,
    )
```

time: 670 us -> 440 us (0.66)
  waiting for transfers between devices: 256 us -> 79 us
  blocking collectives: 95.4 us -> 0 us
  starting transfers between devices: 13.8 us -> 74.6 us
  local copies, waits for them, and re-layouts: 83.1 us -> 24.6 us
  Pallas kernels: 99.9 us -> 156 us
  matrix products: 57 us -> 44.8 us
    reduce_scatter x2 -> x0, waiting for transfers between devices: 211 us -> none  [scatter_blocks(): lax.psum_scatter(parts, ('dp', 'mp'), scatter_dimension=0, tiled=True)]
    ppermute x4 -> x55, waiting for transfers between devices: 0.01 us -> 79 us  [the longest x32 36.9 us: swap(): lax.ppermute(x, 'dp', [(j, j ^ bit) for j in range(lax.axis_size('dp'))])]
    ppermute x4 -> x55, starting transfers between devices: 13.4 us -> 74.5 us  [the longest x32 26.7 us: swap(): lax.ppermute(x, 'dp', [(j, j ^ bit) for j in range(lax.axis_size('dp'))])]
    pallas_call x3 -> x13, Pallas kernels: 99.9 us -> 156 us  [the longest x2 43.5 us: ffn(): pl.pallas_call(functools.partial(ffn_kernel, sums is None, last, entries)...]
    all_gather x2 -> x0, blocking collectives: 54.2 us -> none  [the longest x1 45.4 us: shards(): table_all = lax.all_gather(table, 'mp', axis=1, tiled=True)]
    psum x1 -> x0, blocking collectives: 41.2 us -> none  [shards(): gain_sum, table_sum = lax.psum((gain_sum, table_sum), ('dp', 'mp'))]
    another operation x3 -> x1, local copies, waits for them, and re-layouts: 26.2 us -> 0.08 us  [shards(): small = jnp.concatenate([gain_terms.reshape(-1), table_sum.reshape(-1)])]
    psum x1 -> x0, waiting for transfers between devices: 23.3 us -> none  [shards(): gram_attn = lax.psum(grams_of(blocks_attn), 'dp')]
  transfers between devices with their start and end apart: 9 -> 56, of which waited for: 4 -> 21; matrix products, arithmetic and copies ran while one was open for 16% -> 18% of each run, Pallas kernels for 4% -> 28%
where the time goes in v2:
time: 440 us; the launch traced here: 434 us
  Pallas kernels  156 us (35%)
  waiting for transfers between devices  79 us (18%)
  starting transfers between devices  74.6 us (17%)
  matrix products  44.8 us (10%)
  other arithmetic  39.1 us (9%)
  local copies, waits for them, and re-layouts  24.6 us (6%)
  between operations  16 us (4%)
    pallas_call x2, Pallas kernels, ffn(): pl.pallas_call(functools.partial(ffn_kernel, sums is None, last, entries)...  43.5 us
    pallas_call x3, Pallas kernels, attend_back(): pl.pallas_call(functools.partial(attend_back_kernel, kept), grid_spec=plt...  37.9 us
    ppermute x32, waiting for transfers between devices, swap(): lax.ppermute(x, 'dp', [(j, j ^ bit) for j in range(lax.axis_size('dp'))])  36.9 us
    ppermute x32, starting transfers between devices, swap(): lax.ppermute(x, 'dp', [(j, j ^ bit) for j in range(lax.axis_size('dp'))])  26.7 us
    pallas_call x2, Pallas kernels, attend(): pl.pallas_call(functools.partial(attend_kernel, mb), grid_spec=pltpu.Pref...  23.1 us
    ppermute x4, waiting for transfers between devices, shards(): sides.append((lax.ppermute(part, 'mp', up), lax.ppermute(part, 'mp', down)))  22.6 us
    dot_general x5, matrix products, dot(): return lax.dot_general(a, b, dims, preferred_element_type=f32)  19.9 us
    ppermute x6, waiting for transfers between devices, to_above(): return lax.ppermute(x, 'mp', [(j, (j + k) % 4) for j in range(4)])  16.7 us
  transfers between devices with their start and end apart: 56, of which 21 were waited for; matrix products, arithmetic and copies ran while one was open for 18% of the time, Pallas kernels for 28%

profile of v2, /device:TPU:0, one launch (start us, length us, event | category | flops | bytes accessed | tf_op | source)
XLA Modules:
  0.0 434.1 jit_solution(11330433742819333763)
XLA Ops:
  9.7 5.1 %collective-permute-start = (bf16[6,96,128]{2,1,0:T(8,128)(2,1)S(1)}, bf16[6,96,128]{2,1,0:T(8,128)(2,1)S(1)}, u32[]{:S(2)}, u32[]{:S(2)}) collective-permute-start(bf16[6,96,128]{2,1,0:T(8,128)(2,1)S(1)} %fusion.76), channel_id=1, source_target_pairs={{1,0},{2,1},{3,2},{0,3},{5,4},{6,5},{7,6},{4,7},{9,8},{10,9},{11,1... | collective-permute-start | bytes 442376 | tf_op jit(solution)/shard_map/ppermute | solution.py:576
  32.2 5.2 %collective-permute-start.8 = (bf16[384,768]{1,0:T(8,128)(2,1)}, bf16[384,768]{1,0:T(8,128)(2,1)}, u32[]{:S(2)}, u32[]{:S(2)}) collective-permute-start(bf16[384,768]{1,0:T(8,128)(2,1)} %get-tuple-element.227), channel_id=1, source_target_pairs={{0,1},{1,2},{2,3},{4,5},{5,6},{6,7},{8,9},{9,10},{10,11},{12,13},{... | collective-permute-start | bytes 1769480 | tf_op jit(solution)/shard_map/ppermute | solution.py:706
  41.9 6.3 %make_bias.1.bias_ref = f32[6,2,1024,128]{3,2,1,0:T(8,128)} custom-call(f32[6,2,1024]{2,1,0:T(2,128)} %reshape.291.line_ref), custom_call_target="tpu_custom_call" | custom-call | flops 2400000000 | tf_op jit(solution)/shard_map/make_bias/pallas_call | solution.py:84
  48.2 5.6 %collective-permute-done.8 = bf16[384,768]{1,0:T(8,128)(2,1)} collective-permute-done((bf16[384,768]{1,0:T(8,128)(2,1)}, bf16[384,768]{1,0:T(8,128)(2,1)}, u32[]{:S(2)}, u32[]{:S(2)}) %collective-permute-start.8) | collective-permute-done | bytes 589856 | tf_op jit(solution)/shard_map/ppermute | solution.py:706
  53.8 4.9 %collective-permute-done.9 = bf16[384,768]{1,0:T(8,128)(2,1)} collective-permute-done((bf16[384,768]{1,0:T(8,128)(2,1)}, bf16[384,768]{1,0:T(8,128)(2,1)}, u32[]{:S(2)}, u32[]{:S(2)}) %collective-permute-start.9) | collective-permute-done | bytes 589856 | tf_op jit(solution)/shard_map/ppermute | solution.py:706
  63.1 6.6 %collective-permute-done.17 = bf16[2,6,96,128]{3,2,1,0:T(8,128)(2,1)S(1)} collective-permute-done((bf16[2,6,96,128]{3,2,1,0:T(8,128)(2,1)S(1)}, bf16[2,6,96,128]{3,2,1,0:T(8,128)(2,1)S(1)}, u32[]{:S(2)}, u32[]{:S(2)}) %collective-permute-start.17) | collective-permute-done | bytes 294944 | tf_op jit(solution)/shard_map/ppermute | solution.py:572
  77.3 9.1 %collective-permute-done.10 = bf16[384,768]{1,0:T(8,128)(2,1)S(1)} collective-permute-done((bf16[384,768]{1,0:T(8,128)(2,1)}, bf16[384,768]{1,0:T(8,128)(2,1)S(1)}, u32[]{:S(2)}, u32[]{:S(2)}) %collective-permute-start.10) | collective-permute-done | bytes 589856 | tf_op jit(solution)/shard_map/ppermute | solution.py:706
  90.2 5.5 %join.1.w_ref = bf16[4,768,768]{2,1,0:T(8,128)(2,1)} custom-call(s32[2]{0:T(128)} %pad_add_fusion.place, bf16[4,6,96,128]{3,2,1,0:T(8,128)(2,1)} %copy-done.14, bf16[4,6,96,128]{3,2,1,0:T(8,128)(2,1)} %copy-done.34, bf16[4,6,96,128]{3,2,1,0:T(8,128)(2,1)} %copy-done.22, bf16[4,6,96,128]{3,2,1,0:T(8,128)(2,1)} %copy-done.35, ...), custom_call_target="tpu_custom_call" | custom-call | flops 1500000000 | tf_op jit(solution)/shard_map/join/pallas_call | solution.py:281
  98.8 7.6 %project.2 = (bf16[2,384,768]{2,1,0:T(8,128)(2,1)}, bf16[2,1024,768]{2,1,0:T(8,128)(2,1)}, bf16[2,1024,768]{2,1,0:T(8,128)(2,1)}, bf16[2,1024,768]{2,1,0:T(8,128)(2,1)}, bf16[2,384,768]{2,1,0:T(8,128)(2,1)}) custom-call(bf16[1024,768]{1,0:T(8,128)(2,1)} %fusion.19.x_ref, bf16[2,384,768]{2,1,0:T(8,128)(2,1)} %own_ref.3, ...), custom_call_target="tpu_custom_call" | custom-call | flops 2100000000 | tf_op jit(solution)/shard_map/project/pallas_call | solution.py:320
  106.4 11.6 %attend.2.refs_5_.refs_0_ = bf16[2,384,768]{2,1,0:T(8,128)(2,1)} custom-call(s32[10]{0:T(128)} %pad_add_fusion.1.meta, bf16[2,384,768]{2,1,0:T(8,128)(2,1)} %get-tuple-element.109.q_ref.refs_0_, bf16[2,1024,768]{2,1,0:T(8,128)(2,1)} %get-tuple-element.110.k_ref.refs_1_, bf16[2,1024,768]{2,1,0:T(8,128)(2,1)} %get-tuple-element.111.v_ref.refs_2_, ...), custom_call_target="tpu_custom_call" | custom-call | flops 3300000000 | tf_op jit(solution)/shard_map/attend/pallas_call | solution.py:194
  120.2 7.3 %project.3 = (bf16[2,384,768]{2,1,0:T(8,128)(2,1)}, bf16[2,1024,768]{2,1,0:T(8,128)(2,1)}, bf16[2,1024,768]{2,1,0:T(8,128)(2,1)}, bf16[2,1024,768]{2,1,0:T(8,128)(2,1)}, bf16[2,384,768]{2,1,0:T(8,128)(2,1)}) custom-call(bf16[1024,768]{1,0:T(8,128)(2,1)} %fusion.16.x_ref, ...), custom_call_target="tpu_custom_call", output_to_operand_aliasing={{0}: (4, {}), {1}: (5, {}), {2}: (6, {}), {3}: (7, {}), {4}... | custom-call | flops 2100000000 | tf_op jit(solution)/shard_map/project/pallas_call | solution.py:320
  127.6 11.6 %attend.3 = bf16[2,384,768]{2,1,0:T(8,128)(2,1)} custom-call(s32[10]{0:T(128)} %pad_add_fusion.1.meta, bf16[2,384,768]{2,1,0:T(8,128)(2,1)} %get-tuple-element.116.q_ref, bf16[2,1024,768]{2,1,0:T(8,128)(2,1)} %get-tuple-element.117.k_ref, bf16[2,1024,768]{2,1,0:T(8,128)(2,1)} %get-tuple-element.118.v_ref, ...), custom_call_target="tpu_custom_call", output_to_operand_aliasing={{}: (5, {})} | custom-call | flops 3300000000 | tf_op jit(solution)/shard_map/attend/pallas_call | solution.py:194
  139.2 4.1 bitcast_add_fusion.2.refs_0_
  143.3 21.0 %ffn.2 = (f32[768,768]{1,0:T(8,128)}, f32[768,768]{1,0:T(8,128)}, bf16[4,2,96,1536]{3,2,1,0:T(8,128)(2,1)}, bf16[4,2,96,1536]{3,2,1,0:T(8,128)(2,1)}) custom-call(s32[2]{0:T(128)} %pad_add_fusion.place, f32[768,768]{1,0:T(8,128)} %bitcast_add_fusion.2.refs_0_, bf16[768,768]{1,0:T(8,128)(2,1)} %bitcast.322, f32[1,768]{1,0:T(1,128)} %get-tuple-element.266.refs_2_, ...), custom_call_target="tpu_custom_call" | custom-call | flops 6000000000 | tf_op jit(solution)/shard_map/ffn/pallas_call | solution.py:512
  166.0 22.5 %ffn.3 = (bf16[768,768]{1,0:T(8,128)(2,1)}, f32[768,768]{1,0:T(8,128)}, bf16[768,768]{1,0:T(8,128)(2,1)}, bf16[4,2,96,1536]{3,2,1,0:T(8,128)(2,1)}, bf16[4,2,96,1536]{3,2,1,0:T(8,128)(2,1)}) custom-call(s32[2]{0:T(128)} %pad_add_fusion.place, f32[768,768]{1,0:T(8,128)} %bitcast_add_fusion.2.refs_0_, bf16[768,768]{1,0:T(8,128)(2,1)} %bitcast.323, ...), custom_call_target="tpu_custom_call" | custom-call | flops 6000000000 | tf_op jit(solution)/shard_map/ffn/pallas_call | solution.py:512
  193.2 3.9 convolution_convert_fusion
  201.4 3.7 add_convert_fusion.1.refs_4_
  205.1 12.4 %attend_back.3 = (bf16[2,384,768]{2,1,0:T(8,128)(2,1)}, bf16[2,1024,768]{2,1,0:T(8,128)(2,1)}, bf16[2,1024,768]{2,1,0:T(8,128)(2,1)}, f32[6,2,1024,128]{3,2,1,0:T(8,128)}) custom-call(s32[10]{0:T(128)} %pad_add_fusion.1.meta, bf16[2,384,768]{2,1,0:T(8,128)(2,1)} %get-tuple-element.116.q_ref, bf16[2,1024,768]{2,1,0:T(8,128)(2,1)} %get-tuple-element.117.k_ref, ...), custom_call_target="tpu_custom_call" | custom-call | flops 4200000000 | tf_op jit(solution)/shard_map/attend_back/pallas_call | solution.py:218
  217.6 12.5 %attend_back.4 = (bf16[2,384,768]{2,1,0:T(8,128)(2,1)}, bf16[2,1024,768]{2,1,0:T(8,128)(2,1)}, bf16[2,1024,768]{2,1,0:T(8,128)(2,1)}, f32[6,2,1024,128]{3,2,1,0:T(8,128)}) custom-call(s32[10]{0:T(128)} %pad_add_fusion.1.meta, bf16[2,384,768]{2,1,0:T(8,128)(2,1)} %get-tuple-element.116.q_ref, ...), custom_call_target="tpu_custom_call", output_to_operand_aliasing={{0}: (6, {}), {1}: (7, {}), {2}: (8, {}), {3}: (9, {})} | custom-call | flops 4200000000 | tf_op jit(solution)/shard_map/attend_back/pallas_call | solution.py:218
  233.4 13.0 %attend_back.5 = (bf16[2,384,768]{2,1,0:T(8,128)(2,1)}, bf16[2,1024,768]{2,1,0:T(8,128)(2,1)}, bf16[2,1024,768]{2,1,0:T(8,128)(2,1)}, f32[6,2,1024,128]{3,2,1,0:T(8,128)}) custom-call(s32[10]{0:T(128)} %pad_add_fusion.1.meta, bf16[2,384,768]{2,1,0:T(8,128)(2,1)} %get-tuple-element.116.q_ref, ...), custom_call_target="tpu_custom_call", output_to_operand_aliasing={{0}: (6, {}), {1}: (7, {}), {2}: (8, {}), {3}: (9, {})} | custom-call | flops 4200000000 | tf_op jit(solution)/shard_map/attend_back/pallas_call | solution.py:218
  252.6 15.9 %attn_grads.1 = (bf16[4,4,6,96,128]{4,3,2,1,0:T(8,128)(2,1)}, bf16[4,4,6,96,128]{4,3,2,1,0:T(8,128)(2,1)}) custom-call(s32[2]{0:T(128)} %pad_add_fusion.place, bf16[2048,768]{1,0:T(8,128)(2,1)} %bitcast.302, bf16[2048,768]{1,0:T(8,128)(2,1)} %bitcast.292, bf16[2048,768]{1,0:T(8,128)(2,1)} %bitcast.294, bf16[768,768]{1,0:T(8,128)(2,1)} %bitcast.309, ...), custom_call_target="tpu_custom_call" | custom-call | flops 3000000000 | tf_op jit(solution)/shard_map/attn_grads/pallas_call | solution.py:392
  268.5 5.2 %fusion.32 = f32[2048,768]{1,0:T(8,128)S(1)} fusion(bf16[2048,768]{1,0:T(8,128)(2,1)} %bitcast.293, bf16[4,768,768]{2,1,0:T(8,128)(2,1)} %join.1.w_ref), kind=kOutput, calls=%fused_computation.66 | convolution fusion | flops 2415919104 | bytes 10616832 | tf_op jit(solution)/shard_map/dot_general | solution.py:56
  273.7 4.1 convolution_add_fusion
  287.4 9.5 %collective-permute-done.30 = bf16[96,1536]{1,0:T(8,128)(2,1)S(1)} collective-permute-done((bf16[96,1536]{1,0:T(8,128)(2,1)S(1)}, bf16[96,1536]{1,0:T(8,128)(2,1)S(1)}, u32[]{:S(2)}, u32[]{:S(2)}) %collective-permute-start.30) | collective-permute-done | bytes 294944 | tf_op jit(solution)/shard_map/ppermute | solution.py:580
  299.2 10.1 %collective-permute-start.33 = (bf16[2,384,768]{2,1,0:T(8,128)(2,1)}, bf16[2,384,768]{2,1,0:T(8,128)(2,1)}, u32[]{:S(2)}, u32[]{:S(2)}) collective-permute-start(bf16[2,384,768]{2,1,0:T(8,128)(2,1)} %get-tuple-element.156), channel_id=1, source_target_pairs={{0,1},{1,2},{2,3},{4,5},{5,6},{6,7},{8,9},{9,10},{10,11},{12,13},{... | collective-permute-start | bytes 3538952 | tf_op jit(solution)/shard_map/ppermute | solution.py:781
  316.2 4.4 %fusion.47 = f32[3,512,512]{2,1,0:T(8,128)} fusion(f32[1,96,512]{2,1,0:T(8,128)S(1)} %get-tuple-element.230, f32[2,96,512]{2,1,0:T(8,128)S(1)} %get-tuple-element.232), kind=kOutput, calls=%fused_computation.118 | convolution fusion | flops 906117120 | bytes 3735552 | tf_op jit(solution)/shard_map/our,ouw->orw/dot_general | solution.py:539
  320.6 8.9 %diagonals.1 = f32[6,2,1024]{2,1,0:T(2,128)} custom-call(f32[6,2,1024,128]{3,2,1,0:T(8,128)} %get-tuple-element.163.acc_ref), custom_call_target="tpu_custom_call" | custom-call | flops 300000000 | tf_op jit(solution)/shard_map/diagonals/pallas_call | solution.py:107
  333.7 6.0 %collective-permute-done.35 = bf16[4,6,96,128]{3,2,1,0:T(8,128)(2,1)} collective-permute-done((bf16[4,6,96,128]{3,2,1,0:T(8,128)(2,1)}, bf16[4,6,96,128]{3,2,1,0:T(8,128)(2,1)}, u32[]{:S(2)}, u32[]{:S(2)}) %collective-permute-start.35) | collective-permute-done | bytes 589856 | tf_op jit(solution)/shard_map/ppermute | solution.py:572
  350.2 3.7 collective-permute-done.38
  362.9 6.8 %collective-permute-done.44 = bf16[384,512]{1,0:T(8,128)(2,1)S(1)} collective-permute-done((bf16[384,512]{1,0:T(8,128)(2,1)S(1)}, bf16[384,512]{1,0:T(8,128)(2,1)S(1)}, u32[]{:S(2)}, u32[]{:S(2)}) %collective-permute-start.44) | collective-permute-done | bytes 393248 | tf_op jit(solution)/shard_map/ppermute | solution.py:572
  375.0 6.3 %collective-permute-done.46 = bf16[384,512]{1,0:T(8,128)(2,1)S(1)} collective-permute-done((bf16[384,512]{1,0:T(8,128)(2,1)S(1)}, bf16[384,512]{1,0:T(8,128)(2,1)S(1)}, u32[]{:S(2)}, u32[]{:S(2)}) %collective-permute-start.46) | collective-permute-done | bytes 393248 | tf_op jit(solution)/shard_map/ppermute | solution.py:572
  395.1 3.5 fusion.1
  (374 shorter events, 154.2 us)
Async XLA Ops:
  7.3 136.0 %all-gather.3.cloned.1.call-start = ((), (), s32[]{:S(2)}) async-start(), calls=%async_computation | async-start | bytes 9732096 | tf_op jit(solution)/shard_map/all_gather | solution.py:593
  9.7 21.1 %collective-permute-start = (bf16[6,96,128]{2,1,0:T(8,128)(2,1)S(1)}, bf16[6,96,128]{2,1,0:T(8,128)(2,1)S(1)}, u32[]{:S(2)}, u32[]{:S(2)}) collective-permute-start(bf16[6,96,128]{2,1,0:T(8,128)(2,1)S(1)} %fusion.76), channel_id=1, source_target_pairs={{1,0},{2,1},{3,2},{0,3},{5,4},{6,5},{7,6},{4,7},{9,8},{10,9},{11,1... | collective-permute-start | bytes 442376 | tf_op jit(solution)/shard_map/ppermute | solution.py:576
  14.8 16.0 %collective-permute-start.1 = (bf16[6,96,128]{2,1,0:T(8,128)(2,1)S(1)}, bf16[6,96,128]{2,1,0:T(8,128)(2,1)S(1)}, u32[]{:S(2)}, u32[]{:S(2)}) collective-permute-start(bf16[6,96,128]{2,1,0:T(8,128)(2,1)S(1)} %fusion.76), channel_id=1, source_target_pairs={{2,0},{3,1},{0,2},{1,3},{6,4},{7,5},{4,6},{5,7},{10,8},{11,9},{8,1... | collective-permute-start | bytes 442376 | tf_op jit(solution)/shard_map/ppermute | solution.py:576
  14.8 16.0 %collective-permute-start.2 = (bf16[6,96,128]{2,1,0:T(8,128)(2,1)S(1)}, bf16[6,96,128]{2,1,0:T(8,128)(2,1)S(1)}, u32[]{:S(2)}, u32[]{:S(2)}) collective-permute-start(bf16[6,96,128]{2,1,0:T(8,128)(2,1)S(1)} %fusion.76), channel_id=1, source_target_pairs={{3,0},{0,1},{1,2},{2,3},{7,4},{4,5},{5,6},{6,7},{11,8},{8,9},{9,10... | collective-permute-start | bytes 442376 | tf_op jit(solution)/shard_map/ppermute | solution.py:576
  32.2 21.6 %collective-permute-start.8 = (bf16[384,768]{1,0:T(8,128)(2,1)}, bf16[384,768]{1,0:T(8,128)(2,1)}, u32[]{:S(2)}, u32[]{:S(2)}) collective-permute-start(bf16[384,768]{1,0:T(8,128)(2,1)} %get-tuple-element.227), channel_id=1, source_target_pairs={{0,1},{1,2},{2,3},{4,5},{5,6},{6,7},{8,9},{9,10},{10,11},{12,13},{... | collective-permute-start | bytes 1769480 | tf_op jit(solution)/shard_map/ppermute | solution.py:706
  37.4 21.3 %collective-permute-start.9 = (bf16[384,768]{1,0:T(8,128)(2,1)}, bf16[384,768]{1,0:T(8,128)(2,1)}, u32[]{:S(2)}, u32[]{:S(2)}) collective-permute-start(bf16[384,768]{1,0:T(8,128)(2,1)} %get-tuple-element.227), channel_id=1, source_target_pairs={{1,0},{2,1},{3,2},{5,4},{6,5},{7,6},{9,8},{10,9},{11,10},{13,12},{... | collective-permute-start | bytes 1769480 | tf_op jit(solution)/shard_map/ppermute | solution.py:706
  38.7 20.0 %collective-permute-start.13 = (bf16[4,6,96,128]{3,2,1,0:T(8,128)(2,1)S(1)}, bf16[4,6,96,128]{3,2,1,0:T(8,128)(2,1)S(1)}, u32[]{:S(2)}, u32[]{:S(2)}) collective-permute-start(bf16[4,6,96,128]{3,2,1,0:T(8,128)(2,1)S(1)} %pad_maximum_fusion.2.refs_0_), channel_id=1, source_target_pairs={{0,8},{4,12},{8,0},{12,4},{16,24},{20,28},{24,16},{28,20},{1,9},{5... | collective-permute-start | bytes 1769480 | tf_op jit(solution)/shard_map/ppermute | solution.py:572
  40.2 18.5 %collective-permute-start.14 = (bf16[4,6,96,128]{3,2,1,0:T(8,128)(2,1)S(1)}, bf16[4,6,96,128]{3,2,1,0:T(8,128)(2,1)S(1)}, u32[]{:S(2)}, u32[]{:S(2)}) collective-permute-start(bf16[4,6,96,128]{3,2,1,0:T(8,128)(2,1)S(1)} %pad_maximum_fusion.2.refs_0_), channel_id=1, source_target_pairs={{0,16},{4,20},{8,24},{12,28},{16,0},{20,4},{24,8},{28,12},{1,17},{... | collective-permute-start | bytes 1769480 | tf_op jit(solution)/shard_map/ppermute | solution.py:572
  41.9 32.6 %collective-permute-start.12 = (bf16[4,6,96,128]{3,2,1,0:T(8,128)(2,1)S(1)}, bf16[4,6,96,128]{3,2,1,0:T(8,128)(2,1)S(1)}, u32[]{:S(2)}, u32[]{:S(2)}) collective-permute-start(bf16[4,6,96,128]{3,2,1,0:T(8,128)(2,1)S(1)} %pad_maximum_fusion.2.refs_0_), channel_id=1, source_target_pairs={{0,4},{4,0},{8,12},{12,8},{16,20},{20,16},{24,28},{28,24},{1,5},{5... | collective-permute-start | bytes 1769480 | tf_op jit(solution)/shard_map/ppermute | solution.py:572
  62.6 14.6 %collective-permute-start.15 = (bf16[4,6,96,128]{3,2,1,0:T(8,128)(2,1)S(1)}, bf16[4,6,96,128]{3,2,1,0:T(8,128)(2,1)S(1)}, u32[]{:S(2)}, u32[]{:S(2)}) collective-permute-start(bf16[4,6,96,128]{3,2,1,0:T(8,128)(2,1)S(1)} %collective-permute-done.13.refs_2_), channel_id=1, source_target_pairs={{0,4},{4,0},{8,12},{12,8},{16,20},{20,16},{24,28},{28,24},{1,5},{5... | collective-permute-start | bytes 1769480 | tf_op jit(solution)/shard_map/ppermute | solution.py:572
  62.6 14.6 %collective-permute-start.16 = (bf16[4,6,96,128]{3,2,1,0:T(8,128)(2,1)S(1)}, bf16[4,6,96,128]{3,2,1,0:T(8,128)(2,1)S(1)}, u32[]{:S(2)}, u32[]{:S(2)}) collective-permute-start(bf16[4,6,96,128]{3,2,1,0:T(8,128)(2,1)S(1)} %collective-permute-done.14.refs_4_), channel_id=1, source_target_pairs={{0,4},{4,0},{8,12},{12,8},{16,20},{20,16},{24,28},{28,24},{1,5},{5... | collective-permute-start | bytes 1769480 | tf_op jit(solution)/shard_map/ppermute | solution.py:572
  69.8 16.6 %collective-permute-start.10 = (bf16[384,768]{1,0:T(8,128)(2,1)}, bf16[384,768]{1,0:T(8,128)(2,1)S(1)}, u32[]{:S(2)}, u32[]{:S(2)}) collective-permute-start(bf16[384,768]{1,0:T(8,128)(2,1)} %get-tuple-element.95), channel_id=1, source_target_pairs={{0,1},{1,2},{2,3},{4,5},{5,6},{6,7},{8,9},{9,10},{10,11},{12,13},{... | collective-permute-start | bytes 1769480 | tf_op jit(solution)/shard_map/ppermute | solution.py:706
  73.1 16.2 %collective-permute-start.11 = (bf16[384,768]{1,0:T(8,128)(2,1)}, bf16[384,768]{1,0:T(8,128)(2,1)S(1)}, u32[]{:S(2)}, u32[]{:S(2)}) collective-permute-start(bf16[384,768]{1,0:T(8,128)(2,1)} %get-tuple-element.95), channel_id=1, source_target_pairs={{1,0},{2,1},{3,2},{5,4},{6,5},{7,6},{9,8},{10,9},{11,10},{13,12},{... | collective-permute-start | bytes 1769480 | tf_op jit(solution)/shard_map/ppermute | solution.py:706
  74.5 15.7 %collective-permute-start.19 = (bf16[4,6,96,128]{3,2,1,0:T(8,128)(2,1)S(1)}, bf16[4,6,96,128]{3,2,1,0:T(8,128)(2,1)}, u32[]{:S(2)}, u32[]{:S(2)}) collective-permute-start(bf16[4,6,96,128]{3,2,1,0:T(8,128)(2,1)S(1)} %constant_dynamic-update-slice_fusion.refs_6_), channel_id=1, source_target_pairs={{0,4},{4,0},{8,12},{12,8},{16,20},{20,16},{24,28},{28,24},{1,5},{5... | collective-permute-start | bytes 1769480 | tf_op jit(solution)/shard_map/ppermute | solution.py:572
  164.3 32.8 %collective-permute-start.20 = (bf16[4,2,96,1536]{3,2,1,0:T(8,128)(2,1)}, bf16[4,2,96,1536]{3,2,1,0:T(8,128)(2,1)S(1)}, u32[]{:S(2)}, u32[]{:S(2)}) collective-permute-start(bf16[4,2,96,1536]{3,2,1,0:T(8,128)(2,1)} %get-tuple-element.126), channel_id=1, source_target_pairs={{0,4},{4,0},{8,12},{12,8},{16,20},{20,16},{24,28},{28,24},{1,5},{5... | collective-permute-start | bytes 7077896 | tf_op jit(solution)/shard_map/ppermute | solution.py:572
  188.5 12.9 %collective-permute-start.21 = (bf16[4,2,96,1536]{3,2,1,0:T(8,128)(2,1)}, bf16[4,2,96,1536]{3,2,1,0:T(8,128)(2,1)}, u32[]{:S(2)}, u32[]{:S(2)}) collective-permute-start(bf16[4,2,96,1536]{3,2,1,0:T(8,128)(2,1)} %get-tuple-element.132), channel_id=1, source_target_pairs={{0,4},{4,0},{8,12},{12,8},{16,20},{20,16},{24,28},{28,24},{1,5},{5... | collective-permute-start | bytes 7077896 | tf_op jit(solution)/shard_map/ppermute | solution.py:572
  197.8 32.2 %collective-permute-start.22 = (bf16[2,96,1536]{2,1,0:T(8,128)(2,1)S(1)}, bf16[2,96,1536]{2,1,0:T(8,128)(2,1)S(1)}, u32[]{:S(2)}, u32[]{:S(2)}) collective-permute-start(bf16[2,96,1536]{2,1,0:T(8,128)(2,1)S(1)} %get-tuple-element.218), channel_id=1, source_target_pairs={{0,8},{4,12},{8,0},{12,4},{16,24},{20,28},{24,16},{28,20},{1,9},{5... | collective-permute-start | bytes 1769480 | tf_op jit(solution)/shard_map/ppermute | solution.py:572
  199.1 31.0 %collective-permute-start.23 = (bf16[2,96,1536]{2,1,0:T(8,128)(2,1)S(1)}, bf16[2,96,1536]{2,1,0:T(8,128)(2,1)}, u32[]{:S(2)}, u32[]{:S(2)}) collective-permute-start(bf16[2,96,1536]{2,1,0:T(8,128)(2,1)S(1)} %get-tuple-element.217), channel_id=1, source_target_pairs={{0,16},{4,20},{8,24},{12,28},{16,0},{20,4},{24,8},{28,12},{1,17},{... | collective-permute-start | bytes 1769480 | tf_op jit(solution)/shard_map/ppermute | solution.py:572
  200.0 30.1 %collective-permute-start.24 = (bf16[2,96,1536]{2,1,0:T(8,128)(2,1)S(1)}, bf16[2,96,1536]{2,1,0:T(8,128)(2,1)}, u32[]{:S(2)}, u32[]{:S(2)}) collective-permute-start(bf16[2,96,1536]{2,1,0:T(8,128)(2,1)S(1)} %get-tuple-element.216), channel_id=1, source_target_pairs={{0,24},{4,28},{8,16},{12,20},{16,8},{20,12},{24,0},{28,4},{1,25},{... | collective-permute-start | bytes 1769480 | tf_op jit(solution)/shard_map/ppermute | solution.py:572
  247.6 30.5 %collective-permute-start.27 = (bf16[2,96,1536]{2,1,0:T(8,128)(2,1)}, bf16[2,96,1536]{2,1,0:T(8,128)(2,1)}, u32[]{:S(2)}, u32[]{:S(2)}) collective-permute-start(bf16[2,96,1536]{2,1,0:T(8,128)(2,1)} %get-tuple-element.215), channel_id=1, source_target_pairs={{0,8},{4,12},{8,0},{12,4},{16,24},{20,28},{24,16},{28,20},{1,9},{5... | collective-permute-start | bytes 1769480 | tf_op jit(solution)/shard_map/ppermute | solution.py:572
  248.8 29.3 %collective-permute-start.28 = (bf16[2,96,1536]{2,1,0:T(8,128)(2,1)}, bf16[2,96,1536]{2,1,0:T(8,128)(2,1)}, u32[]{:S(2)}, u32[]{:S(2)}) collective-permute-start(bf16[2,96,1536]{2,1,0:T(8,128)(2,1)} %get-tuple-element.214), channel_id=1, source_target_pairs={{0,16},{4,20},{8,24},{12,28},{16,0},{20,4},{24,8},{28,12},{1,17},{... | collective-permute-start | bytes 1769480 | tf_op jit(solution)/shard_map/ppermute | solution.py:572
  249.7 28.4 %collective-permute-start.29 = (bf16[2,96,1536]{2,1,0:T(8,128)(2,1)}, bf16[2,96,1536]{2,1,0:T(8,128)(2,1)}, u32[]{:S(2)}, u32[]{:S(2)}) collective-permute-start(bf16[2,96,1536]{2,1,0:T(8,128)(2,1)} %get-tuple-element.213), channel_id=1, source_target_pairs={{0,24},{4,28},{8,16},{12,20},{16,8},{20,12},{24,0},{28,4},{1,25},{... | collective-permute-start | bytes 1769480 | tf_op jit(solution)/shard_map/ppermute | solution.py:572
  251.1 36.3 %collective-permute-start.26 = (bf16[96,1536]{1,0:T(8,128)(2,1)}, bf16[96,1536]{1,0:T(8,128)(2,1)S(1)}, u32[]{:S(2)}, u32[]{:S(2)}) collective-permute-start(bf16[96,1536]{1,0:T(8,128)(2,1)} %slice_bitcast_fusion.27), channel_id=1, source_target_pairs={{0,1},{1,2},{2,3},{3,0},{4,5},{5,6},{6,7},{7,4},{8,9},{9,10},{10,1... | collective-permute-start | bytes 884744 | tf_op jit(solution)/shard_map/ppermute | solution.py:580
  268.4 28.7 %collective-permute-start.25 = (bf16[4,4,6,96,128]{4,3,2,1,0:T(8,128)(2,1)}, bf16[4,4,6,96,128]{4,3,2,1,0:T(8,128)(2,1)S(1)}, u32[]{:S(2)}, u32[]{:S(2)}) collective-permute-start(bf16[4,4,6,96,128]{4,3,2,1,0:T(8,128)(2,1)} %get-tuple-element.149), channel_id=1, source_target_pairs={{0,4},{4,0},{8,12},{12,8},{16,20},{20,16},{24,28},{28,24},{1,5},{5... | collective-permute-start | bytes 7077896 | tf_op jit(solution)/shard_map/ppermute | solution.py:572
  279.9 17.0 %collective-permute-start.30 = (bf16[96,1536]{1,0:T(8,128)(2,1)S(1)}, bf16[96,1536]{1,0:T(8,128)(2,1)S(1)}, u32[]{:S(2)}, u32[]{:S(2)}) collective-permute-start(bf16[96,1536]{1,0:T(8,128)(2,1)S(1)} %get-tuple-element.236), channel_id=1, source_target_pairs={{0,2},{1,3},{2,0},{3,1},{4,6},{5,7},{6,4},{7,5},{8,10},{9,11},{10,... | collective-permute-start | bytes 884744 | tf_op jit(solution)/shard_map/ppermute | solution.py:580
  281.4 15.5 %collective-permute-start.31 = (bf16[96,1536]{1,0:T(8,128)(2,1)S(1)}, bf16[96,1536]{1,0:T(8,128)(2,1)S(1)}, u32[]{:S(2)}, u32[]{:S(2)}) collective-permute-start(bf16[96,1536]{1,0:T(8,128)(2,1)S(1)} %get-tuple-element.237), channel_id=1, source_target_pairs={{0,3},{1,0},{2,1},{3,2},{4,7},{5,4},{6,5},{7,6},{8,11},{9,8},{10,9... | collective-permute-start | bytes 884744 | tf_op jit(solution)/shard_map/ppermute | solution.py:580
  297.9 41.9 %collective-permute-start.32 = (bf16[2,384,768]{2,1,0:T(8,128)(2,1)}, bf16[2,384,768]{2,1,0:T(8,128)(2,1)}, u32[]{:S(2)}, u32[]{:S(2)}) collective-permute-start(bf16[2,384,768]{2,1,0:T(8,128)(2,1)} %get-tuple-element.155), channel_id=1, source_target_pairs={{1,0},{2,1},{3,2},{5,4},{6,5},{7,6},{9,8},{10,9},{11,10},{13,12},{... | collective-permute-start | bytes 3538952 | tf_op jit(solution)/shard_map/ppermute | solution.py:781
  299.2 40.6 %collective-permute-start.33 = (bf16[2,384,768]{2,1,0:T(8,128)(2,1)}, bf16[2,384,768]{2,1,0:T(8,128)(2,1)}, u32[]{:S(2)}, u32[]{:S(2)}) collective-permute-start(bf16[2,384,768]{2,1,0:T(8,128)(2,1)} %get-tuple-element.156), channel_id=1, source_target_pairs={{0,1},{1,2},{2,3},{4,5},{5,6},{6,7},{8,9},{9,10},{10,11},{12,13},{... | collective-permute-start | bytes 3538952 | tf_op jit(solution)/shard_map/ppermute | solution.py:781
  311.3 22.5 %collective-permute-start.34 = (bf16[4,6,96,128]{3,2,1,0:T(8,128)(2,1)}, bf16[4,6,96,128]{3,2,1,0:T(8,128)(2,1)}, u32[]{:S(2)}, u32[]{:S(2)}) collective-permute-start(bf16[4,6,96,128]{3,2,1,0:T(8,128)(2,1)} %get-tuple-element.212), channel_id=1, source_target_pairs={{0,8},{4,12},{8,0},{12,4},{16,24},{20,28},{24,16},{28,20},{1,9},{5... | collective-permute-start | bytes 1769480 | tf_op jit(solution)/shard_map/ppermute | solution.py:572
  312.4 27.3 %collective-permute-start.35 = (bf16[4,6,96,128]{3,2,1,0:T(8,128)(2,1)}, bf16[4,6,96,128]{3,2,1,0:T(8,128)(2,1)}, u32[]{:S(2)}, u32[]{:S(2)}) collective-permute-start(bf16[4,6,96,128]{3,2,1,0:T(8,128)(2,1)} %get-tuple-element.211), channel_id=1, source_target_pairs={{0,16},{4,20},{8,24},{12,28},{16,0},{20,4},{24,8},{28,12},{1,17},{... | collective-permute-start | bytes 1769480 | tf_op jit(solution)/shard_map/ppermute | solution.py:572
  313.4 26.3 %collective-permute-start.36 = (bf16[4,6,96,128]{3,2,1,0:T(8,128)(2,1)}, bf16[4,6,96,128]{3,2,1,0:T(8,128)(2,1)}, u32[]{:S(2)}, u32[]{:S(2)}) collective-permute-start(bf16[4,6,96,128]{3,2,1,0:T(8,128)(2,1)} %get-tuple-element.210), channel_id=1, source_target_pairs={{0,24},{4,28},{8,16},{12,20},{16,8},{20,12},{24,0},{28,4},{1,25},{... | collective-permute-start | bytes 1769480 | tf_op jit(solution)/shard_map/ppermute | solution.py:572
  355.7 26.8 %collective-permute-start.40 = (bf16[2,208,192]{1,2,0:T(8,128)(2,1)S(1)}, bf16[2,208,192]{1,2,0:T(8,128)(2,1)S(1)}, u32[]{:S(2)}, u32[]{:S(2)}) collective-permute-start(bf16[2,208,192]{1,2,0:T(8,128)(2,1)S(1)} %select_convert_fusion.1), channel_id=1, source_target_pairs={{0,4},{4,0},{8,12},{12,8},{16,20},{20,16},{24,28},{28,24},{1,5},{5... | collective-permute-start | bytes 479240 | tf_op jit(solution)/shard_map/ppermute | solution.py:572
  (85 other events, 747.1 us)
Sparse Core Ops, SparseCore 0:
  31.1 90.6 all-gather.2

commit v3 on v2

--- a/solution.py
+++ b/solution.py
@@ -127,33 +127,45 @@
     )
 
 
-def exp_scores(meta, block, mb, keys, queries_two, bias_ref):
+def block_scores(meta, block, mb, keys, queries_two, bias_ref):
     start = pl.multiple_of((LEN - QB) - QB * meta[3 + block], QB)
     length = meta[6 + 2 * mb + meta[block]]
     bias = jnp.concatenate([bias_ref[0, 0, pl.ds(start, LEN), :], bias_ref[0, 1, pl.ds(start, LEN), :]], axis=1)
     scores = dot(keys, queries_two, NT) + bias
     row = lax.broadcasted_iota(jnp.int32, scores.shape, 0)
-    scores = jnp.where(row < length, scores, negative_fill)
-    top = jnp.max(scores, axis=0, keepdims=True)
-    weights = jnp.exp(scores - top)
-    return weights, jnp.sum(weights, axis=0, keepdims=True)
-
-
-def attend_kernel(mb, meta, q_ref, k_ref, v_ref, bias_ref, *refs):
-    o_ref = refs[-1]
-    for block in range(3):
-        rows = pl.ds(pl.multiple_of(meta[block] * LEN, LEN), LEN)
-        keys, values = k_ref[0, rows, :], v_ref[0, rows, :]
+    return jnp.where(row < length, scores, negative_fill)
+
+
+def block_rows(meta, block):
+    return pl.ds(pl.multiple_of(meta[block] * LEN, LEN), LEN)
+
+
+def one_of_two(pair):
+    top = lax.broadcasted_iota(jnp.int32, (QB, QB), 0) < DH
+    return jnp.where(top, pair[:, :QB], pair[:, QB:]).T
+
+
+def attend_kernel(meta, q_ref, k_ref, v_ref, bias_ref, o_ref, lse_ref):
+    mb = pl.program_id(1)
+    blocks = range(q_ref.shape[1] // QB)
+    scores, values = [], []
+    for block in blocks:
+        rows = block_rows(meta, block)
+        values.append(v_ref[0, rows, :].T)
         queries_two = both_heads(q_ref[0, block * QB : (block + 1) * QB, :])
-        weights, total = exp_scores(meta, block, mb, keys, queries_two, bias_ref)
-        out_two = dot(values.T, weights.astype(bf16)) / total
-        top = lax.broadcasted_iota(jnp.int32, (QB, QB), 0) < DH
-        out = jnp.where(top, out_two[:, :QB], out_two[:, QB:])
-        o_ref[0, block * QB : (block + 1) * QB, :] = out.T.astype(bf16)
-
-
-def attend_back_kernel(kept, meta, q_ref, k_ref, v_ref, do_ref, bias_ref, *refs):
-    dq_ref, dk_ref, dv_ref, acc_ref, dk_acc, dv_acc = refs[kept:]
+        scores.append(block_scores(meta, block, mb, k_ref[0, rows, :], queries_two, bias_ref))
+    for block in blocks:
+        top = jnp.max(scores[block], axis=0, keepdims=True)
+        weights = jnp.exp(scores[block] - top)
+        total = jnp.sum(weights, axis=0, keepdims=True)
+        lse_ref[0, 0, block : block + 1, :] = top + jnp.log(total)
+        out = one_of_two(dot(values[block], weights.astype(bf16)) / total)
+        o_ref[0, block * QB : (block + 1) * QB, :] = out.astype(bf16)
+
+
+def attend_back_kernel(
+    meta, q_ref, k_ref, v_ref, do_ref, o_ref, lse_ref, bias_ref, dq_ref, dk_ref, dv_ref, acc_ref, dk_acc, dv_acc
+):
     mb = pl.program_id(1)
 
     @pl.when(mb == 0)
@@ -162,65 +174,77 @@
 
     dk_acc[...] = jnp.zeros_like(dk_acc)
     dv_acc[...] = jnp.zeros_like(dv_acc)
-    for block in range(3):
-        rows = pl.ds(pl.multiple_of(meta[block] * LEN, LEN), LEN)
+    parts = []
+    for block in range(q_ref.shape[1] // QB):
+        rows = block_rows(meta, block)
         own = slice(block * QB, (block + 1) * QB)
-        keys, values = k_ref[0, rows, :], v_ref[0, rows, :]
-        queries_two = both_heads(q_ref[0, own, :])
-        grad_two = both_heads(do_ref[0, own, :])
-        weights, total = exp_scores(meta, block, mb, keys, queries_two, bias_ref)
-        soft = weights * (1.0 / total)
-        grad_soft = dot(values, grad_two, NT)
-        inner = jnp.sum(grad_soft * soft, axis=0, keepdims=True)
+        keys = k_ref[0, rows, :]
+        grad = do_ref[0, own, :]
+        queries_two, grad_two = both_heads(q_ref[0, own, :]), both_heads(grad)
+        scores = block_scores(meta, block, mb, keys, queries_two, bias_ref)
+        grad_soft = dot(v_ref[0, rows, :], grad_two, NT)
+        inner = (grad.astype(f32) * o_ref[0, own, :].astype(f32)).T
+        inner = jnp.concatenate(
+            [jnp.sum(inner[:DH], axis=0, keepdims=True), jnp.sum(inner[DH:], axis=0, keepdims=True)], axis=1
+        )
+        parts.append((rows, own, keys, queries_two, grad_two, scores, grad_soft, inner))
+    lows = []
+    for block, (_, _, _, _, _, scores, grad_soft, inner) in enumerate(parts):
+        soft = jnp.exp(scores - lse_ref[0, 0, block : block + 1, :])
         grad_scores = soft * (grad_soft - inner)
         start = pl.multiple_of((LEN - QB) - QB * meta[3 + block], QB)
         acc_ref[0, 0, pl.ds(start, LEN), :] += grad_scores[:, :QB]
         acc_ref[0, 1, pl.ds(start, LEN), :] += grad_scores[:, QB:]
-        grad_low = grad_scores.astype(bf16)
-        dk_acc[rows, :] += dot(grad_low, queries_two)
-        dv_acc[rows, :] += dot(soft.astype(bf16), grad_two)
-        dq_two = dot(keys.T, grad_low)
-        top = lax.broadcasted_iota(jnp.int32, (QB, QB), 0) < DH
-        dq_ref[0, own, :] = jnp.where(top, dq_two[:, :QB], dq_two[:, QB:]).T.astype(bf16)
+        lows.append((soft.astype(bf16), grad_scores.astype(bf16)))
+    for (rows, own, keys, queries_two, grad_two, _, _, _), (soft, grad_low) in zip(parts, lows):
+        both = dot(jnp.concatenate([grad_low, soft], axis=0), jnp.concatenate([queries_two, grad_two], axis=1))
+        dk_acc[rows, :] += both[:LEN, :QB]
+        dv_acc[rows, :] += both[LEN:, QB:]
+        dq_ref[0, own, :] = one_of_two(dot(keys.T, grad_low)).astype(bf16)
     dk_ref[0] = dk_acc[...].astype(bf16)
     dv_ref[0] = dv_acc[...].astype(bf16)
 
 
-def attend(meta, q, k, v, bias, mb, earlier=()):
-    rows, window = q.shape[1], k.shape[1]
-    own = pl.BlockSpec((1, rows, QB), lambda p, _: (mb, 0, p))
-    wide = pl.BlockSpec((1, window, QB), lambda p, _: (mb, 0, p))
-    lines = pl.BlockSpec((1, 2, SKEW, QB), lambda p, _: (p, 0, 0, 0))
+def attention_specs(rows, window):
+    own = pl.BlockSpec((1, rows, QB), lambda p, m, _: (m, 0, p))
+    wide = pl.BlockSpec((1, window, QB), lambda p, m, _: (m, 0, p))
+    lines = pl.BlockSpec((1, 2, SKEW, QB), lambda p, m, _: (p, 0, 0, 0))
+    stats = pl.BlockSpec((1, 1, 8, 2 * QB), lambda p, m, _: (m, p, 0, 0))
+    return own, wide, lines, stats
+
+
+def attend(meta, q, k, v, bias):
+    micro, rows, _ = q.shape
+    own, wide, lines, stats = attention_specs(rows, k.shape[1])
     return pl.pallas_call(
-        functools.partial(attend_kernel, mb),
+        attend_kernel,
         grid_spec=pltpu.PrefetchScalarGridSpec(
             num_scalar_prefetch=1,
-            grid=(PAIRS,),
-            in_specs=[own, wide, wide, lines] + [ANY] * len(earlier),
-            out_specs=own,
+            grid=(PAIRS, micro),
+            in_specs=[own, wide, wide, lines],
+            out_specs=[own, stats],
         ),
-        out_shape=jax.ShapeDtypeStruct(q.shape, bf16),
-        input_output_aliases={5 + j: j for j in range(len(earlier))},
+        out_shape=[
+            jax.ShapeDtypeStruct(q.shape, bf16),
+            jax.ShapeDtypeStruct((micro, PAIRS, 8, 2 * QB), f32),
+        ],
         compiler_params=pltpu.CompilerParams(vmem_limit_bytes=VMEM_GRANT),
-        cost_estimate=cost(11),
+        cost_estimate=cost(17),
         name="attend",
-    )(meta, q, k, v, bias, *earlier)
-
-
-def attend_back(meta, q, k, v, grad, bias, pairs, earlier=(), after=()):
+    )(meta, q, k, v, bias)
+
+
+def attend_back(meta, q, k, v, grad, out, stats, bias, after=()):
     micro, rows, _ = q.shape
     window = k.shape[1]
-    first, count = pairs
-    own = pl.BlockSpec((1, rows, QB), lambda p, m, _: (m, 0, p + first))
-    wide = pl.BlockSpec((1, window, QB), lambda p, m, _: (m, 0, p + first))
-    lines = pl.BlockSpec((1, 2, SKEW, QB), lambda p, m, _: (p + first, 0, 0, 0))
-    kept = len(earlier) + len(after)
+    own, wide, lines, lse = attention_specs(rows, window)
+    kernel = lambda *refs: attend_back_kernel(*refs[:8], *refs[8 + len(after) :])
     return pl.pallas_call(
-        functools.partial(attend_back_kernel, kept),
+        kernel,
         grid_spec=pltpu.PrefetchScalarGridSpec(
             num_scalar_prefetch=1,
-            grid=(count, micro),
-            in_specs=[own, wide, wide, own, lines] + [ANY] * kept,
+            grid=(PAIRS, micro),
+            in_specs=[own, wide, wide, own, own, lse, lines] + [ANY] * len(after),
             out_specs=[own, wide, wide, lines],
             scratch_shapes=[pltpu.VMEM((window, QB), f32), pltpu.VMEM((window, QB), f32)],
         ),
@@ -230,11 +254,10 @@
             jax.ShapeDtypeStruct(k.shape, bf16),
             jax.ShapeDtypeStruct(bias.shape, f32),
         ],
-        input_output_aliases={6 + j: j for j in range(len(earlier))},
         compiler_params=pltpu.CompilerParams(vmem_limit_bytes=VMEM_GRANT),
-        cost_estimate=cost(7 * count),
+        cost_estimate=cost(24),
         name="attend_back",
-    )(meta, q, k, v, grad, bias, *earlier, *after)
+    )(meta, q, k, v, grad, out, stats, bias, *after)
 
 
 PARTS = 8
@@ -290,15 +313,42 @@
     )(place, *pieces, *later)
 
 
-def project_kernel(x_ref, own_ref, gain_ref, w_ref, *refs):
-    q_ref, k_ref, v_ref, n_ref, n_own_ref = refs[-5:]
+PROJECT_STEPS = 2
+
+
+def project_kernel(place, above, own_all, below, own_ref, gain_ref, w_ref, *refs):
+    q_ref, k_ref, v_ref, n_ref, n_own_ref, x_ref, sems = refs
+    mb, step = pl.program_id(0), pl.program_id(1)
+    own_rows = own_all.shape[1]
+
+    @pl.when((mb == 0) & (step == 0))
+    def _():
+        for m in range(own_all.shape[0]):
+            for block in range(2 * LEN // QB):
+                row = block * QB - place[2]
+                for source, first, here in (
+                    (above, row + own_rows, row < 0),
+                    (own_all, row, (row >= 0) & (row < own_rows)),
+                    (below, jnp.minimum(row - own_rows, own_rows - QB), row >= own_rows),
+                ):
+
+                    @pl.when(here)
+                    def _():
+                        rows = pl.ds(pl.multiple_of(first, QB), QB)
+                        into = x_ref.at[m, pl.ds(block * QB, QB)]
+                        pltpu.make_async_copy(source.at[m, rows], into, sems.at[m]).start()
+
+    @pl.when(step == 0)
+    def _():
+        wait_for(x_ref.at[mb], sems.at[mb])
 
     def norm(rows):
         rows = rows.astype(f32)
         rho = lax.rsqrt(jnp.mean(rows * rows, axis=-1, keepdims=True) + epsilon)
         return (rows * rho * gain_ref[...]).astype(bf16)
 
-    normed = norm(x_ref[...])
+    size = k_ref.shape[1]
+    normed = norm(x_ref[mb, pl.ds(pl.multiple_of(step * size, size), size), :])
     n_ref[0] = normed
     k_ref[0] = dot(normed, w_ref[1]).astype(bf16)
     v_ref[0] = dot(normed, w_ref[2]).astype(bf16)
@@ -307,36 +357,35 @@
     q_ref[0] = dot(normed, w_ref[0]).astype(bf16)
 
 
-PROJECT_STEPS = 4
-
-
-def project(window, own, gain, weights, mb, earlier=(), later=()):
+def project(place, sides, own, gain, weights):
     micro, own_rows, _ = own.shape
-    rows, few = window.shape[0] // PROJECT_STEPS, own_rows // PROJECT_STEPS
-    wide = pl.BlockSpec((1, rows, D), lambda t: (mb, t, 0))
-    small = pl.BlockSpec((1, few, D), lambda t: (mb, t, 0))
-    many_shape = jax.ShapeDtypeStruct((micro, window.shape[0], D), bf16)
+    rows, few = 2 * LEN // PROJECT_STEPS, own_rows // PROJECT_STEPS
+    wide = pl.BlockSpec((1, rows, D), lambda m, t: (m, t, 0))
+    small = pl.BlockSpec((1, few, D), lambda m, t: (m, t, 0))
+    many_shape = jax.ShapeDtypeStruct((micro, 2 * LEN, D), bf16)
     few_shape = jax.ShapeDtypeStruct(own.shape, bf16)
     return pl.pallas_call(
         project_kernel,
-        grid=(PROJECT_STEPS,),
+        grid=(micro, PROJECT_STEPS),
         in_specs=[
-            pl.BlockSpec((rows, D), lambda t: (t, 0)),
+            SMEM,
+            ANY,
+            ANY,
+            ANY,
             small,
-            pl.BlockSpec((1, D), lambda t: (0, 0)),
-            pl.BlockSpec((3, D, D), lambda t: (0, 0, 0)),
-        ]
-        + [ANY] * (len(earlier) + len(later)),
+            pl.BlockSpec((1, D), lambda m, t: (0, 0)),
+            pl.BlockSpec((3, D, D), lambda m, t: (0, 0, 0)),
+        ],
         out_specs=[small, wide, wide, wide, small],
         out_shape=[few_shape, many_shape, many_shape, many_shape, few_shape],
-        input_output_aliases={4 + j: j for j in range(len(earlier))},
+        scratch_shapes=[pltpu.VMEM((micro, 2 * LEN, D), bf16), pltpu.SemaphoreType.DMA((micro,))],
         compiler_params=pltpu.CompilerParams(vmem_limit_bytes=VMEM_GRANT),
-        cost_estimate=cost(7),
+        cost_estimate=cost(12),
         name="project",
-    )(window, own, gain, weights, *earlier, *later)
-
-
-GRAD_STEPS = 8
+    )(place, sides[0], own, sides[1], own, gain, weights)
+
+
+GRAD_STEPS = 4
 
 
 def attn_grads_kernel(place, n_ref, dk_ref, dv_ref, own_ref, dq_ref, dh_ref, o_ref, even_ref, odd_ref, *scratch):
@@ -407,9 +456,6 @@
     )(place, normed_window, dk, dv, normed_own, dq, dh, o)
 
 
-ROWS = 256
-
-
 def gelu_and_slope(gate):
     root = 0.7978845608028654
     cube = 0.044715
@@ -420,119 +466,123 @@
     return gate * half, slope
 
 
-def ffn_kernel(first, last, entries, place, *refs):
-    refs = list(refs)
-    take = lambda count: [refs.pop(0) for _ in range(count)]
-    y_ref, dy_ref, gain_ref = take(3)
-    acc_in, dn_in = (None, None) if first else take(2)
-    (all_w,) = take(1)
-    outs = take(3 if last else 2)
-    even_ref, odd_ref = take(2)
-    w_ref, g_ref, n_ref, nt_ref, dyt_ref, acc_ref, dn_ref, hid_ref, dgate_ref, dup_ref, w_sems, g_sems = refs
-    tokens = y_ref.shape[0]
+def ffn_kernel(place, o_ref, x_ref, dy_ref, wo_ref, gain_ref, all_w, *refs):
+    out_ref, dy1_ref, dh1_ref = refs[:3]
+    parts = (refs[3:5], refs[5:7])
+    (w_ref, g_ref, y_ref, n_ref, nt_ref, dyt_ref, acc_ref, dn_ref, hid_ref, dgate_ref, dup_ref,
+     out_held, dy1_held, dh1_held, w_sems, g_sems, out_sems) = refs[7:]
     width = w_ref.shape[2] // 3
     gate_cols, up_cols, down_cols = (slice(c * width, (c + 1) * width) for c in range(3))
 
-    for at, entry in enumerate(entries):
+    def load(entry):
         group = lax.rem(entry + place[1], 4)
         for k in range(PARTS):
-            pltpu.make_async_copy(all_w.at[k, group], w_ref.at[at, pl.ds(k * PART, PART)], w_sems.at[at]).start()
-    y = y_ref[...]
+            rows = pl.ds(k * PART, PART)
+            pltpu.make_async_copy(all_w.at[k, group], w_ref.at[entry, rows], w_sems.at[entry]).start()
+
+    load(0)
+    y = x_ref[...].astype(f32) + dot(o_ref[...], wo_ref[...], NT)
+    y_ref[...] = y
     rho = lax.rsqrt(jnp.mean(y * y, axis=-1, keepdims=True) + epsilon)
     normed = (y * rho * gain_ref[...]).astype(bf16)
     n_ref[...] = normed
     nt_ref[...] = normed.T
     dyt_ref[...] = dy_ref[...].T
-    acc_ref[...] = y if first else acc_in[...]
-    dn_ref[...] = jnp.zeros_like(dn_ref) if first else dn_in[...]
-
-    def one_group(at, _):
-        wait_for(w_ref.at[at], w_sems.at[at])
-        w = w_ref.at[at]
-
-        def tile(t, _):
-            rows = pl.ds(pl.multiple_of(t * ROWS, ROWS), ROWS)
-            normed = n_ref[rows, :]
-            gate = dot(normed, w[:, gate_cols])
-            up = dot(normed, w[:, up_cols])
-            grad_hid = dot(dy_ref[rows, :], w[:, down_cols])
-            act, slope = gelu_and_slope(gate)
-            hid = (act * up).astype(bf16)
-            dgate = (grad_hid * up * slope).astype(bf16)
-            dup = (grad_hid * act).astype(bf16)
-            hid_ref[rows, :] = hid
-            dgate_ref[rows, :] = dgate
-            dup_ref[rows, :] = dup
-            acc_ref[rows, :] += dot(hid, w[:, down_cols], NT)
-            dn_ref[rows, :] += dot(dgate, w[:, gate_cols], NT) + dot(dup, w[:, up_cols], NT)
-            return 0
-
-        lax.fori_loop(0, tokens // ROWS, tile, 0)
-
-        def grads(t, _):
-            rows = pl.ds(pl.multiple_of(t * ROWS, ROWS), ROWS)
-            g_ref[at, rows, gate_cols] = dot(nt_ref[rows, :], dgate_ref[...]).astype(bf16)
-            g_ref[at, rows, up_cols] = dot(nt_ref[rows, :], dup_ref[...]).astype(bf16)
-            g_ref[at, rows, down_cols] = dot(dyt_ref[rows, :], hid_ref[...]).astype(bf16)
-            return 0
-
-        lax.fori_loop(0, D // ROWS, grads, 0)
+    acc_ref[...] = y
+    dn_ref[...] = jnp.zeros_like(dn_ref)
+    for entry in range(1, 4):
+        load(entry)
+
+    def through(entry):
+        wait_for(w_ref.at[entry], w_sems.at[entry])
+        w = w_ref.at[entry]
+        normed = n_ref[...]
+        gate = dot(normed, w[:, gate_cols])
+        up = dot(normed, w[:, up_cols])
+        grad_hid = dot(dy_ref[...], w[:, down_cols])
+        act, slope = gelu_and_slope(gate)
+        hid = (act * up).astype(bf16)
+        dgate = (grad_hid * up * slope).astype(bf16)
+        dup = (grad_hid * act).astype(bf16)
+        hid_ref[...] = hid
+        dgate_ref[...] = dgate
+        dup_ref[...] = dup
+        acc_ref[...] += dot(hid, w[:, down_cols], NT)
+        dn_ref[...] += dot(dgate, w[:, gate_cols], NT) + dot(dup, w[:, up_cols], NT)
+
+    def grads(entry, slot, pair):
+        g_ref[slot, :, gate_cols] = dot(nt_ref[...], dgate_ref[...]).astype(bf16)
+        g_ref[slot, :, up_cols] = dot(nt_ref[...], dup_ref[...]).astype(bf16)
+        g_ref[slot, :, down_cols] = dot(dyt_ref[...], hid_ref[...]).astype(bf16)
         for k in range(PARTS):
-            part = (odd_ref if k % 2 else even_ref).at[k // 2, at]
-            pltpu.make_async_copy(g_ref.at[at, part_rows(place, k)], part, g_sems.at[0]).start()
+            part = parts[pair][k % 2].at[k // 2, slot]
+            pltpu.make_async_copy(g_ref.at[slot, part_rows(place, k)], part, g_sems.at[slot]).start()
+
+    def one_group(entry, _):
+        through(entry)
+        grads(entry, entry, 0)
         return 0
 
-    lax.fori_loop(0, len(entries), one_group, 0)
-
-    if last:
-        out_ref, dy1_ref, dh1_ref = outs
-        out_ref[...] = acc_ref[...].astype(bf16)
-        y = y_ref[...]
-        rho = lax.rsqrt(jnp.mean(y * y, axis=-1, keepdims=True) + epsilon)
-        scaled_y = y * rho
-        u = dn_ref[...] * gain_ref[...]
-        inner = jnp.mean(u * scaled_y, axis=-1, keepdims=True)
-        dy1 = dy_ref[...].astype(f32) + rho * (u - scaled_y * inner)
-        dy1_ref[...] = dy1
-        dh1_ref[...] = dy1.astype(bf16)
-    else:
-        outs[0][...] = acc_ref[...]
-        outs[1][...] = dn_ref[...]
-    wait_for(even_ref, g_sems.at[0])
-    wait_for(odd_ref, g_sems.at[0])
-
-
-def ffn(place, y, dy, gain, weights, entries, sums=None, last=False):
-    tokens = y.shape[0]
+    lax.fori_loop(0, 2, one_group, 0)
+    through(2)
+    wait_for(g_ref.at[0], g_sems.at[0])
+    grads(2, 0, 1)
+    through(3)
+    outs = [(out_held, out_ref), (dy1_held, dy1_ref), (dh1_held, dh1_ref)]
+    out_held[...] = acc_ref[...].astype(bf16)
+    scaled_y = y_ref[...]
+    rho = lax.rsqrt(jnp.mean(scaled_y * scaled_y, axis=-1, keepdims=True) + epsilon)
+    scaled_y = scaled_y * rho
+    u = dn_ref[...] * gain_ref[...]
+    inner = jnp.mean(u * scaled_y, axis=-1, keepdims=True)
+    dy1 = dy_ref[...].astype(f32) + rho * (u - scaled_y * inner)
+    dy1_held[...] = dy1
+    dh1_held[...] = dy1.astype(bf16)
+    copies = [pltpu.make_async_copy(held, ref, out_sems.at[j]) for j, (held, ref) in enumerate(outs)]
+    for copy in copies:
+        copy.start()
+    wait_for(g_ref.at[1], g_sems.at[1])
+    grads(3, 1, 1)
+    for copy in copies:
+        copy.wait()
+    for slot in range(2):
+        wait_for(g_ref.at[slot], g_sems.at[slot])
+
+
+def ffn(place, attended, x, dy, w_o, gain, weights):
+    tokens = x.shape[0]
     columns = weights.shape[3]
     wide = lambda dtype: jax.ShapeDtypeStruct((tokens, D), dtype)
-    outs = [wide(bf16), wide(f32), wide(bf16)] if last else [wide(f32), wide(f32)]
-    operands = [y, dy, gain] + list(sums or [])
-    parts = jax.ShapeDtypeStruct((PARTS // 2, len(entries), PART, columns), bf16)
-    results = pl.pallas_call(
-        functools.partial(ffn_kernel, sums is None, last, entries),
-        in_specs=[SMEM] + [VMEM] * len(operands) + [ANY],
-        out_specs=[VMEM] * len(outs) + [ANY] * 2,
-        out_shape=outs + [parts] * 2,
+    parts = jax.ShapeDtypeStruct((PARTS // 2, 2, PART, columns), bf16)
+    scratch = lambda rows, width, dtype: pltpu.VMEM((rows, width), dtype)
+    return pl.pallas_call(
+        ffn_kernel,
+        in_specs=[SMEM] + [VMEM] * 5 + [ANY],
+        out_specs=[ANY] * 7,
+        out_shape=[wide(bf16), wide(f32), wide(bf16)] + [parts] * 4,
         scratch_shapes=[
-            pltpu.VMEM((len(entries), D, columns), bf16),
-            pltpu.VMEM((len(entries), D, columns), bf16),
-            pltpu.VMEM((tokens, D), bf16),
-            pltpu.VMEM((D, tokens), bf16),
-            pltpu.VMEM((D, tokens), bf16),
-            pltpu.VMEM((tokens, D), f32),
-            pltpu.VMEM((tokens, D), f32),
-            pltpu.VMEM((tokens, columns // 3), bf16),
-            pltpu.VMEM((tokens, columns // 3), bf16),
-            pltpu.VMEM((tokens, columns // 3), bf16),
-            pltpu.SemaphoreType.DMA((len(entries),)),
-            pltpu.SemaphoreType.DMA((1,)),
+            pltpu.VMEM((4, D, columns), bf16),
+            pltpu.VMEM((2, D, columns), bf16),
+            scratch(tokens, D, f32),
+            scratch(tokens, D, bf16),
+            scratch(D, tokens, bf16),
+            scratch(D, tokens, bf16),
+            scratch(tokens, D, f32),
+            scratch(tokens, D, f32),
+            scratch(tokens, columns // 3, bf16),
+            scratch(tokens, columns // 3, bf16),
+            scratch(tokens, columns // 3, bf16),
+            scratch(tokens, D, bf16),
+            scratch(tokens, D, f32),
+            scratch(tokens, D, bf16),
+            pltpu.SemaphoreType.DMA((4,)),
+            pltpu.SemaphoreType.DMA((2,)),
+            pltpu.SemaphoreType.DMA((3,)),
         ],
         compiler_params=pltpu.CompilerParams(vmem_limit_bytes=VMEM_GRANT),
-        cost_estimate=cost(20),
+        cost_estimate=cost(32),
         name="ffn",
-    )(place, *operands, weights)
-    return results[: len(outs)], results[len(outs) :]
+    )(place, attended, x, dy, w_o, gain, weights)
 
 
 def grams_of(blocks):
@@ -700,20 +750,16 @@
     attn_own = behind(gather_pieces(attn_tiles), gain_low, line)
     halo, ffn_low = behind((tokens, ffn_low), attn_own)
     up, down = [(j, j + 1) for j in range(n_mp - 1)], [(j + 1, j) for j in range(n_mp - 1)]
-    sides = []
-    for mb in range(micro):
-        part = behind(halo[mb], sides)
-        sides.append((lax.ppermute(part, "mp", up), lax.ppermute(part, "mp", down)))
+    sides = (lax.ppermute(halo, "mp", up), lax.ppermute(halo, "mp", down))
     ffn_all = gather_all(ffn_low)
     bias = make_bias(behind(line, attn_own))
-    attn_pieces = spread_pieces(attn_own, (bias, sides[0]))
+    attn_pieces = spread_pieces(attn_own, bias)
     weights = join(place, behind(attn_pieces, sides))
     w_q, w_k, w_v, w_o = weights
 
     first_row = own_rows * here
     first_doc = first_row // LEN
     inset = first_row - first_doc * LEN
-    gap = jnp.zeros((2 * LEN - 2 * own_rows + QB, D), bf16)
     block_place = first_row // QB + jnp.arange(own_rows // QB, dtype=jnp.int32)
     slot = block_place // (LEN // QB) - first_doc
     lens_window = lax.dynamic_slice_in_dim(
@@ -721,42 +767,33 @@
     )
     meta = jnp.concatenate([slot, block_place % (LEN // QB), lens_window.reshape(-1)]).astype(jnp.int32)
 
-    projected, attended = (), ()
-    for mb in range(micro):
-        above, below = behind(sides[mb], weights, attended)
-        window = jnp.concatenate([above, tokens[mb], below, gap])
-        window = lax.dynamic_slice_in_dim(window, own_rows - inset, 2 * LEN, axis=0)
-        projected = project(window, tokens, gain_low[0:1], weights, mb, projected, attended)
-        q, k, v, normed_window, normed_own = projected
-        attended = (attend(meta, q, k, v, bias, mb, attended),)
-    attended = attended[0].reshape(micro * own_rows, D)
+    there = jnp.concatenate([place, inset[None].astype(jnp.int32)])
+    q, k, v, normed_window, normed_own = project(there, sides, tokens, gain_low[0:1], weights)
+    attended, stats = attend(meta, q, k, v, bias)
+    out_seq = attended
+    attended = attended.reshape(micro * own_rows, D)
     normed_window = normed_window.reshape(micro * 2 * LEN, D)
     normed_own = normed_own.reshape(micro * own_rows, D)
-    rows = tokens.reshape(micro * own_rows, D).astype(f32)
-    middle = rows + dot(attended, w_o, NT)
 
     dy = cotangent.reshape(micro * own_rows, D)
-    ffn_args = (place, middle, dy, gain_low[1:2], ffn_all)
-    sums, (even_one, odd_one) = ffn(*ffn_args, (0, 1))
-    (output, grad_middle, grad_mid_low), (even_two, odd_two) = ffn(*ffn_args, (2, 3), sums, last=True)
+    output, grad_middle, grad_mid_low, even_one, odd_one, even_two, odd_two = ffn(
+        place, attended, tokens.reshape(micro * own_rows, D), dy, w_o, gain_low[1:2], ffn_all
+    )
+    grad_att = dot(grad_mid_low, w_o).astype(bf16).reshape(micro, own_rows, D)
+    back_args = (meta, q, k, v, grad_att, out_seq, stats, bias)
     if direct():
         mine_one, mine_two = scatter_core(even_one, odd_one), scatter_core(even_two, odd_two)
+        grads = attend_back(*back_args, [mine_one, mine_two])
+        line_one = scatter_plane(mine_one, grads)
+        line_two = scatter_plane(behind(mine_two, line_one))
+        sent_one = to_above(line_one[1], 1)
+        grads = behind(grads, line_one)
     else:
         shard_ffn = scatter_plain(
             jnp.concatenate([even_one, even_two], axis=1), jnp.concatenate([odd_one, odd_two], axis=1), rows_dev
         )[0]
-        mine_one = mine_two = ()
-
-    grad_att = dot(grad_mid_low, w_o).astype(bf16).reshape(micro, own_rows, D)
-    back_args = (meta, q, k, v, grad_att, bias)
-    grads = attend_back(*back_args, (0, 2), (), [mine_one] if direct() else ())
-    grads = attend_back(*back_args, (2, 2), grads, [mine_two] if direct() else ())
-    line_one, line_two = (), ()
-    if direct():
-        line_one = scatter_plane(mine_one, grads)
-        line_two = scatter_plane(behind(mine_two, line_one))
-        sent_one = to_above(line_one[1], 1)
-    grad_q, grad_k, grad_v, grad_bias = attend_back(*back_args, (4, 2), grads, [line_one] if direct() else ())
+        grads = attend_back(*back_args)
+    grad_q, grad_k, grad_v, grad_bias = grads
     grad_q = grad_q.reshape(micro * own_rows, D)
     grad_k = grad_k.reshape(micro * 2 * LEN, D)
     grad_v = grad_v.reshape(micro * 2 * LEN, D)
@@ -788,6 +825,7 @@
     grad_bias = behind(grad_bias, mine_attn)
     back, forth = behind((back, forth), shard_attn)
     grad_normed = own_part + (back.astype(f32) + forth.astype(f32)).reshape(micro * own_rows, D)
+    rows = tokens.reshape(micro * own_rows, D).astype(f32)
     rho = lax.rsqrt(jnp.mean(rows * rows, axis=-1, keepdims=True) + epsilon)
     u = grad_normed * gain_low[0]
     tokens_grad = grad_middle + rho * (u - rows * rho * rho * jnp.mean(u * rows, axis=-1, keepdims=True))

time: 440 us -> 397 us (0.902)
  Pallas kernels: 156 us -> 119 us
  matrix products: 44.8 us -> 39.1 us
    pallas_call x9 -> x4, Pallas kernels: 119 us -> 83.6 us  [the longest x1 32.5 us: ffn(): pl.pallas_call(ffn_kernel, in_specs=[SMEM] + [VMEM] * 5 + [ANY], out_spec...]
    ppermute x32, waiting for transfers between devices: 36.9 us -> 48.3 us  [swap(): lax.ppermute(x, 'dp', [(j, j ^ bit) for j in range(lax.axis_size('dp'))])]
    ppermute x4 -> x2, waiting for transfers between devices: 22.6 us -> 16.4 us  [shards(): sides = (lax.ppermute(halo, 'mp', up), lax.ppermute(halo, 'mp', down))]
    concatenate x2 -> x1, other arithmetic: 5.25 us -> 0.59 us  [shards(): there = jnp.concatenate([place, inset[None].astype(jnp.int32)])]
    dot_general x5 -> x4, matrix products: 19.9 us -> 15.9 us  [dot(): return lax.dot_general(a, b, dims, preferred_element_type=f32)]
    ppermute x4 -> x2, starting transfers between devices: 9.09 us -> 6.92 us  [shards(): sides = (lax.ppermute(halo, 'mp', up), lax.ppermute(halo, 'mp', down))]
  transfers between devices with their start and end apart: 56 -> 54, of which waited for: 21 -> 21; matrix products, arithmetic and copies ran while one was open for 18% -> 19% of each run, Pallas kernels for 28% -> 22%
where the time goes in v3:
time: 397 us; the launch traced here: 393 us
  Pallas kernels  119 us (30%)
  waiting for transfers between devices  82.7 us (21%)
  starting transfers between devices  73.2 us (18%)
  matrix products  39.1 us (10%)
  other arithmetic  36.5 us (9%)
  local copies, waits for them, and re-layouts  27.2 us (7%)
  between operations  15.6 us (4%)
    ppermute x32, waiting for transfers between devices, swap(): lax.ppermute(x, 'dp', [(j, j ^ bit) for j in range(lax.axis_size('dp'))])  48.3 us
    pallas_call x1, Pallas kernels, ffn(): pl.pallas_call(ffn_kernel, in_specs=[SMEM] + [VMEM] * 5 + [ANY], out_spec...  32.5 us
    ppermute x32, starting transfers between devices, swap(): lax.ppermute(x, 'dp', [(j, j ^ bit) for j in range(lax.axis_size('dp'))])  26.5 us
    pallas_call x1, Pallas kernels, attend_back(): pl.pallas_call(kernel, grid_spec=pltpu.PrefetchScalarGridSpec(num_scalar_...  22 us
    pallas_call x1, Pallas kernels, attend(): pl.pallas_call(attend_kernel, grid_spec=pltpu.PrefetchScalarGridSpec(num_...  17.1 us
    ppermute x2, waiting for transfers between devices, shards(): sides = (lax.ppermute(halo, 'mp', up), lax.ppermute(halo, 'mp', down))  16.4 us
    dot_general x4, matrix products, dot(): return lax.dot_general(a, b, dims, preferred_element_type=f32)  15.9 us
    ppermute x6, waiting for transfers between devices, to_above(): return lax.ppermute(x, 'mp', [(j, (j + k) % 4) for j in range(4)])  15.2 us
  transfers between devices with their start and end apart: 54, of which 21 were waited for; matrix products, arithmetic and copies ran while one was open for 19% of the time, Pallas kernels for 22%

profile of v3, /device:TPU:0, one launch (start us, length us, event | category | flops | bytes accessed | tf_op | source)
XLA Modules:
  0.0 392.8 jit_solution(15434851648875614847)
XLA Ops:
  9.7 5.1 %collective-permute-start = (bf16[6,96,128]{2,1,0:T(8,128)(2,1)S(1)}, bf16[6,96,128]{2,1,0:T(8,128)(2,1)S(1)}, u32[]{:S(2)}, u32[]{:S(2)}) collective-permute-start(bf16[6,96,128]{2,1,0:T(8,128)(2,1)S(1)} %fusion.69), channel_id=1, source_target_pairs={{1,0},{2,1},{3,2},{0,3},{5,4},{6,5},{7,6},{4,7},{9,8},{10,9},{11,1... | collective-permute-start | bytes 442376 | tf_op jit(solution)/shard_map/ppermute | solution.py:626
  34.1 6.3 %make_bias.1.bias_ref.refs_7_ = f32[6,2,1024,128]{3,2,1,0:T(8,128)} custom-call(f32[6,2,1024]{2,1,0:T(2,128)} %reshape.292.line_ref), custom_call_target="tpu_custom_call" | custom-call | flops 2400000000 | tf_op jit(solution)/shard_map/make_bias/pallas_call | solution.py:84
  40.4 6.3 %collective-permute-done.11.refs_2_ = bf16[4,6,96,128]{3,2,1,0:T(8,128)(2,1)S(1)} collective-permute-done((bf16[4,6,96,128]{3,2,1,0:T(8,128)(2,1)S(1)}, bf16[4,6,96,128]{3,2,1,0:T(8,128)(2,1)S(1)}, u32[]{:S(2)}, u32[]{:S(2)}) %collective-permute-start.11) | collective-permute-done | bytes 589856 | tf_op jit(solution)/shard_map/ppermute | solution.py:622
  50.5 5.5 %collective-permute-start.8 = (bf16[2,384,768]{2,1,0:T(8,128)(2,1)S(1)}, bf16[2,384,768]{2,1,0:T(8,128)(2,1)}, u32[]{:S(2)}, u32[]{:S(2)}) collective-permute-start(bf16[2,384,768]{2,1,0:T(8,128)(2,1)S(1)} %copy-done), channel_id=1, source_target_pairs={{0,1},{1,2},{2,3},{4,5},{5,6},{6,7},{8,9},{9,10},{10,11},{12,13},{... | collective-permute-start | bytes 3538952 | tf_op jit(solution)/shard_map/ppermute | solution.py:753
  61.2 10.0 %collective-permute-done.16 = bf16[2,6,96,128]{3,2,1,0:T(8,128)(2,1)} collective-permute-done((bf16[2,6,96,128]{3,2,1,0:T(8,128)(2,1)}, bf16[2,6,96,128]{3,2,1,0:T(8,128)(2,1)}, u32[]{:S(2)}, u32[]{:S(2)}) %collective-permute-start.16) | collective-permute-done | bytes 294944 | tf_op jit(solution)/shard_map/ppermute | solution.py:622
  75.9 12.7 %collective-permute-done.8.above = bf16[2,384,768]{2,1,0:T(8,128)(2,1)} collective-permute-done((bf16[2,384,768]{2,1,0:T(8,128)(2,1)S(1)}, bf16[2,384,768]{2,1,0:T(8,128)(2,1)}, u32[]{:S(2)}, u32[]{:S(2)}) %collective-permute-start.8) | collective-permute-done | bytes 1179680 | tf_op jit(solution)/shard_map/ppermute | solution.py:753
  88.6 3.6 collective-permute-done.9.below
  93.1 5.5 %join.1.w_ref = bf16[4,768,768]{2,1,0:T(8,128)(2,1)} custom-call(s32[2]{0:T(128)} %pad_add_fusion.place, bf16[4,6,96,128]{3,2,1,0:T(8,128)(2,1)} %copy-done.14, bf16[4,6,96,128]{3,2,1,0:T(8,128)(2,1)} %collective-permute-done.10.refs_1_, bf16[4,6,96,128]{3,2,1,0:T(8,128)(2,1)} %copy-done.22, bf16[4,6,96,128]{3,2,1,0:T(8,128)(2,1)} %collective-permute-done.13.refs_3_, ...), custom_call_target="tpu_custom_call" | custom-call | flops 1500000000 | tf_op jit(solution)/shard_map/join/pallas_call | solution.py:304
  101.0 12.0 %project.1 = (bf16[2,384,768]{2,1,0:T(8,128)(2,1)}, bf16[2,1024,768]{2,1,0:T(8,128)(2,1)}, bf16[2,1024,768]{2,1,0:T(8,128)(2,1)}, bf16[2,1024,768]{2,1,0:T(8,128)(2,1)}, bf16[2,384,768]{2,1,0:T(8,128)(2,1)}) custom-call(s32[3]{0:T(128)} %pad_add_fusion.2.place, bf16[2,384,768]{2,1,0:T(8,128)(2,1)} %collective-permute-done.8.above, ...), custom_call_target="tpu_custom_call" | custom-call | flops 3600000000 | tf_op jit(solution)/shard_map/project/pallas_call | solution.py:367
  113.0 17.1 %attend.1 = (bf16[2,384,768]{2,1,0:T(8,128)(2,1)}, f32[2,6,8,256]{3,2,1,0:T(8,128)}) custom-call(s32[10]{0:T(128)} %pad_add_fusion.1.meta.refs_0_, bf16[2,384,768]{2,1,0:T(8,128)(2,1)} %get-tuple-element.92.q_ref.refs_1_, bf16[2,1024,768]{2,1,0:T(8,128)(2,1)} %get-tuple-element.93.k_ref.refs_2_, bf16[2,1024,768]{2,1,0:T(8,128)(2,1)} %get-tuple-element.94.v_ref.refs_3_, ...), custom_call_target="tpu_custom_call" | custom-call | flops 5100000256 | tf_op jit(solution)/shard_map/attend/pallas_call | solution.py:219
  130.2 32.5 %ffn.1 = (bf16[768,768]{1,0:T(8,128)(2,1)}, f32[768,768]{1,0:T(8,128)}, bf16[768,768]{1,0:T(8,128)(2,1)}, bf16[4,2,96,1536]{3,2,1,0:T(8,128)(2,1)}, bf16[4,2,96,...) custom-call(s32[2]{0:T(128)} %pad_add_fusion.place, ...), custom_call_target="tpu_custom_call" | custom-call | flops 9600000000 | tf_op jit(solution)/shard_map/ffn/pallas_call | solution.py:558
  168.9 4.1 %convolution_convert_fusion = bf16[768,768]{1,0:T(8,128)(2,1)} fusion(bf16[768,768]{1,0:T(8,128)(2,1)} %get-tuple-element.99.dh_ref, bf16[4,768,768]{2,1,0:T(8,128)(2,1)} %join.1.w_ref), kind=kOutput, calls=%fused_computation.42 | convolution fusion | flops 906559488 | bytes 3538944 | tf_op jit(solution)/shard_map/dot_general | solution.py:56
  177.4 3.7 add_convert_fusion.1.refs_9_
  181.2 22.0 %attend_back.1 = (bf16[2,384,768]{2,1,0:T(8,128)(2,1)}, bf16[2,1024,768]{2,1,0:T(8,128)(2,1)}, bf16[2,1024,768]{2,1,0:T(8,128)(2,1)}, f32[6,2,1024,128]{3,2,1,0:T(8,128)}) custom-call(s32[10]{0:T(128)} %pad_add_fusion.1.meta.refs_0_, bf16[2,384,768]{2,1,0:T(8,128)(2,1)} %get-tuple-element.92.q_ref.refs_1_, ...), custom_call_target="tpu_custom_call" | custom-call | flops 7200000000 | tf_op jit(solution)/shard_map/attend_back/pallas_call | solution.py:242
  210.5 14.1 %attn_grads.1 = (bf16[4,4,6,96,128]{4,3,2,1,0:T(8,128)(2,1)}, bf16[4,4,6,96,128]{4,3,2,1,0:T(8,128)(2,1)}) custom-call(s32[2]{0:T(128)} %pad_add_fusion.place, bf16[2048,768]{1,0:T(8,128)(2,1)} %bitcast.277, bf16[2048,768]{1,0:T(8,128)(2,1)} %bitcast.280, bf16[2048,768]{1,0:T(8,128)(2,1)} %bitcast.278, bf16[768,768]{1,0:T(8,128)(2,1)} %bitcast.286, ...), custom_call_target="tpu_custom_call" | custom-call | flops 3000000000 | tf_op jit(solution)/shard_map/attn_grads/pallas_call | solution.py:441
  224.8 5.2 %fusion.25 = f32[2048,768]{1,0:T(8,128)S(1)} fusion(bf16[2048,768]{1,0:T(8,128)(2,1)} %bitcast.281, bf16[4,768,768]{2,1,0:T(8,128)(2,1)} %join.1.w_ref), kind=kOutput, calls=%fused_computation.52 | convolution fusion | flops 2415919104 | bytes 10616832 | tf_op jit(solution)/shard_map/dot_general | solution.py:56
  230.0 4.1 %convolution_add_fusion = f32[2048,768]{1,0:T(8,128)S(1)} fusion(f32[2048,768]{1,0:T(8,128)S(1)} %fusion.25, bf16[2048,768]{1,0:T(8,128)(2,1)S(1)} %bitcast.279, bf16[4,768,768]{2,1,0:T(8,128)(2,1)} %join.1.w_ref), kind=kOutput, calls=%fused_computation.7 | convolution fusion | flops 2417491968 | bytes 16908288 | tf_op jit(solution)/shard_map/dot_general | solution.py:56
  244.3 9.1 %collective-permute-done.28 = bf16[96,1536]{1,0:T(8,128)(2,1)S(1)} collective-permute-done((bf16[96,1536]{1,0:T(8,128)(2,1)S(1)}, bf16[96,1536]{1,0:T(8,128)(2,1)S(1)}, u32[]{:S(2)}, u32[]{:S(2)}) %collective-permute-start.28) | collective-permute-done | bytes 294944 | tf_op jit(solution)/shard_map/ppermute | solution.py:630
  256.6 10.4 %collective-permute-start.31 = (bf16[2,384,768]{2,1,0:T(8,128)(2,1)}, bf16[2,384,768]{2,1,0:T(8,128)(2,1)}, u32[]{:S(2)}, u32[]{:S(2)}) collective-permute-start(bf16[2,384,768]{2,1,0:T(8,128)(2,1)} %get-tuple-element.128), channel_id=1, source_target_pairs={{0,1},{1,2},{2,3},{4,5},{5,6},{6,7},{8,9},{9,10},{10,11},{12,13},{... | collective-permute-start | bytes 3538952 | tf_op jit(solution)/shard_map/ppermute | solution.py:818
  273.9 2.7 fusion.40
  276.5 8.9 %diagonals.1 = f32[6,2,1024]{2,1,0:T(2,128)} custom-call(f32[6,2,1024,128]{3,2,1,0:T(8,128)} %get-tuple-element.135.acc_ref), custom_call_target="tpu_custom_call" | custom-call | flops 300000000 | tf_op jit(solution)/shard_map/diagonals/pallas_call | solution.py:107
  289.7 7.5 %collective-permute-done.33 = bf16[4,6,96,128]{3,2,1,0:T(8,128)(2,1)} collective-permute-done((bf16[4,6,96,128]{3,2,1,0:T(8,128)(2,1)}, bf16[4,6,96,128]{3,2,1,0:T(8,128)(2,1)}, u32[]{:S(2)}, u32[]{:S(2)}) %collective-permute-start.33) | collective-permute-done | bytes 589856 | tf_op jit(solution)/shard_map/ppermute | solution.py:622
  302.1 2.8 collective-permute-start.37
  305.2 2.7 collective-permute-done.35
  307.9 3.4 collective-permute-done.36
  319.5 2.6 fusion.11
  322.2 6.3 %collective-permute-done.42 = bf16[384,512]{1,0:T(8,128)(2,1)S(1)} collective-permute-done((bf16[384,512]{1,0:T(8,128)(2,1)S(1)}, bf16[384,512]{1,0:T(8,128)(2,1)S(1)}, u32[]{:S(2)}, u32[]{:S(2)}) %collective-permute-start.42) | collective-permute-done | bytes 393248 | tf_op jit(solution)/shard_map/ppermute | solution.py:622
  334.3 6.3 %collective-permute-done.44 = bf16[384,512]{1,0:T(8,128)(2,1)S(1)} collective-permute-done((bf16[384,512]{1,0:T(8,128)(2,1)S(1)}, bf16[384,512]{1,0:T(8,128)(2,1)S(1)}, u32[]{:S(2)}, u32[]{:S(2)}) %collective-permute-start.44) | collective-permute-done | bytes 393248 | tf_op jit(solution)/shard_map/ppermute | solution.py:622
  350.6 2.9 fusion.87
  353.5 3.4 fusion.1
  357.0 3.2 fusion
  372.6 4.7 %collective-permute-start.50 = (f32[8,128]{1,0:T(8,128)S(1)}, f32[8,128]{1,0:T(8,128)S(1)}, u32[]{:S(2)}, u32[]{:S(2)}) collective-permute-start(f32[8,128]{1,0:T(8,128)S(1)} %fusion.72), channel_id=1, source_target_pairs={{1,0},{2,1},{3,2},{0,3},{5,4},{6,5},{7,6},{4,7},{9,8},{10,9},{11,1... | collective-permute-start | bytes 12296 | tf_op jit(solution)/shard_map/ppermute | solution.py:626
  (356 shorter events, 130.4 us)
Async XLA Ops:
  7.3 122.9 %all-gather.3.cloned.1.call-start = ((), (), s32[]{:S(2)}) async-start(), calls=%async_computation | async-start | bytes 9732096 | tf_op jit(solution)/shard_map/all_gather | solution.py:643
  9.7 21.1 %collective-permute-start = (bf16[6,96,128]{2,1,0:T(8,128)(2,1)S(1)}, bf16[6,96,128]{2,1,0:T(8,128)(2,1)S(1)}, u32[]{:S(2)}, u32[]{:S(2)}) collective-permute-start(bf16[6,96,128]{2,1,0:T(8,128)(2,1)S(1)} %fusion.69), channel_id=1, source_target_pairs={{1,0},{2,1},{3,2},{0,3},{5,4},{6,5},{7,6},{4,7},{9,8},{10,9},{11,1... | collective-permute-start | bytes 442376 | tf_op jit(solution)/shard_map/ppermute | solution.py:626
  14.8 16.0 %collective-permute-start.1 = (bf16[6,96,128]{2,1,0:T(8,128)(2,1)S(1)}, bf16[6,96,128]{2,1,0:T(8,128)(2,1)S(1)}, u32[]{:S(2)}, u32[]{:S(2)}) collective-permute-start(bf16[6,96,128]{2,1,0:T(8,128)(2,1)S(1)} %fusion.69), channel_id=1, source_target_pairs={{2,0},{3,1},{0,2},{1,3},{6,4},{7,5},{4,6},{5,7},{10,8},{11,9},{8,1... | collective-permute-start | bytes 442376 | tf_op jit(solution)/shard_map/ppermute | solution.py:626
  14.8 16.0 %collective-permute-start.2 = (bf16[6,96,128]{2,1,0:T(8,128)(2,1)S(1)}, bf16[6,96,128]{2,1,0:T(8,128)(2,1)S(1)}, u32[]{:S(2)}, u32[]{:S(2)}) collective-permute-start(bf16[6,96,128]{2,1,0:T(8,128)(2,1)S(1)} %fusion.69), channel_id=1, source_target_pairs={{3,0},{0,1},{1,2},{2,3},{7,4},{4,5},{5,6},{6,7},{11,8},{8,9},{9,10... | collective-permute-start | bytes 442376 | tf_op jit(solution)/shard_map/ppermute | solution.py:626
  31.0 15.7 %collective-permute-start.11 = (bf16[4,6,96,128]{3,2,1,0:T(8,128)(2,1)S(1)}, bf16[4,6,96,128]{3,2,1,0:T(8,128)(2,1)S(1)}, u32[]{:S(2)}, u32[]{:S(2)}) collective-permute-start(bf16[4,6,96,128]{3,2,1,0:T(8,128)(2,1)S(1)} %pad_maximum_fusion.2.refs_0_), channel_id=1, source_target_pairs={{0,8},{4,12},{8,0},{12,4},{16,24},{20,28},{24,16},{28,20},{1,9},{5... | collective-permute-start | bytes 1769480 | tf_op jit(solution)/shard_map/ppermute | solution.py:622
  32.6 16.5 %collective-permute-start.12 = (bf16[4,6,96,128]{3,2,1,0:T(8,128)(2,1)S(1)}, bf16[4,6,96,128]{3,2,1,0:T(8,128)(2,1)S(1)}, u32[]{:S(2)}, u32[]{:S(2)}) collective-permute-start(bf16[4,6,96,128]{3,2,1,0:T(8,128)(2,1)S(1)} %pad_maximum_fusion.2.refs_0_), channel_id=1, source_target_pairs={{0,16},{4,20},{8,24},{12,28},{16,0},{20,4},{24,8},{28,12},{1,17},{... | collective-permute-start | bytes 1769480 | tf_op jit(solution)/shard_map/ppermute | solution.py:622
  34.1 38.2 %collective-permute-start.10 = (bf16[4,6,96,128]{3,2,1,0:T(8,128)(2,1)S(1)}, bf16[4,6,96,128]{3,2,1,0:T(8,128)(2,1)}, u32[]{:S(2)}, u32[]{:S(2)}) collective-permute-start(bf16[4,6,96,128]{3,2,1,0:T(8,128)(2,1)S(1)} %pad_maximum_fusion.2.refs_0_), channel_id=1, source_target_pairs={{0,4},{4,0},{8,12},{12,8},{16,20},{20,16},{24,28},{28,24},{1,5},{5... | collective-permute-start | bytes 1769480 | tf_op jit(solution)/shard_map/ppermute | solution.py:622
  50.5 38.1 %collective-permute-start.8 = (bf16[2,384,768]{2,1,0:T(8,128)(2,1)S(1)}, bf16[2,384,768]{2,1,0:T(8,128)(2,1)}, u32[]{:S(2)}, u32[]{:S(2)}) collective-permute-start(bf16[2,384,768]{2,1,0:T(8,128)(2,1)S(1)} %copy-done), channel_id=1, source_target_pairs={{0,1},{1,2},{2,3},{4,5},{5,6},{6,7},{8,9},{9,10},{10,11},{12,13},{... | collective-permute-start | bytes 3538952 | tf_op jit(solution)/shard_map/ppermute | solution.py:753
  56.0 36.3 %collective-permute-start.9 = (bf16[2,384,768]{2,1,0:T(8,128)(2,1)S(1)}, bf16[2,384,768]{2,1,0:T(8,128)(2,1)}, u32[]{:S(2)}, u32[]{:S(2)}) collective-permute-start(bf16[2,384,768]{2,1,0:T(8,128)(2,1)S(1)} %copy-done), channel_id=1, source_target_pairs={{1,0},{2,1},{3,2},{5,4},{6,5},{7,6},{9,8},{10,9},{11,10},{13,12},{... | collective-permute-start | bytes 3538952 | tf_op jit(solution)/shard_map/ppermute | solution.py:753
  58.2 13.1 %collective-permute-start.16 = (bf16[2,6,96,128]{3,2,1,0:T(8,128)(2,1)}, bf16[2,6,96,128]{3,2,1,0:T(8,128)(2,1)}, u32[]{:S(2)}, u32[]{:S(2)}) collective-permute-start(bf16[2,6,96,128]{3,2,1,0:T(8,128)(2,1)} %slice.230), channel_id=1, source_target_pairs={{0,8},{4,12},{8,0},{12,4},{16,24},{20,28},{24,16},{28,20},{1,9},{5... | collective-permute-start | bytes 884744 | tf_op jit(solution)/shard_map/ppermute | solution.py:622
  60.3 15.6 %collective-permute-start.13 = (bf16[4,6,96,128]{3,2,1,0:T(8,128)(2,1)S(1)}, bf16[4,6,96,128]{3,2,1,0:T(8,128)(2,1)}, u32[]{:S(2)}, u32[]{:S(2)}) collective-permute-start(bf16[4,6,96,128]{3,2,1,0:T(8,128)(2,1)S(1)} %collective-permute-done.11.refs_2_), channel_id=1, source_target_pairs={{0,4},{4,0},{8,12},{12,8},{16,20},{20,16},{24,28},{28,24},{1,5},{5... | collective-permute-start | bytes 1769480 | tf_op jit(solution)/shard_map/ppermute | solution.py:622
  72.3 20.0 %collective-permute-start.17 = (bf16[4,6,96,128]{3,2,1,0:T(8,128)(2,1)S(1)}, bf16[4,6,96,128]{3,2,1,0:T(8,128)(2,1)S(1)}, u32[]{:S(2)}, u32[]{:S(2)}) collective-permute-start(bf16[4,6,96,128]{3,2,1,0:T(8,128)(2,1)S(1)} %constant_dynamic-update-slice_fusion.refs_6_), channel_id=1, source_target_pairs={{0,4},{4,0},{8,12},{12,8},{16,20},{20,16},{24,28},{28,24},{1,5},{5... | collective-permute-start | bytes 1769480 | tf_op jit(solution)/shard_map/ppermute | solution.py:622
  164.4 13.1 %collective-permute-start.19 = (bf16[4,2,96,1536]{3,2,1,0:T(8,128)(2,1)}, bf16[4,2,96,1536]{3,2,1,0:T(8,128)(2,1)}, u32[]{:S(2)}, u32[]{:S(2)}) collective-permute-start(bf16[4,2,96,1536]{3,2,1,0:T(8,128)(2,1)} %get-tuple-element.104), channel_id=1, source_target_pairs={{0,4},{4,0},{8,12},{12,8},{16,20},{20,16},{24,28},{28,24},{1,5},{5... | collective-permute-start | bytes 7077896 | tf_op jit(solution)/shard_map/ppermute | solution.py:622
  173.9 29.3 %collective-permute-start.20 = (bf16[2,96,1536]{2,1,0:T(8,128)(2,1)S(1)}, bf16[2,96,1536]{2,1,0:T(8,128)(2,1)}, u32[]{:S(2)}, u32[]{:S(2)}) collective-permute-start(bf16[2,96,1536]{2,1,0:T(8,128)(2,1)S(1)} %get-tuple-element.190), channel_id=1, source_target_pairs={{0,8},{4,12},{8,0},{12,4},{16,24},{20,28},{24,16},{28,20},{1,9},{5... | collective-permute-start | bytes 1769480 | tf_op jit(solution)/shard_map/ppermute | solution.py:622
  174.3 28.9 %collective-permute-start.21 = (bf16[2,96,1536]{2,1,0:T(8,128)(2,1)S(1)}, bf16[2,96,1536]{2,1,0:T(8,128)(2,1)}, u32[]{:S(2)}, u32[]{:S(2)}) collective-permute-start(bf16[2,96,1536]{2,1,0:T(8,128)(2,1)S(1)} %get-tuple-element.189), channel_id=1, source_target_pairs={{0,16},{4,20},{8,24},{12,28},{16,0},{20,4},{24,8},{28,12},{1,17},{... | collective-permute-start | bytes 1769480 | tf_op jit(solution)/shard_map/ppermute | solution.py:622
  175.0 28.2 %collective-permute-start.22 = (bf16[2,96,1536]{2,1,0:T(8,128)(2,1)S(1)}, bf16[2,96,1536]{2,1,0:T(8,128)(2,1)}, u32[]{:S(2)}, u32[]{:S(2)}) collective-permute-start(bf16[2,96,1536]{2,1,0:T(8,128)(2,1)S(1)} %get-tuple-element.188), channel_id=1, source_target_pairs={{0,24},{4,28},{8,16},{12,20},{16,8},{20,12},{24,0},{28,4},{1,25},{... | collective-permute-start | bytes 1769480 | tf_op jit(solution)/shard_map/ppermute | solution.py:622
  207.0 27.3 %collective-permute-start.25 = (bf16[2,96,1536]{2,1,0:T(8,128)(2,1)}, bf16[2,96,1536]{2,1,0:T(8,128)(2,1)}, u32[]{:S(2)}, u32[]{:S(2)}) collective-permute-start(bf16[2,96,1536]{2,1,0:T(8,128)(2,1)} %get-tuple-element.187), channel_id=1, source_target_pairs={{0,8},{4,12},{8,0},{12,4},{16,24},{20,28},{24,16},{28,20},{1,9},{5... | collective-permute-start | bytes 1769480 | tf_op jit(solution)/shard_map/ppermute | solution.py:622
  207.5 26.9 %collective-permute-start.26 = (bf16[2,96,1536]{2,1,0:T(8,128)(2,1)S(1)}, bf16[2,96,1536]{2,1,0:T(8,128)(2,1)}, u32[]{:S(2)}, u32[]{:S(2)}) collective-permute-start(bf16[2,96,1536]{2,1,0:T(8,128)(2,1)S(1)} %get-tuple-element.186), channel_id=1, source_target_pairs={{0,16},{4,20},{8,24},{12,28},{16,0},{20,4},{24,8},{28,12},{1,17},{... | collective-permute-start | bytes 1769480 | tf_op jit(solution)/shard_map/ppermute | solution.py:622
  208.1 26.3 %collective-permute-start.27 = (bf16[2,96,1536]{2,1,0:T(8,128)(2,1)S(1)}, bf16[2,96,1536]{2,1,0:T(8,128)(2,1)}, u32[]{:S(2)}, u32[]{:S(2)}) collective-permute-start(bf16[2,96,1536]{2,1,0:T(8,128)(2,1)S(1)} %get-tuple-element.185), channel_id=1, source_target_pairs={{0,24},{4,28},{8,16},{12,20},{16,8},{20,12},{24,0},{28,4},{1,25},{... | collective-permute-start | bytes 1769480 | tf_op jit(solution)/shard_map/ppermute | solution.py:622
  210.5 33.8 %collective-permute-start.24 = (bf16[96,1536]{1,0:T(8,128)(2,1)}, bf16[96,1536]{1,0:T(8,128)(2,1)}, u32[]{:S(2)}, u32[]{:S(2)}) collective-permute-start(bf16[96,1536]{1,0:T(8,128)(2,1)} %slice_bitcast_fusion.21), channel_id=1, source_target_pairs={{0,1},{1,2},{2,3},{3,0},{4,5},{5,6},{6,7},{7,4},{8,9},{9,10},{10,1... | collective-permute-start | bytes 884744 | tf_op jit(solution)/shard_map/ppermute | solution.py:630
  224.7 29.8 %collective-permute-start.23 = (bf16[4,4,6,96,128]{4,3,2,1,0:T(8,128)(2,1)}, bf16[4,4,6,96,128]{4,3,2,1,0:T(8,128)(2,1)S(1)}, u32[]{:S(2)}, u32[]{:S(2)}) collective-permute-start(bf16[4,4,6,96,128]{4,3,2,1,0:T(8,128)(2,1)} %get-tuple-element.121), channel_id=1, source_target_pairs={{0,4},{4,0},{8,12},{12,8},{16,20},{20,16},{24,28},{28,24},{1,5},{5... | collective-permute-start | bytes 7077896 | tf_op jit(solution)/shard_map/ppermute | solution.py:622
  236.2 17.1 %collective-permute-start.28 = (bf16[96,1536]{1,0:T(8,128)(2,1)S(1)}, bf16[96,1536]{1,0:T(8,128)(2,1)S(1)}, u32[]{:S(2)}, u32[]{:S(2)}) collective-permute-start(bf16[96,1536]{1,0:T(8,128)(2,1)S(1)} %get-tuple-element.204), channel_id=1, source_target_pairs={{0,2},{1,3},{2,0},{3,1},{4,6},{5,7},{6,4},{7,5},{8,10},{9,11},{10,... | collective-permute-start | bytes 884744 | tf_op jit(solution)/shard_map/ppermute | solution.py:630
  238.3 15.1 %collective-permute-start.29 = (bf16[96,1536]{1,0:T(8,128)(2,1)S(1)}, bf16[96,1536]{1,0:T(8,128)(2,1)S(1)}, u32[]{:S(2)}, u32[]{:S(2)}) collective-permute-start(bf16[96,1536]{1,0:T(8,128)(2,1)S(1)} %get-tuple-element.205), channel_id=1, source_target_pairs={{0,3},{1,0},{2,1},{3,2},{4,7},{5,4},{6,5},{7,6},{8,11},{9,8},{10,9... | collective-permute-start | bytes 884744 | tf_op jit(solution)/shard_map/ppermute | solution.py:630
  255.3 41.9 %collective-permute-start.30 = (bf16[2,384,768]{2,1,0:T(8,128)(2,1)}, bf16[2,384,768]{2,1,0:T(8,128)(2,1)}, u32[]{:S(2)}, u32[]{:S(2)}) collective-permute-start(bf16[2,384,768]{2,1,0:T(8,128)(2,1)} %get-tuple-element.127), channel_id=1, source_target_pairs={{1,0},{2,1},{3,2},{5,4},{6,5},{7,6},{9,8},{10,9},{11,10},{13,12},{... | collective-permute-start | bytes 3538952 | tf_op jit(solution)/shard_map/ppermute | solution.py:818
  256.6 40.6 %collective-permute-start.31 = (bf16[2,384,768]{2,1,0:T(8,128)(2,1)}, bf16[2,384,768]{2,1,0:T(8,128)(2,1)}, u32[]{:S(2)}, u32[]{:S(2)}) collective-permute-start(bf16[2,384,768]{2,1,0:T(8,128)(2,1)} %get-tuple-element.128), channel_id=1, source_target_pairs={{0,1},{1,2},{2,3},{4,5},{5,6},{6,7},{8,9},{9,10},{10,11},{12,13},{... | collective-permute-start | bytes 3538952 | tf_op jit(solution)/shard_map/ppermute | solution.py:818
  269.0 20.7 %collective-permute-start.32 = (bf16[4,6,96,128]{3,2,1,0:T(8,128)(2,1)}, bf16[4,6,96,128]{3,2,1,0:T(8,128)(2,1)}, u32[]{:S(2)}, u32[]{:S(2)}) collective-permute-start(bf16[4,6,96,128]{3,2,1,0:T(8,128)(2,1)} %get-tuple-element.184), channel_id=1, source_target_pairs={{0,8},{4,12},{8,0},{12,4},{16,24},{20,28},{24,16},{28,20},{1,9},{5... | collective-permute-start | bytes 1769480 | tf_op jit(solution)/shard_map/ppermute | solution.py:622
  269.6 27.6 %collective-permute-start.33 = (bf16[4,6,96,128]{3,2,1,0:T(8,128)(2,1)}, bf16[4,6,96,128]{3,2,1,0:T(8,128)(2,1)}, u32[]{:S(2)}, u32[]{:S(2)}) collective-permute-start(bf16[4,6,96,128]{3,2,1,0:T(8,128)(2,1)} %get-tuple-element.183), channel_id=1, source_target_pairs={{0,16},{4,20},{8,24},{12,28},{16,0},{20,4},{24,8},{28,12},{1,17},{... | collective-permute-start | bytes 1769480 | tf_op jit(solution)/shard_map/ppermute | solution.py:622
  271.3 25.9 %collective-permute-start.34 = (bf16[4,6,96,128]{3,2,1,0:T(8,128)(2,1)}, bf16[4,6,96,128]{3,2,1,0:T(8,128)(2,1)}, u32[]{:S(2)}, u32[]{:S(2)}) collective-permute-start(bf16[4,6,96,128]{3,2,1,0:T(8,128)(2,1)} %get-tuple-element.182), channel_id=1, source_target_pairs={{0,24},{4,28},{8,16},{12,20},{16,8},{20,12},{24,0},{28,4},{1,25},{... | collective-permute-start | bytes 1769480 | tf_op jit(solution)/shard_map/ppermute | solution.py:622
  300.0 11.3 %collective-permute-start.36 = (bf16[6,96,128]{2,1,0:T(8,128)(2,1)S(1)}, bf16[6,96,128]{2,1,0:T(8,128)(2,1)S(1)}, u32[]{:S(2)}, u32[]{:S(2)}) collective-permute-start(bf16[6,96,128]{2,1,0:T(8,128)(2,1)S(1)} %get-tuple-element.203), channel_id=1, source_target_pairs={{0,2},{1,3},{2,0},{3,1},{4,6},{5,7},{6,4},{7,5},{8,10},{9,11},{10,... | collective-permute-start | bytes 442376 | tf_op jit(solution)/shard_map/ppermute | solution.py:630
  305.1 11.3 %collective-permute-start.41 = (bf16[2,384,512]{2,1,0:T(8,128)(2,1)S(1)}, bf16[2,384,512]{2,1,0:T(8,128)(2,1)S(1)}, u32[]{:S(2)}, u32[]{:S(2)}) collective-permute-start(bf16[2,384,512]{2,1,0:T(8,128)(2,1)S(1)} %select_convert_fusion), channel_id=1, source_target_pairs={{0,4},{4,0},{8,12},{12,8},{16,20},{20,16},{24,28},{28,24},{1,5},{5... | collective-permute-start | bytes 2359304 | tf_op jit(solution)/shard_map/ppermute | solution.py:622
  314.3 27.3 %collective-permute-start.38 = (bf16[2,208,192]{1,2,0:T(8,128)(2,1)S(1)}, bf16[2,208,192]{1,2,0:T(8,128)(2,1)S(1)}, u32[]{:S(2)}, u32[]{:S(2)}) collective-permute-start(bf16[2,208,192]{1,2,0:T(8,128)(2,1)S(1)} %select_convert_fusion.1), channel_id=1, source_target_pairs={{0,4},{4,0},{8,12},{12,8},{16,20},{20,16},{24,28},{28,24},{1,5},{5... | collective-permute-start | bytes 479240 | tf_op jit(solution)/shard_map/ppermute | solution.py:622
  316.9 11.6 %collective-permute-start.42 = (bf16[384,512]{1,0:T(8,128)(2,1)S(1)}, bf16[384,512]{1,0:T(8,128)(2,1)S(1)}, u32[]{:S(2)}, u32[]{:S(2)}) collective-permute-start(bf16[384,512]{1,0:T(8,128)(2,1)S(1)} %get-tuple-element.196), channel_id=1, source_target_pairs={{0,8},{4,12},{8,0},{12,4},{16,24},{20,28},{24,16},{28,20},{1,9},{5... | collective-permute-start | bytes 1179656 | tf_op jit(solution)/shard_map/ppermute | solution.py:622
  (81 other events, 684.7 us)
Sparse Core Ops, SparseCore 0:
  31.1 92.6 all-gather.2
